TPU v7x, 32 devices: a whole 2x2x4 slice. The times are simulated.
32 devices in a mesh: dp: 4 (over z), seq: 8 (over y, x, core).
Axes of the slice: x: 2, y: 2, z: 4, core: 2. Of those that a mesh axis runs over, the one named last changes fastest.
Arguments:
- layer_input: bfloat16 [4096, 2560], P(('dp', 'seq')), may hold values from -6 to 6
- positions: int32 [4096], P(('dp', 'seq')), may hold values from 0 to 1023, as said below
- attn_gain: bfloat16 [2560], P(('dp', 'seq')), may hold values from 0.5 to 1.5
- query_down: bfloat16 [2560, 768], P(('dp', 'seq')), may hold values from -0.125 to 0.125
- query_gain: bfloat16 [768], P(('dp', 'seq')), may hold values from 0.5 to 1.5
- query_up: bfloat16 [768, 3840], P(None, ('dp', 'seq')), may hold values from -0.4375 to 0.4375
- latent_down: bfloat16 [2560, 288], P(('dp', 'seq')), may hold values from -0.125 to 0.125
- latent_gain: bfloat16 [256], P(('dp', 'seq')), may hold values from 0.5 to 1.5
- latent_up: bfloat16 [256, 5120], P(None, ('dp', 'seq')), may hold values from -0.375 to 0.375
- output_proj: bfloat16 [2560, 2560], P(('dp', 'seq')), may hold values from -3 to 3
- ffn_gain: bfloat16 [2560], P(('dp', 'seq')), may hold values from 0.5 to 1.5
- ffn_gate: bfloat16 [2560, 6400], P(None, ('dp', 'seq')), may hold values from -0.125 to 0.125
- ffn_up: bfloat16 [2560, 6400], P(None, ('dp', 'seq')), may hold values from -0.125 to 0.125
- ffn_down: bfloat16 [6400, 2560], P(('dp', 'seq')), may hold values from -0.75 to 0.75
- cotangent: bfloat16 [4096, 2560], P(('dp', 'seq')), may hold values from -6 to 6
Outputs:
- layer_output: bfloat16 [4096, 2560], P(('dp', 'seq'))
- input_grad: float32 [4096, 2560], P(('dp', 'seq'))
- grad_attn_gain: float32 [2560], P(('dp', 'seq'))
- grad_query_down: float32 [2560, 768], P(('dp', 'seq'))
- grad_query_gain: float32 [768], P(('dp', 'seq'))
- grad_query_up: float32 [768, 3840], P(None, ('dp', 'seq'))
- grad_latent_down: float32 [2560, 288], P(('dp', 'seq'))
- grad_latent_gain: float32 [256], P(('dp', 'seq'))
- grad_latent_up: float32 [256, 5120], P(None, ('dp', 'seq'))
- grad_output_proj: float32 [2560, 2560], P(('dp', 'seq'))
- grad_ffn_gain: float32 [2560], P(('dp', 'seq'))
- grad_ffn_gate: float32 [2560, 6400], P(None, ('dp', 'seq'))
- grad_ffn_up: float32 [2560, 6400], P(None, ('dp', 'seq'))
- grad_ffn_down: float32 [6400, 2560], P(('dp', 'seq'))
Inputs may be any that keep to these rules, and one draw needn't show every extreme that they name: Each sequence of 1024 tokens is a pack of documents: positions count 0, 1, 2, ... from each document's first token, the first token of every sequence starts a document, and one sequence, drawn from the seed, is a single document.
All inputs are finite; a program needn't handle non-finite values.
Results may differ from a plain program's by a relative error of at most 0.02.
Values may be sent and summed in bfloat16 or wider, within the bound.
No kernel may reach another device: no remote copies, remote signals or barrier semaphores. Data moves between devices by JAX's collectives and lax.ppermute only.
A program may use at most 768 MiB of HBM per device.

v0:
```python
import math

import jax
import jax.numpy as jnp
from jax import lax
from jax.sharding import PartitionSpec as P

KV_RANK = 256
HEADS = 40
NOPE = 64
ROPE = 32
VDIM = 64


EPSILON = 1e-05
RESIDUAL_SCALE = 1.4 / math.sqrt(62.0)


def norm_parts(values):
    inverse = lax.rsqrt(jnp.mean(values * values, axis=-1, keepdims=True) + EPSILON)
    return (values * inverse, inverse)


def norm_back(grad_scaled, normalized, inverse, scale_gain):
    gain_grad = jnp.sum(grad_scaled * normalized, axis=0)
    grad_normal = grad_scaled * scale_gain
    values_grad = inverse * (
        grad_normal - normalized * jnp.mean(grad_normal * normalized, axis=-1, keepdims=True)
    )
    return (values_grad, gain_grad)


def rotary_tables(positions):
    half_width = ROPE // 2
    inverse = 10000.0 ** (-2.0 * jnp.arange(half_width, dtype=jnp.float32) / ROPE)
    angles = positions.astype(jnp.float32)[:, None] * inverse[None, :]
    cos_table = jnp.cos(angles)
    sin_table = jnp.sin(angles)
    return (
        jnp.concatenate([cos_table, cos_table], -1),
        jnp.concatenate([sin_table, sin_table], -1),
    )


def rotate(values, cos_table, sin_table):
    half_width = values.shape[-1] // 2
    turned = jnp.concatenate([-values[..., half_width:], values[..., :half_width]], -1)
    return values * cos_table + turned * sin_table


def rotate_back(grads, cos_table, sin_table):
    half_width = grads.shape[-1] // 2
    scaled = grads * sin_table
    return grads * cos_table + jnp.concatenate(
        [scaled[..., half_width:], -scaled[..., :half_width]], -1
    )


def score_block(query_block, keys_values, rotary_all, allowed):
    score_scale = (NOPE + ROPE) ** (-0.5)
    scores = jnp.einsum(
        "thd,lhd->htl",
        query_block[..., :NOPE],
        keys_values[..., :NOPE],
        preferred_element_type=jnp.float32,
    )
    scores = scores + jnp.einsum(
        "thr,lr->htl", query_block[..., NOPE:], rotary_all, preferred_element_type=jnp.float32
    )
    return jnp.where(allowed[None], scores * score_scale, -1e30)


def swiglu_back(grad_activated, gate_values, upward):
    sigmoid_gate = jax.nn.sigmoid(gate_values)
    grad_upward = (grad_activated * gate_values * sigmoid_gate).astype(jnp.bfloat16)
    grad_gate = (
        grad_activated * upward * sigmoid_gate * (1.0 + gate_values * (1.0 - sigmoid_gate))
    ).astype(jnp.bfloat16)
    return (grad_gate, grad_upward)


def per_device(
    layer_input,
    positions,
    attn_gain,
    query_down,
    query_gain,
    query_up,
    latent_down,
    latent_gain,
    latent_up,
    output_proj,
    ffn_gain,
    ffn_gate,
    ffn_up,
    ffn_down,
    cotangent,
):
    attn_full = (
        lax.all_gather(attn_gain, ("dp", "seq"), axis=0, tiled=True),
        lax.all_gather(query_down, ("dp", "seq"), axis=0, tiled=True),
        lax.all_gather(query_gain, ("dp", "seq"), axis=0, tiled=True),
        lax.all_gather(query_up, ("dp", "seq"), axis=1, tiled=True),
        lax.all_gather(latent_down, ("dp", "seq"), axis=0, tiled=True),
        lax.all_gather(latent_gain, ("dp", "seq"), axis=0, tiled=True),
        lax.all_gather(latent_up, ("dp", "seq"), axis=1, tiled=True),
        lax.all_gather(output_proj, ("dp", "seq"), axis=0, tiled=True),
    )
    token_count = layer_input.shape[0]
    score_scale = (NOPE + ROPE) ** (-0.5)
    inputs = layer_input.astype(jnp.float32)
    cos_table, sin_table = rotary_tables(positions)
    normal_one, inverse_one = norm_parts(inputs)
    normed = (normal_one * attn_full[0].astype(jnp.float32)).astype(jnp.bfloat16)
    query_latent = jnp.dot(normed, attn_full[1], preferred_element_type=jnp.float32)
    normal_query, inverse_query = norm_parts(query_latent)
    query_normed = (normal_query * attn_full[2].astype(jnp.float32)).astype(jnp.bfloat16)
    projected = jnp.dot(query_normed, attn_full[3], preferred_element_type=jnp.float32).reshape(
        token_count, HEADS, NOPE + ROPE
    )
    queries = jnp.concatenate(
        [
            projected[..., :NOPE],
            rotate(projected[..., NOPE:], cos_table[:, None, :], sin_table[:, None, :]),
        ],
        -1,
    ).astype(jnp.bfloat16)
    compressed = jnp.dot(normed, attn_full[4], preferred_element_type=jnp.float32)
    normal_latent, inverse_latent = norm_parts(compressed[:, :KV_RANK])
    latent = (normal_latent * attn_full[5].astype(jnp.float32)).astype(jnp.bfloat16)
    rotary_keys = rotate(compressed[:, KV_RANK:], cos_table, sin_table).astype(jnp.bfloat16)
    latent_all, rotary_all = (
        lax.all_gather(latent, "seq", axis=0, tiled=True),
        lax.all_gather(rotary_keys, "seq", axis=0, tiled=True),
    )
    key_count = latent_all.shape[0]
    head_group = math.gcd(HEADS, 8)
    group_count = HEADS // head_group
    first_row = lax.axis_index("seq") * token_count
    allowed = (first_row + jnp.arange(token_count))[:, None] >= jnp.arange(key_count)[None, :]
    up_grouped = (
        attn_full[6].reshape(KV_RANK, group_count, head_group * (NOPE + VDIM)).transpose(1, 0, 2)
    )
    query_grouped = queries.reshape(token_count, group_count, head_group, NOPE + ROPE).transpose(
        1, 0, 2, 3
    )

    def forward_group(operands):
        query_block, up_block = operands
        keys_values = jnp.dot(latent_all, up_block, preferred_element_type=jnp.float32).astype(
            jnp.bfloat16
        )
        keys_values = keys_values.reshape(key_count, head_group, NOPE + VDIM)
        scores = score_block(query_block, keys_values, rotary_all, allowed)
        row_peak = jnp.max(scores, axis=-1, keepdims=True)
        exponent_terms = jnp.exp(scores - row_peak)
        row_totals = jnp.sum(exponent_terms, axis=-1, keepdims=True)
        probabilities = (exponent_terms / row_totals).astype(jnp.bfloat16)
        attended_block = jnp.einsum(
            "htl,lhv->thv",
            probabilities,
            keys_values[..., NOPE:],
            preferred_element_type=jnp.float32,
        )
        return (keys_values, attended_block, (row_peak + jnp.log(row_totals))[..., 0])

    kept_values, attended_grouped, log_totals = lax.map(forward_group, (query_grouped, up_grouped))
    attended_low = (
        attended_grouped.transpose(1, 0, 2, 3)
        .reshape(token_count, HEADS * VDIM)
        .astype(jnp.bfloat16)
    )
    branch = jnp.dot(attended_low, attn_full[7], preferred_element_type=jnp.float32)
    middle = inputs + RESIDUAL_SCALE * branch
    ffn_full = (
        lax.all_gather(ffn_gain, ("dp", "seq"), axis=0, tiled=True),
        lax.all_gather(ffn_gate, ("dp", "seq"), axis=1, tiled=True),
        lax.all_gather(ffn_up, ("dp", "seq"), axis=1, tiled=True),
        lax.all_gather(ffn_down, ("dp", "seq"), axis=0, tiled=True),
    )
    normal_two, inverse_two = norm_parts(middle)
    normed_two = (normal_two * ffn_full[0].astype(jnp.float32)).astype(jnp.bfloat16)
    gate_values = jnp.dot(normed_two, ffn_full[1], preferred_element_type=jnp.float32)
    upward = jnp.dot(normed_two, ffn_full[2], preferred_element_type=jnp.float32)
    activated = (gate_values * jax.nn.sigmoid(gate_values) * upward).astype(jnp.bfloat16)
    layer_output = (
        middle
        + RESIDUAL_SCALE * jnp.dot(activated, ffn_full[3], preferred_element_type=jnp.float32)
    ).astype(jnp.bfloat16)
    grad_out = cotangent.astype(jnp.float32)
    grad_two = (RESIDUAL_SCALE * grad_out).astype(jnp.bfloat16)
    grad_activated = jnp.einsum(
        "td,fd->tf", grad_two, ffn_full[3], preferred_element_type=jnp.float32
    )
    grad_gate, grad_upward = swiglu_back(grad_activated, gate_values, upward)
    grad_normed_two = jnp.einsum(
        "tf,df->td", grad_gate, ffn_full[1], preferred_element_type=jnp.float32
    )
    grad_normed_two = grad_normed_two + jnp.einsum(
        "tf,df->td", grad_upward, ffn_full[2], preferred_element_type=jnp.float32
    )
    grad_middle_norm, grad_ffn_gain_part = norm_back(
        grad_normed_two, normal_two, inverse_two, ffn_full[0].astype(jnp.float32)
    )
    grad_middle = grad_out + grad_middle_norm
    grad_branch = (RESIDUAL_SCALE * grad_middle).astype(jnp.bfloat16)
    own_width = output_proj.shape[0]
    own_start = lax.axis_index(("dp", "seq")) * own_width
    normed_rows = lax.all_gather(normed_two, ("dp", "seq"), axis=0, tiled=True)
    grad_rows = lax.all_gather(grad_two, ("dp", "seq"), axis=0, tiled=True)
    attended_rows = lax.all_gather(attended_low, ("dp", "seq"), axis=0, tiled=True)
    branch_rows = lax.all_gather(grad_branch, ("dp", "seq"), axis=0, tiled=True)
    gate_own = jnp.dot(normed_rows, ffn_gate, preferred_element_type=jnp.float32)
    up_own = jnp.dot(normed_rows, ffn_up, preferred_element_type=jnp.float32)
    activated_own = (gate_own * jax.nn.sigmoid(gate_own) * up_own).astype(jnp.bfloat16)
    grad_act_own = jnp.einsum("td,fd->tf", grad_rows, ffn_down, preferred_element_type=jnp.float32)
    grad_gate_rows, grad_up_rows = swiglu_back(grad_act_own, gate_own, up_own)
    sum_gate = jnp.einsum(
        "td,tf->df", normed_rows, grad_gate_rows, preferred_element_type=jnp.float32
    )
    sum_up = jnp.einsum("td,tf->df", normed_rows, grad_up_rows, preferred_element_type=jnp.float32)
    sum_down = jnp.einsum("tf,td->fd", activated_own, grad_rows, preferred_element_type=jnp.float32)
    attended_own = lax.dynamic_slice_in_dim(attended_rows, own_start, own_width, 1)
    sum_out = jnp.einsum("tk,td->kd", attended_own, branch_rows, preferred_element_type=jnp.float32)
    grad_attended = jnp.einsum(
        "td,kd->tk", grad_branch, attn_full[7], preferred_element_type=jnp.float32
    ).astype(jnp.bfloat16)
    grad_att_grouped = grad_attended.reshape(token_count, group_count, head_group, VDIM).transpose(
        1, 0, 2, 3
    )
    up_back = (
        attn_full[6].reshape(KV_RANK, group_count, head_group * (NOPE + VDIM)).transpose(1, 0, 2)
    )

    def backward_group(carried, operands):
        latent_sum, rotary_sum = carried
        query_block, keys_values, log_block, grad_att, attended_block, up_block = operands
        scores = score_block(query_block, keys_values, rotary_all, allowed)
        probabilities = jnp.exp(scores - log_block[..., None])
        grad_probs = jnp.einsum(
            "thv,lhv->htl", grad_att, keys_values[..., NOPE:], preferred_element_type=jnp.float32
        )
        row_delta = jnp.sum(grad_att.astype(jnp.float32) * attended_block, axis=-1)
        grad_scores = (probabilities * (grad_probs - jnp.transpose(row_delta)[..., None])).astype(
            jnp.bfloat16
        )
        grad_query_nope = (
            jnp.einsum(
                "htl,lhd->thd",
                grad_scores,
                keys_values[..., :NOPE],
                preferred_element_type=jnp.float32,
            )
            * score_scale
        )
        grad_query_rot = (
            jnp.einsum("htl,lr->thr", grad_scores, rotary_all, preferred_element_type=jnp.float32)
            * score_scale
        )
        grad_keys = (
            jnp.einsum(
                "htl,thd->lhd",
                grad_scores,
                query_block[..., :NOPE],
                preferred_element_type=jnp.float32,
            )
            * score_scale
        )
        grad_rotary_part = (
            jnp.einsum(
                "htl,thr->lr",
                grad_scores,
                query_block[..., NOPE:],
                preferred_element_type=jnp.float32,
            )
            * score_scale
        )
        grad_values = jnp.einsum(
            "htl,thv->lhv",
            probabilities.astype(jnp.bfloat16),
            grad_att,
            preferred_element_type=jnp.float32,
        )
        grad_pairs = (
            jnp.concatenate([grad_keys, grad_values], -1)
            .astype(jnp.bfloat16)
            .reshape(key_count, head_group * (NOPE + VDIM))
        )
        grad_up_block = jnp.einsum(
            "lc,lk->ck", latent_all, grad_pairs, preferred_element_type=jnp.float32
        )
        latent_sum = latent_sum + jnp.einsum(
            "lk,ck->lc", grad_pairs, up_block, preferred_element_type=jnp.float32
        )
        return (
            (latent_sum, rotary_sum + grad_rotary_part),
            (jnp.concatenate([grad_query_nope, grad_query_rot], -1), grad_up_block),
        )

    start_sums = (
        jnp.zeros((key_count, KV_RANK), jnp.float32),
        jnp.zeros((key_count, ROPE), jnp.float32),
    )
    (grad_latent_all, grad_rotary_all), (grad_query_grouped, grad_up_grouped) = lax.scan(
        backward_group,
        start_sums,
        (query_grouped, kept_values, log_totals, grad_att_grouped, attended_grouped, up_back),
    )
    grad_latent_up_part = grad_up_grouped.transpose(1, 0, 2).reshape(KV_RANK, HEADS * (NOPE + VDIM))
    grad_latent_own, grad_rotary_own = (
        lax.psum_scatter(
            grad_latent_all.astype(jnp.bfloat16), "seq", scatter_dimension=0, tiled=True
        ).astype(jnp.float32),
        lax.psum_scatter(
            grad_rotary_all.astype(jnp.bfloat16), "seq", scatter_dimension=0, tiled=True
        ).astype(jnp.float32),
    )
    grad_queries = grad_query_grouped.transpose(1, 0, 2, 3).reshape(token_count, HEADS, NOPE + ROPE)
    grad_projected = jnp.concatenate(
        [
            grad_queries[..., :NOPE],
            rotate_back(grad_queries[..., NOPE:], cos_table[:, None, :], sin_table[:, None, :]),
        ],
        -1,
    )
    grad_projected = grad_projected.astype(jnp.bfloat16).reshape(token_count, HEADS * (NOPE + ROPE))
    grad_query_up_part = jnp.einsum(
        "tq,tk->qk", query_normed, grad_projected, preferred_element_type=jnp.float32
    )
    grad_query_normed = jnp.einsum(
        "tk,qk->tq", grad_projected, attn_full[3], preferred_element_type=jnp.float32
    )
    grad_query_latent, grad_query_gain_part = norm_back(
        grad_query_normed, normal_query, inverse_query, attn_full[2].astype(jnp.float32)
    )
    grad_query_latent = grad_query_latent.astype(jnp.bfloat16)
    grad_query_down_part = jnp.einsum(
        "td,tq->dq", normed, grad_query_latent, preferred_element_type=jnp.float32
    )
    grad_normed = jnp.einsum(
        "tq,dq->td", grad_query_latent, attn_full[1], preferred_element_type=jnp.float32
    )
    grad_latent_norm, grad_latent_gain_part = norm_back(
        grad_latent_own, normal_latent, inverse_latent, attn_full[5].astype(jnp.float32)
    )
    grad_compressed = jnp.concatenate(
        [grad_latent_norm, rotate_back(grad_rotary_own, cos_table, sin_table)], -1
    ).astype(jnp.bfloat16)
    grad_latent_down_part = jnp.einsum(
        "td,tc->dc", normed, grad_compressed, preferred_element_type=jnp.float32
    )
    grad_normed = grad_normed + jnp.einsum(
        "tc,dc->td", grad_compressed, attn_full[4], preferred_element_type=jnp.float32
    )
    grad_input_norm, grad_attn_gain_part = norm_back(
        grad_normed, normal_one, inverse_one, attn_full[0].astype(jnp.float32)
    )
    input_grad = grad_middle + grad_input_norm
    attn_grads = (
        lax.psum_scatter(grad_attn_gain_part, ("dp", "seq"), scatter_dimension=0, tiled=True),
        lax.psum_scatter(grad_query_down_part, ("dp", "seq"), scatter_dimension=0, tiled=True),
        lax.psum_scatter(grad_query_gain_part, ("dp", "seq"), scatter_dimension=0, tiled=True),
        lax.psum_scatter(grad_query_up_part, ("dp", "seq"), scatter_dimension=1, tiled=True),
        lax.psum_scatter(grad_latent_down_part, ("dp", "seq"), scatter_dimension=0, tiled=True),
        lax.psum_scatter(grad_latent_gain_part, ("dp", "seq"), scatter_dimension=0, tiled=True),
        lax.psum_scatter(grad_latent_up_part, ("dp", "seq"), scatter_dimension=1, tiled=True),
        lax.psum_scatter(grad_ffn_gain_part, ("dp", "seq"), scatter_dimension=0, tiled=True),
    )
    return (
        layer_output,
        input_grad,
        attn_grads[0],
        attn_grads[1],
        attn_grads[2],
        attn_grads[3],
        attn_grads[4],
        attn_grads[5],
        attn_grads[6],
        sum_out,
        attn_grads[7],
        sum_gate,
        sum_up,
        sum_down,
    )


def solution(mesh):
    in_specs = (
        P(("dp", "seq"), None),
        P(("dp", "seq")),
        P(("dp", "seq")),
        P(("dp", "seq"), None),
        P(("dp", "seq")),
        P(None, ("dp", "seq")),
        P(("dp", "seq"), None),
        P(("dp", "seq")),
        P(None, ("dp", "seq")),
        P(("dp", "seq"), None),
        P(("dp", "seq")),
        P(None, ("dp", "seq")),
        P(None, ("dp", "seq")),
        P(("dp", "seq"), None),
        P(("dp", "seq"), None),
    )
    out_specs = (
        P(("dp", "seq"), None),
        P(("dp", "seq"), None),
        P(("dp", "seq")),
        P(("dp", "seq"), None),
        P(("dp", "seq")),
        P(None, ("dp", "seq")),
        P(("dp", "seq"), None),
        P(("dp", "seq")),
        P(None, ("dp", "seq")),
        P(("dp", "seq"), None),
        P(("dp", "seq")),
        P(None, ("dp", "seq")),
        P(None, ("dp", "seq")),
        P(("dp", "seq"), None),
    )
    return jax.shard_map(
        per_device, mesh=mesh, in_specs=in_specs, out_specs=out_specs, check_vma=False
    )
```

profile of v0, /device:TPU:2, one launch (start us, length us, event | category | flops | bytes accessed | tf_op | source)
XLA Modules:
  0.0 2253.3 jit_solution(14079816641421087543)
XLA Ops:
  13.8 41.6 %all-reduce.9 = (bf16[2560]{0:T(1024)(128)(2,1)S(1)}, bf16[256]{0:T(256)(128)(2,1)S(1)}, bf16[768]{0:T(1024)(128)(2,1)S(1)}, bf16[2560]{0:T(1024)(128)(2,1)S(1)}) all-reduce(bf16[2560]{0:T(1024)(128)(2,1)S(1)} %dynamic-update-slice, bf16[256]{0:T(256)(128)(2,1)S(1)} %dynamic-update-slice.1, ...), channel_id=1, replica_groups=mesh['dp'=4,'seq'=8] {'dp','seq'}, use_global_device_ids=true, to_apply=%add | all-reduce | flops 6144 | bytes 24576
  90.6 37.3 %all-gather.13.cloned.1.call-done = bf16[256,5120]{0,1:T(8,128)(2,1)} async-done(((bf16[256,160]{0,1:T(8,128)(2,1)}), bf16[256,5120]{0,1:T(8,128)(2,1)}) %all-gather.13.cloned.1.call-update) | async-done | bytes 2621456 | tf_op jit(solution)/shard_map/all_gather | solution.py:106
  130.9 60.2 %all-gather.17.cloned.1.call-done = bf16[2560,768]{1,0:T(8,128)(2,1)} async-done(((bf16[80,768]{1,0:T(8,128)(2,1)}), bf16[2560,768]{1,0:T(8,128)(2,1)}) %all-gather.17.cloned.1.call-update) | async-done | bytes 3932176 | tf_op jit(solution)/shard_map/all_gather | solution.py:101
  194.7 65.5 %all-gather.19.cloned.1.call-done = bf16[768,3840]{0,1:T(8,128)(2,1)} async-done(((bf16[768,120]{0,1:T(8,128)(2,1)}), bf16[768,3840]{0,1:T(8,128)(2,1)}) %all-gather.19.cloned.1.call-update) | async-done | bytes 5898256 | tf_op jit(solution)/shard_map/all_gather | solution.py:103
  266.2 49.5 %while.32 = (s32[]{:T(128)}, bf16[5,1024,8,128]{1,3,2,0:T(8,128)(2,1)}, f32[5,128,8,64]{1,3,2,0:T(8,128)}, f32[5,8,128]{2,1,0:T(8,128)}, bf16[5,256,1024]{2,1,0:...) while((s32[]{:T(128)}, ...), condition=%wide.region_6.7_spmd.clone, body=%wide.region_3.6_spmd.clone.sunk | while | flops 883031040 | bytes 31623276 | solution.py:167
  318.9 41.6 %all-gather.21.cloned.1.call-done = bf16[2560,2560]{1,0:T(8,128)(2,1)} async-done(((bf16[80,2560]{1,0:T(8,128)(2,1)}), bf16[2560,2560]{1,0:T(8,128)(2,1)}) %all-gather.21.cloned.1.call-update) | async-done | bytes 13107216 | tf_op jit(solution)/shard_map/all_gather | solution.py:107
  368.7 183.7 %all-gather.23.cloned.1.call-done = bf16[2560,6400]{0,1:T(8,128)(2,1)} async-done(((bf16[2560,200]{0,1:T(8,128)(2,1)}), bf16[2560,6400]{0,1:T(8,128)(2,1)}) %all-gather.23.cloned.1.call-update) | async-done | bytes 32768016 | tf_op jit(solution)/shard_map/all_gather | solution.py:177
  569.5 175.1 %all-gather.25.cloned.1.call-done = bf16[2560,6400]{0,1:T(8,128)(2,1)} async-done(((bf16[2560,200]{0,1:T(8,128)(2,1)}), bf16[2560,6400]{0,1:T(8,128)(2,1)}) %all-gather.25.cloned.1.call-update) | async-done | bytes 32768016 | tf_op jit(solution)/shard_map/all_gather | solution.py:178
  744.6 17.3 fusion.119
  761.9 174.8 %all-gather.27.cloned.1.call-done = bf16[6400,2560]{1,0:T(8,128)(2,1)} async-done(((bf16[200,2560]{1,0:T(8,128)(2,1)}), bf16[6400,2560]{1,0:T(8,128)(2,1)}) %all-gather.27.cloned.1.call-update) | async-done | bytes 32768016 | tf_op jit(solution)/shard_map/all_gather | solution.py:179
  969.4 18.9 multiply_reduce_fusion
  1000.4 93.8 %while.33 = (s32[]{:T(128)}, f32[1024,256]{1,0:T(8,128)S(1)}, f32[1024,32]{0,1:T(8,128)S(1)}, f32[5,128,8,96]{1,3,2,0:T(8,128)}, f32[5,256,1024]{1,2,0:T(8,128)}...) while((s32[]{:T(128)}, f32[1024,256]{1,0:T(8,128)S(1)}, ...), condition=%wide.region_11.12_spmd.clone, body=%wide.region_9.11_spmd.clone.sunk | while | flops 1960934400 | bytes 67263720 | solution.py:304
  1108.1 19.0 reduce-scatter.21.cloned.1.call-done
  1128.0 37.1 %reduce-scatter.19.cloned.1.call-done = bf16[128,256]{1,0:T(8,128)(2,1)} async-done(((bf16[1024,256]{1,0:T(8,128)(2,1)}), bf16[128,256]{1,0:T(8,128)(2,1)}) %reduce-scatter.19.cloned.1.call-update) | async-done | bytes 65552
  1188.4 18.4 fusion.56
  1206.9 41.6 %all-reduce.8 = (f32[2560]{0:T(1024)S(1)}, f32[768]{0:T(1024)S(1)}, f32[256]{0:T(256)S(1)}, f32[2560]{0:T(1024)S(1)}) all-reduce(f32[2560]{0:T(1024)S(1)} %copy-done.36, f32[768]{0:T(1024)S(1)} %copy-done.39, f32[256]{0:T(256)S(1)} %copy-done.49, f32[2560]{0:T(1024)S(1)} %copy-done.43), channel_id=4, replica_groups=mesh['dp'=4,'seq'=8] {'dp','seq'}, use_global_device_ids=true, to_apply=%region_18.19.clone | all-reduce | flops 6144 | bytes 49152
  1250.9 53.6 %all-gather.33.cloned.1.call-done = bf16[4096,2560]{1,0:T(8,128)(2,1)} async-done(((bf16[128,2560]{1,0:T(8,128)(2,1)}), bf16[4096,2560]{1,0:T(8,128)(2,1)}) %all-gather.33.cloned.1.call-update) | async-done | bytes 20971536 | tf_op jit(solution)/shard_map/all_gather | solution.py:209
  1327.3 114.8 %all-gather.29.cloned.1.call-done = bf16[4096,2560]{0,1:T(8,128)(2,1)} async-done(((bf16[128,2560]{0,1:T(8,128)(2,1)}), bf16[4096,2560]{0,1:T(8,128)(2,1)}) %all-gather.29.cloned.1.call-update) | async-done | bytes 20971536 | tf_op jit(solution)/shard_map/all_gather | solution.py:211
  1442.1 136.6 %all-gather.31.cloned.1.call-done = bf16[4096,2560]{1,0:T(8,128)(2,1)} async-done(((bf16[128,2560]{1,0:T(8,128)(2,1)}), bf16[4096,2560]{1,0:T(8,128)(2,1)}) %all-gather.31.cloned.1.call-update) | async-done | bytes 20971536 | tf_op jit(solution)/shard_map/all_gather | solution.py:212
  1590.4 124.2 %all-gather.35.cloned.1.call-done = bf16[4096,2560]{1,0:T(8,128)(2,1)} async-done(((bf16[128,2560]{1,0:T(8,128)(2,1)}), bf16[4096,2560]{1,0:T(8,128)(2,1)}) %all-gather.35.cloned.1.call-update) | async-done | bytes 20971536 | tf_op jit(solution)/shard_map/all_gather | solution.py:210
  1761.1 61.5 %reduce-scatter.15.cloned.1.call-done = f32[80,288]{1,0:T(8,128)} async-done(((f32[2560,288]{1,0:T(8,128)}), f32[80,288]{1,0:T(8,128)}) %reduce-scatter.15.cloned.1.call-update) | async-done | bytes 92176 | tf_op jit(solution)/shard_map/reduce_scatter | solution.py:364
  1822.6 127.5 %reduce-scatter.11.cloned.1.call-done = f32[80,768]{1,0:T(8,128)} async-done(((f32[2560,768]{1,0:T(8,128)}), f32[80,768]{1,0:T(8,128)}) %reduce-scatter.11.cloned.1.call-update) | async-done | bytes 245776 | tf_op jit(solution)/shard_map/reduce_scatter | solution.py:361
  1950.2 139.5 %reduce-scatter.17.cloned.1.call-done = f32[256,160]{0,1:T(8,128)} async-done(((f32[256,5120]{0,1:T(8,128)}), f32[256,160]{0,1:T(8,128)}) %reduce-scatter.17.cloned.1.call-update) | async-done | bytes 163856 | tf_op jit(solution)/shard_map/reduce_scatter | solution.py:366
  2089.7 156.6 %reduce-scatter.13.cloned.1.call-done = f32[768,120]{0,1:T(8,128)} async-done(((f32[768,3840]{0,1:T(8,128)}), f32[768,120]{0,1:T(8,128)}) %reduce-scatter.13.cloned.1.call-update) | async-done | bytes 368656 | tf_op jit(solution)/shard_map/reduce_scatter | solution.py:363
  (397 shorter events, 390.4 us)
Async XLA Ops:
  7.2 61.2 %all-gather.15.cloned.1.call-start = ((), (), s32[]{:S(2)}) async-start(), calls=%async_computation.7 | async-start | bytes 2027520 | tf_op jit(solution)/shard_map/all_gather | solution.py:104
  8.0 119.9 %all-gather.13.cloned.1.call-start = ((), (), s32[]{:S(2)}) async-start(), calls=%async_computation.6 | async-start | bytes 2703360 | tf_op jit(solution)/shard_map/all_gather | solution.py:106
  8.7 182.4 %all-gather.17.cloned.1.call-start = ((), (), s32[]{:S(2)}) async-start(), calls=%async_computation.8 | async-start | bytes 4055040 | tf_op jit(solution)/shard_map/all_gather | solution.py:101
  9.5 250.8 %all-gather.19.cloned.1.call-start = ((), (), s32[]{:S(2)}) async-start(), calls=%async_computation.9 | async-start | bytes 6082560 | tf_op jit(solution)/shard_map/all_gather | solution.py:103
  10.0 350.5 %all-gather.21.cloned.1.call-start = ((), (), s32[]{:S(2)}) async-start(), calls=%async_computation.10 | async-start | bytes 13516800 | tf_op jit(solution)/shard_map/all_gather | solution.py:107
  10.6 541.9 %all-gather.23.cloned.1.call-start = ((), (), s32[]{:S(2)}) async-start(), calls=%async_computation.11 | async-start | bytes 33792000 | tf_op jit(solution)/shard_map/all_gather | solution.py:177
  11.2 733.4 %all-gather.25.cloned.1.call-start = ((), (), s32[]{:S(2)}) async-start(), calls=%async_computation.12 | async-start | bytes 33792000 | tf_op jit(solution)/shard_map/all_gather | solution.py:178
  12.0 924.7 %all-gather.27.cloned.1.call-start = ((), (), s32[]{:S(2)}) async-start(), calls=%async_computation.13 | async-start | bytes 33792000 | tf_op jit(solution)/shard_map/all_gather | solution.py:179
  12.7 1114.4 %reduce-scatter.21.cloned.1.call-start = ((), (), s32[]{:S(2)}) async-start(), calls=%async_computation.23 | async-start | bytes 294912
  55.5 204.7 %copy-start.26 = (f32[768]{0:T(1024)}, f32[768]{0:T(1024)S(1)}, u32[]{:S(2)}) copy-start(f32[768]{0:T(1024)S(1)} %convert_element_type.139) | copy-start | bytes 9220
  81.1 183.9 %copy-start.28 = (f32[128,32]{0,1:T(8,128)}, f32[128,32]{0,1:T(8,128)S(1)}, u32[]{:S(2)}) copy-start(f32[128,32]{0,1:T(8,128)S(1)} %get-tuple-element.358) | copy-start | bytes 49156
  367.5 620.8 %copy-start.48 = (f32[128]{0:T(128)}, f32[128]{0:T(128)S(1)}, u32[]{:S(2)}) copy-start(f32[128]{0:T(128)S(1)} %add_rsqrt_fusion) | copy-start | bytes 1540
  368.7 375.9 %copy-start.10 = (bf16[128,2560]{1,0:T(8,128)(2,1)}, bf16[128,2560]{1,0:T(8,128)(2,1)S(1)}, u32[]{:S(2)}) copy-start(bf16[128,2560]{1,0:T(8,128)(2,1)S(1)} %multiply_convert_fusion.14) | copy-start | bytes 1966084
  569.5 367.2 %copy-start.14 = (bf16[128,2560]{1,0:T(8,128)(2,1)S(1)}, bf16[128,2560]{1,0:T(8,128)(2,1)}, u32[]{:S(2)}) copy-start(bf16[128,2560]{1,0:T(8,128)(2,1)} %param.33) | copy-start | bytes 1966084
  1095.1 69.9 %reduce-scatter.19.cloned.1.call-start = ((), (), s32[]{:S(2)}) async-start(), calls=%async_computation.22 | async-start | bytes 589824
  1096.4 208.1 %all-gather.33.cloned.1.call-start = ((), (), s32[]{:S(2)}) async-start(), calls=%async_computation.20 | async-start | bytes 21626880 | tf_op jit(solution)/shard_map/all_gather | solution.py:209
  1097.2 345.0 %all-gather.29.cloned.1.call-start = ((), (), s32[]{:S(2)}) async-start(), calls=%async_computation.18 | async-start | bytes 21626880 | tf_op jit(solution)/shard_map/all_gather | solution.py:211
  1097.7 480.9 %all-gather.31.cloned.1.call-start = ((), (), s32[]{:S(2)}) async-start(), calls=%async_computation.19 | async-start | bytes 21626880 | tf_op jit(solution)/shard_map/all_gather | solution.py:212
  1098.5 616.2 %all-gather.35.cloned.1.call-start = ((), (), s32[]{:S(2)}) async-start(), calls=%async_computation.21 | async-start | bytes 21626880 | tf_op jit(solution)/shard_map/all_gather | solution.py:210
  1173.9 648.7 %reduce-scatter.15.cloned.1.call-start = ((), (), s32[]{:S(2)}) async-start(), calls=%async_computation.16 | async-start | bytes 4055040 | tf_op jit(solution)/shard_map/reduce_scatter | solution.py:364
  1176.6 773.5 %reduce-scatter.11.cloned.1.call-start = ((), (), s32[]{:S(2)}) async-start(), calls=%async_computation.14 | async-start | bytes 8110080 | tf_op jit(solution)/shard_map/reduce_scatter | solution.py:361
  1181.1 908.5 %reduce-scatter.17.cloned.1.call-start = ((), (), s32[]{:S(2)}) async-start(), calls=%async_computation.17 | async-start | bytes 5406720 | tf_op jit(solution)/shard_map/reduce_scatter | solution.py:366
  1181.7 1064.6 %reduce-scatter.13.cloned.1.call-start = ((), (), s32[]{:S(2)}) async-start(), calls=%async_computation.15 | async-start | bytes 12165120 | tf_op jit(solution)/shard_map/reduce_scatter | solution.py:363
  1327.3 387.4 %copy-start.23 = (bf16[200,2560]{1,0:T(8,128)(2,1)S(1)}, bf16[200,2560]{1,0:T(8,128)(2,1)}, u32[]{:S(2)}) copy-start(bf16[200,2560]{1,0:T(8,128)(2,1)} %param.32) | copy-start | bytes 3072004
  (63 other events, 1889.2 us)
Sparse Core Ops, SparseCore 0:
  11.0 57.4 all-gather.14
  71.3 56.5 all-gather.12
  130.8 60.2 all-gather.16
  193.9 66.3 all-gather.18
  262.9 97.5 all-gather.20
  363.2 189.2 all-gather.22
  555.3 189.1 all-gather.24
  747.4 189.1 all-gather.26
  1095.3 31.7 reduce-scatter.20
  1130.9 34.1 reduce-scatter.18
  1167.9 136.5 all-gather.32
  1306.4 135.6 all-gather.28
  1445.0 133.6 all-gather.30
  1582.0 132.6 all-gather.34
  1720.5 102.0 reduce-scatter.14
  1828.7 121.4 reduce-scatter.10
  1953.0 136.6 reduce-scatter.16
  2097.2 148.9 reduce-scatter.12
where the time goes:
time: 2260 us; the launch traced here: 2250 us
  waiting for transfers between devices  1730 us (77%)
  matrix products  319 us (14%)
  blocking collectives  102 us (5%)
  local copies, waits for them, and re-layouts  51.6 us (2%)
  other arithmetic  34.1 us (2%)
    all_gather x1, waiting for transfers between devices, per_device(): lax.all_gather(ffn_gate, ('dp', 'seq'), axis=1, tiled=True)  184 us
    all_gather x1, waiting for transfers between devices, per_device(): lax.all_gather(ffn_up, ('dp', 'seq'), axis=1, tiled=True)  175 us
    all_gather x1, waiting for transfers between devices, per_device(): lax.all_gather(ffn_down, ('dp', 'seq'), axis=0, tiled=True)  175 us
    reduce_scatter x1, waiting for transfers between devices, per_device(): lax.psum_scatter(grad_query_up_part, ('dp', 'seq'), scatter_dimension=1,...  157 us
    reduce_scatter x1, waiting for transfers between devices, per_device(): lax.psum_scatter(grad_latent_up_part, ('dp', 'seq'), scatter_dimension=1,...  140 us
    all_gather x1, waiting for transfers between devices, per_device(): branch_rows = lax.all_gather(grad_branch, ('dp', 'seq'), axis=0, tiled=True)  137 us
    reduce_scatter x1, waiting for transfers between devices, per_device(): lax.psum_scatter(grad_query_down_part, ('dp', 'seq'), scatter_dimension=0...  128 us
    all_gather x1, waiting for transfers between devices, per_device(): grad_rows = lax.all_gather(grad_two, ('dp', 'seq'), axis=0, tiled=True)  124 us
  transfers between devices with their start and end apart: 18, of which 18 were waited for; matrix products, arithmetic and copies ran while one was open for 11% of the time, Pallas kernels for 0%

commit v1 on v0

v1 whole, which is shorter than its diff:
```python
import math

import jax
import jax.numpy as jnp
from jax import lax
from jax.experimental import pallas as pl
from jax.experimental.pallas import tpu as pltpu
from jax.sharding import PartitionSpec as P

KV_RANK = 256
HEADS = 40
NOPE = 64
ROPE = 32
VDIM = 64


EPSILON = 1e-05
RESIDUAL_SCALE = 1.4 / math.sqrt(62.0)
F32 = jnp.float32
BF16 = jnp.bfloat16


def norm_parts(values):
    inverse = lax.rsqrt(jnp.mean(values * values, axis=-1, keepdims=True) + EPSILON)
    return (values * inverse, inverse)


def norm_back(grad_scaled, normalized, inverse, scale_gain):
    gain_grad = jnp.sum(grad_scaled * normalized, axis=0)
    grad_normal = grad_scaled * scale_gain
    values_grad = inverse * (
        grad_normal - normalized * jnp.mean(grad_normal * normalized, axis=-1, keepdims=True)
    )
    return (values_grad, gain_grad)


def rotary_tables(positions):
    half_width = ROPE // 2
    inverse = 10000.0 ** (-2.0 * jnp.arange(half_width, dtype=F32) / ROPE)
    angles = positions.astype(F32)[:, None] * inverse[None, :]
    cos_table = jnp.cos(angles)
    sin_table = jnp.sin(angles)
    return (
        jnp.concatenate([cos_table, cos_table], -1),
        jnp.concatenate([sin_table, sin_table], -1),
    )


def rotate(values, cos_table, sin_table):
    half_width = values.shape[-1] // 2
    turned = jnp.concatenate([-values[..., half_width:], values[..., :half_width]], -1)
    return values * cos_table + turned * sin_table


def rotate_back(grads, cos_table, sin_table):
    half_width = grads.shape[-1] // 2
    scaled = grads * sin_table
    return grads * cos_table + jnp.concatenate(
        [scaled[..., half_width:], -scaled[..., :half_width]], -1
    )


def score_block(query_block, keys_values, rotary_all, allowed):
    score_scale = (NOPE + ROPE) ** (-0.5)
    scores = jnp.einsum(
        "thd,lhd->htl",
        query_block[..., :NOPE],
        keys_values[..., :NOPE],
        preferred_element_type=F32,
    )
    scores = scores + jnp.einsum(
        "thr,lr->htl", query_block[..., NOPE:], rotary_all, preferred_element_type=F32
    )
    return jnp.where(allowed[None], scores * score_scale, -1e30)


def dot(spec, left, right):
    return jnp.einsum(spec, left, right, preferred_element_type=F32)


def shift(value, axis, count, step):
    return lax.ppermute(value, axis, [(i, (i + step) % count) for i in range(count)])


def gather_dp(value, count):
    return [value] + [shift(value, "dp", count, k) for k in range(1, count)]


def scatter_dp(parts, count):
    total = parts[0].astype(F32)
    for k in range(1, count):
        total = total + shift(parts[k].astype(BF16), "dp", count, -k).astype(F32)
    return total


def gather_all(rows, dp_count):
    by_place = jnp.stack(gather_dp(rows, dp_count))
    place = lax.axis_index("dp")
    order = (place - jnp.arange(dp_count)) % dp_count
    absolute = jnp.take(by_place, order, axis=0)
    whole = lax.all_gather(absolute, "seq", axis=1, tiled=True)
    return whole.reshape(-1, rows.shape[1])


def scatter_all(grads, dp_count):
    blocks = grads.astype(BF16).reshape(dp_count, -1, grads.shape[1])
    own_seq = lax.psum_scatter(blocks, "seq", scatter_dimension=1, tiled=True)
    place = lax.axis_index("dp")
    parts = [
        lax.dynamic_index_in_dim(own_seq, (place - k) % dp_count, 0, keepdims=False)
        for k in range(dp_count)
    ]
    return scatter_dp(parts, dp_count)


def per_device_general(
    dp_count,
    layer_input,
    positions,
    attn_gain,
    query_down,
    query_gain,
    query_up,
    latent_down,
    latent_gain,
    latent_up,
    output_proj,
    ffn_gain,
    ffn_gate,
    ffn_up,
    ffn_down,
    cotangent,
):
    token_count, width = layer_input.shape
    query_rank = query_down.shape[1]
    own_rows = query_down.shape[0]
    score_scale = (NOPE + ROPE) ** (-0.5)

    def column(gain):
        return jnp.pad(gain, (0, own_rows - gain.shape[0]))[:, None]

    down_width = query_rank + KV_RANK + ROPE
    pad_width = -(down_width + 4) % 128
    packed = jnp.concatenate(
        [
            query_down,
            latent_down,
            column(attn_gain),
            column(ffn_gain),
            column(query_gain),
            column(latent_gain),
            jnp.zeros((own_rows, pad_width), BF16),
        ],
        1,
    )
    packed_full = gather_all(packed, dp_count)
    down_full = packed_full[:, :down_width]
    gains = packed_full[:, down_width : down_width + 4].T.astype(F32)
    attn_gain_full = gains[0]
    ffn_gain_full = gains[1]

    def short_gain(row, own):
        return row.reshape(-1, own_rows)[:, : own.shape[0]].reshape(-1)

    query_gain_full = short_gain(gains[2], query_gain)
    latent_gain_full = short_gain(gains[3], latent_gain)

    query_up_full = gather_all(query_up.T, dp_count)
    latent_up_full = gather_all(latent_up.T, dp_count)
    proj_full = gather_all(output_proj, dp_count)
    gate_full = lax.all_gather(ffn_gate.T, "seq", axis=0, tiled=True)
    upward_full = lax.all_gather(ffn_up.T, "seq", axis=0, tiled=True)
    ffn_down_full = lax.all_gather(ffn_down, "seq", axis=0, tiled=True)

    grad_out = cotangent.astype(F32)
    grad_two = (RESIDUAL_SCALE * grad_out).astype(BF16)
    grad_rows = jnp.concatenate(gather_dp(grad_two, dp_count))

    inputs = layer_input.astype(F32)
    cos_table, sin_table = rotary_tables(positions)
    normal_one, inverse_one = norm_parts(inputs)
    normed = (normal_one * attn_gain_full).astype(BF16)
    down_out = jnp.dot(normed, down_full, preferred_element_type=F32)
    query_latent = down_out[:, :query_rank]
    compressed = down_out[:, query_rank:]
    normal_latent, inverse_latent = norm_parts(compressed[:, :KV_RANK])
    latent = (normal_latent * latent_gain_full).astype(BF16)
    rotary_keys = rotate(compressed[:, KV_RANK:], cos_table, sin_table).astype(BF16)
    keys_all = lax.all_gather(
        jnp.concatenate([latent, rotary_keys], -1), "seq", axis=0, tiled=True
    )
    latent_all = keys_all[:, :KV_RANK]
    rotary_all = keys_all[:, KV_RANK:]
    normal_query, inverse_query = norm_parts(query_latent)
    query_normed = (normal_query * query_gain_full).astype(BF16)
    projected = dot("tq,kq->tk", query_normed, query_up_full).reshape(
        token_count, HEADS, NOPE + ROPE
    )
    queries = jnp.concatenate(
        [
            projected[..., :NOPE],
            rotate(projected[..., NOPE:], cos_table[:, None, :], sin_table[:, None, :]),
        ],
        -1,
    ).astype(BF16)
    key_count = latent_all.shape[0]
    head_group = math.gcd(HEADS, 8)
    group_count = HEADS // head_group
    first_row = lax.axis_index("seq") * token_count
    allowed = (first_row + jnp.arange(token_count))[:, None] >= jnp.arange(key_count)[None, :]
    up_grouped = latent_up_full.reshape(group_count, head_group * (NOPE + VDIM), KV_RANK)
    query_grouped = queries.reshape(token_count, group_count, head_group, NOPE + ROPE).transpose(
        1, 0, 2, 3
    )

    def forward_group(operands):
        query_block, up_block = operands
        keys_values = dot("lc,kc->lk", latent_all, up_block).astype(BF16)
        keys_values = keys_values.reshape(key_count, head_group, NOPE + VDIM)
        scores = score_block(query_block, keys_values, rotary_all, allowed)
        row_peak = jnp.max(scores, axis=-1, keepdims=True)
        exponent_terms = jnp.exp(scores - row_peak)
        row_totals = jnp.sum(exponent_terms, axis=-1, keepdims=True)
        probabilities = (exponent_terms / row_totals).astype(BF16)
        attended_block = dot("htl,lhv->thv", probabilities, keys_values[..., NOPE:])
        return (keys_values, attended_block, (row_peak + jnp.log(row_totals))[..., 0])

    kept_values, attended_grouped, log_totals = lax.map(forward_group, (query_grouped, up_grouped))
    attended_low = (
        attended_grouped.transpose(1, 0, 2, 3).reshape(token_count, HEADS * VDIM).astype(BF16)
    )
    branch = jnp.dot(attended_low, proj_full, preferred_element_type=F32)
    middle = inputs + RESIDUAL_SCALE * branch
    normal_two, inverse_two = norm_parts(middle)
    normed_two = (normal_two * ffn_gain_full).astype(BF16)

    normed_rows = jnp.concatenate(gather_dp(normed_two, dp_count))
    gate_values = dot("td,fd->tf", normed_rows, gate_full)
    upward = dot("td,fd->tf", normed_rows, upward_full)
    grad_activated = dot("td,fd->tf", grad_rows, ffn_down_full)
    sigmoid_gate = jax.nn.sigmoid(gate_values)
    activated = (gate_values * sigmoid_gate * upward).astype(BF16)
    grad_upward = (grad_activated * gate_values * sigmoid_gate).astype(BF16)
    grad_gate = (
        grad_activated * upward * sigmoid_gate * (1.0 + gate_values * (1.0 - sigmoid_gate))
    ).astype(BF16)
    grad_normed_part = dot("tf,fd->td", grad_gate, gate_full) + dot(
        "tf,fd->td", grad_upward, upward_full
    )
    grad_normed_two = scatter_dp(jnp.split(grad_normed_part, dp_count), dp_count)
    down_part = dot("tf,fd->td", activated, ffn_down_full)
    layer_output = (
        middle + RESIDUAL_SCALE * scatter_dp(jnp.split(down_part, dp_count), dp_count)
    ).astype(BF16)

    def scatter_seq(grads):
        return lax.psum_scatter(
            grads.astype(BF16), "seq", scatter_dimension=0, tiled=True
        ).astype(F32)

    sum_down = scatter_seq(dot("tf,td->fd", activated, grad_rows))
    sum_gate = scatter_seq(dot("tf,td->fd", grad_gate, normed_rows)).T
    sum_up = scatter_seq(dot("tf,td->fd", grad_upward, normed_rows)).T

    grad_middle_norm, grad_ffn_gain_part = norm_back(
        grad_normed_two, normal_two, inverse_two, ffn_gain_full
    )
    grad_middle = grad_out + grad_middle_norm
    grad_branch = (RESIDUAL_SCALE * grad_middle).astype(BF16)
    sum_out = scatter_all(dot("tk,td->kd", attended_low, grad_branch), dp_count)
    grad_attended = dot("td,kd->tk", grad_branch, proj_full).astype(BF16)
    grad_att_grouped = grad_attended.reshape(token_count, group_count, head_group, VDIM).transpose(
        1, 0, 2, 3
    )

    def backward_group(carried, operands):
        latent_sum, rotary_sum = carried
        query_block, keys_values, log_block, grad_att, attended_block, up_block = operands
        scores = score_block(query_block, keys_values, rotary_all, allowed)
        probabilities = jnp.exp(scores - log_block[..., None])
        grad_probs = dot("thv,lhv->htl", grad_att, keys_values[..., NOPE:])
        row_delta = jnp.sum(grad_att.astype(F32) * attended_block, axis=-1)
        grad_scores = (probabilities * (grad_probs - jnp.transpose(row_delta)[..., None])).astype(
            BF16
        )
        grad_query_nope = dot("htl,lhd->thd", grad_scores, keys_values[..., :NOPE]) * score_scale
        grad_query_rot = dot("htl,lr->thr", grad_scores, rotary_all) * score_scale
        grad_keys = dot("htl,thd->lhd", grad_scores, query_block[..., :NOPE]) * score_scale
        grad_rotary_part = dot("htl,thr->lr", grad_scores, query_block[..., NOPE:]) * score_scale
        grad_values = dot("htl,thv->lhv", probabilities.astype(BF16), grad_att)
        grad_pairs = (
            jnp.concatenate([grad_keys, grad_values], -1)
            .astype(BF16)
            .reshape(key_count, head_group * (NOPE + VDIM))
        )
        grad_up_block = dot("lk,lc->kc", grad_pairs, latent_all)
        latent_sum = latent_sum + dot("lk,kc->lc", grad_pairs, up_block)
        return (
            (latent_sum, rotary_sum + grad_rotary_part),
            (jnp.concatenate([grad_query_nope, grad_query_rot], -1), grad_up_block),
        )

    start_sums = (
        jnp.zeros((key_count, KV_RANK), F32),
        jnp.zeros((key_count, ROPE), F32),
    )
    (grad_latent_all, grad_rotary_all), (grad_query_grouped, grad_up_grouped) = lax.scan(
        backward_group,
        start_sums,
        (query_grouped, kept_values, log_totals, grad_att_grouped, attended_grouped, up_grouped),
    )
    sum_latent_up = scatter_all(
        grad_up_grouped.reshape(HEADS * (NOPE + VDIM), KV_RANK), dp_count
    ).T
    grad_keys_own = lax.psum_scatter(
        jnp.concatenate([grad_latent_all, grad_rotary_all], -1).astype(BF16),
        "seq",
        scatter_dimension=0,
        tiled=True,
    ).astype(F32)
    grad_latent_own = grad_keys_own[:, :KV_RANK]
    grad_rotary_own = grad_keys_own[:, KV_RANK:]
    grad_queries = grad_query_grouped.transpose(1, 0, 2, 3).reshape(token_count, HEADS, NOPE + ROPE)
    grad_projected = jnp.concatenate(
        [
            grad_queries[..., :NOPE],
            rotate_back(grad_queries[..., NOPE:], cos_table[:, None, :], sin_table[:, None, :]),
        ],
        -1,
    )
    grad_projected = grad_projected.astype(BF16).reshape(token_count, HEADS * (NOPE + ROPE))
    sum_query_up = scatter_all(dot("tk,tq->kq", grad_projected, query_normed), dp_count).T
    grad_query_normed = dot("tk,kq->tq", grad_projected, query_up_full)
    grad_query_latent, grad_query_gain_part = norm_back(
        grad_query_normed, normal_query, inverse_query, query_gain_full
    )
    grad_latent_norm, grad_latent_gain_part = norm_back(
        grad_latent_own, normal_latent, inverse_latent, latent_gain_full
    )
    grad_down_out = jnp.concatenate(
        [
            grad_query_latent,
            grad_latent_norm,
            rotate_back(grad_rotary_own, cos_table, sin_table),
        ],
        -1,
    ).astype(BF16)
    grad_down_part = dot("td,tc->dc", normed, grad_down_out)
    grad_normed = dot("tc,dc->td", grad_down_out, down_full)
    grad_input_norm, grad_attn_gain_part = norm_back(
        grad_normed, normal_one, inverse_one, attn_gain_full
    )
    input_grad = grad_middle + grad_input_norm

    def short_column(grads, own):
        blocks = grads.reshape(-1, own.shape[0])
        return jnp.pad(blocks, ((0, 0), (0, own_rows - own.shape[0]))).reshape(-1)

    gain_columns = jnp.stack(
        [
            grad_attn_gain_part,
            grad_ffn_gain_part,
            short_column(grad_query_gain_part, query_gain),
            short_column(grad_latent_gain_part, latent_gain),
        ],
        1,
    )
    sum_packed = scatter_all(
        jnp.concatenate([grad_down_part, gain_columns, jnp.zeros((width, pad_width), F32)], 1),
        dp_count,
    )
    sum_gains = sum_packed[:, down_width : down_width + 4].T
    return (
        layer_output,
        input_grad,
        sum_gains[0],
        sum_packed[:, :query_rank],
        sum_gains[2][: query_gain.shape[0]],
        sum_query_up,
        sum_packed[:, query_rank:down_width],
        sum_gains[3][: latent_gain.shape[0]],
        sum_latent_up,
        sum_out,
        sum_gains[1],
        sum_gate,
        sum_up,
        sum_down,
    )


HEAD_LANES = 128
SCORE_SCALE = (NOPE + ROPE) ** (-0.5)
QUERY_BLOCK = 256


def head_keys(pairs, rotary):
    lane = lax.broadcasted_iota(jnp.int32, pairs.shape, 1)
    return jnp.where(lane < NOPE, pairs, rotary)


def block_scores(query, keys, start):
    scores = lax.dot_general(
        query, keys, (((1,), (1,)), ((), ())), preferred_element_type=F32
    )
    row = start + lax.broadcasted_iota(jnp.int32, scores.shape, 0)
    column = lax.broadcasted_iota(jnp.int32, scores.shape, 1)
    return jnp.where(row >= column, scores * SCORE_SCALE, -1e30)


def turn(values, cos_ref, left_ref, right_ref, sign):
    half = ROPE // 2
    return (
        values * cos_ref
        + sign * (pltpu.roll(values, HEAD_LANES - half, 1) * left_ref)
        + sign * (pltpu.roll(values, half, 1) * right_ref)
    )


def attend_kernel(
    projected_ref, pairs_ref, rotary_ref, cos_ref, left_ref, right_ref,
    query_ref, attended_ref, log_ref, keys_ref,
):
    length = projected_ref.shape[0]
    block = min(QUERY_BLOCK, length)
    keys_ref[...] = head_keys(pairs_ref[...], rotary_ref[...])
    for start in range(0, length, block):
        rows = pl.ds(start, block)
        stop = start + block
        query = turn(
            projected_ref[rows, :], cos_ref[rows, :], left_ref[rows, :], right_ref[rows, :], 1.0
        ).astype(BF16)
        query_ref[rows, :] = query
        scores = block_scores(query, keys_ref[0:stop, :], start)
        peak = jnp.max(scores, axis=-1, keepdims=True)
        terms = jnp.exp(scores - peak)
        totals = jnp.sum(terms, axis=-1, keepdims=True)
        probs = (terms / totals).astype(BF16)
        mixed = jnp.dot(probs, pairs_ref[0:stop, :], preferred_element_type=F32)
        lane = lax.broadcasted_iota(jnp.int32, mixed.shape, 1)
        attended_ref[rows, :] = jnp.where(lane >= NOPE, mixed, 0.0).astype(BF16)
        log_ref[rows, :] = jnp.broadcast_to(peak + jnp.log(totals), mixed.shape)


def attend(projected, pairs, rotary, tables):
    length, lanes = projected.shape
    own = pl.BlockSpec((length, HEAD_LANES), lambda h: (0, h))
    shared = pl.BlockSpec((length, HEAD_LANES), lambda h: (0, 0))
    return pl.pallas_call(
        attend_kernel,
        grid=(lanes // HEAD_LANES,),
        in_specs=[own, own, shared, shared, shared, shared],
        out_specs=[own, own, own],
        out_shape=[
            jax.ShapeDtypeStruct((length, lanes), BF16),
            jax.ShapeDtypeStruct((length, lanes), BF16),
            jax.ShapeDtypeStruct((length, lanes), F32),
        ],
        scratch_shapes=[pltpu.VMEM((length, HEAD_LANES), BF16)],
        compiler_params=pltpu.CompilerParams(vmem_limit_bytes=40 * 1024 * 1024),
        cost_estimate=pl.CostEstimate(
            flops=3 * lanes * length * length, bytes_accessed=12 * lanes * length,
            transcendentals=length * length * lanes // HEAD_LANES,
        ),
        name="attend",
    )(projected, pairs, rotary, *tables)


def attend_back_kernel(
    query_ref, pairs_ref, rotary_ref, log_ref, grad_ref, cos_ref, left_ref, right_ref,
    grad_query_ref, grad_pairs_ref, grad_rotary_ref, keys_ref, grad_keys_ref, grad_values_ref,
):
    length = query_ref.shape[0]
    block = min(QUERY_BLOCK, length)
    keys_ref[...] = head_keys(pairs_ref[...], rotary_ref[...])
    grad_keys_ref[...] = jnp.zeros_like(grad_keys_ref)
    grad_values_ref[...] = jnp.zeros_like(grad_values_ref)
    for start in range(0, length, block):
        rows = pl.ds(start, block)
        stop = start + block
        query = query_ref[rows, :]
        grad = grad_ref[rows, :]
        scores = block_scores(query, keys_ref[0:stop, :], start)
        probs = jnp.exp(scores - log_ref[rows, 0:1])
        grad_probs = lax.dot_general(
            grad, pairs_ref[0:stop, :], (((1,), (1,)), ((), ())), preferred_element_type=F32
        )
        delta = jnp.sum(probs * grad_probs, axis=-1, keepdims=True)
        grad_scores = (probs * (grad_probs - delta)).astype(BF16)
        grad_query = (
            jnp.dot(grad_scores, keys_ref[0:stop, :], preferred_element_type=F32) * SCORE_SCALE
        )
        grad_query_ref[rows, :] = turn(
            grad_query, cos_ref[rows, :], left_ref[rows, :], right_ref[rows, :], -1.0
        ).astype(BF16)
        grad_keys_ref[:, 0:stop] += jnp.dot(
            query.T, grad_scores, preferred_element_type=F32
        )
        grad_values_ref[:, 0:stop] += jnp.dot(
            grad.T, probs.astype(BF16), preferred_element_type=F32
        )
    grad_keys = grad_keys_ref[...].T * SCORE_SCALE
    lane = lax.broadcasted_iota(jnp.int32, grad_keys.shape, 1)
    grad_pairs_ref[...] = jnp.where(lane < NOPE, grad_keys, grad_values_ref[...].T).astype(BF16)

    @pl.when(pl.program_id(0) == 0)
    def _():
        grad_rotary_ref[...] = jnp.zeros_like(grad_rotary_ref)

    grad_rotary_ref[...] += grad_keys


def attend_back(query, pairs, rotary, logs, grad, tables):
    length, lanes = query.shape
    own = pl.BlockSpec((length, HEAD_LANES), lambda h: (0, h))
    shared = pl.BlockSpec((length, HEAD_LANES), lambda h: (0, 0))
    return pl.pallas_call(
        attend_back_kernel,
        grid=(lanes // HEAD_LANES,),
        in_specs=[own, own, shared, own, own, shared, shared, shared],
        out_specs=[own, own, shared],
        out_shape=[
            jax.ShapeDtypeStruct((length, lanes), BF16),
            jax.ShapeDtypeStruct((length, lanes), BF16),
            jax.ShapeDtypeStruct((length, HEAD_LANES), F32),
        ],
        scratch_shapes=[
            pltpu.VMEM((length, HEAD_LANES), BF16),
            pltpu.VMEM((HEAD_LANES, length), F32),
            pltpu.VMEM((HEAD_LANES, length), F32),
        ],
        compiler_params=pltpu.CompilerParams(vmem_limit_bytes=48 * 1024 * 1024),
        cost_estimate=pl.CostEstimate(
            flops=8 * lanes * length * length, bytes_accessed=14 * lanes * length,
            transcendentals=length * length * lanes // HEAD_LANES,
        ),
        name="attend_back",
    )(query, pairs, rotary, logs, grad, *tables)


def ffn_kernel(
    weights_ref, rows_ref, grads_ref,
    hidden_ref, grad_rows_ref, out_rows_ref, grad_sum_ref, out_sum_ref,
):
    step = pl.program_id(0)
    hidden = weights_ref.shape[1] // 3

    def against(rows, start):
        return lax.dot_general(
            rows[...], weights_ref[0, start : start + hidden, :], (((1,), (1,)), ((), ())),
            preferred_element_type=F32,
        )

    gate_values = against(rows_ref, 0)
    upward = against(rows_ref, hidden)
    grad_activated = against(grads_ref, 2 * hidden)
    sigmoid_gate = jax.nn.sigmoid(gate_values)
    activated = gate_values * sigmoid_gate * upward
    grad_upward = grad_activated * gate_values * sigmoid_gate
    grad_gate = (
        grad_activated * upward * sigmoid_gate * (1.0 + gate_values * (1.0 - sigmoid_gate))
    )
    hidden_ref[0, 0:hidden, :] = grad_gate.T.astype(BF16)
    hidden_ref[0, hidden : 2 * hidden, :] = grad_upward.T.astype(BF16)
    hidden_ref[0, 2 * hidden : 3 * hidden, :] = activated.T.astype(BF16)

    def through(values, start):
        return jnp.dot(
            values.astype(BF16), weights_ref[0, start : start + hidden, :],
            preferred_element_type=F32,
        )

    grad_part = through(grad_gate, 0) + through(grad_upward, hidden)
    out_part = through(activated, 2 * hidden)

    @pl.when(step == 0)
    def _():
        grad_sum_ref[...] = grad_part
        out_sum_ref[...] = out_part

    @pl.when(step > 0)
    def _():
        grad_sum_ref[...] += grad_part
        out_sum_ref[...] += out_part

    @pl.when(step == pl.num_programs(0) - 1)
    def _():
        grad_rows_ref[...] = grad_sum_ref[...].astype(BF16)
        out_rows_ref[...] = out_sum_ref[...].astype(BF16)


def feed_forward(weights, rows, grads):
    steps, triple, width = weights.shape
    count = rows.shape[0]
    whole = pl.BlockSpec(memory_space=pltpu.VMEM)
    return pl.pallas_call(
        ffn_kernel,
        grid=(steps,),
        in_specs=[pl.BlockSpec((1, triple, width), lambda i: (i, 0, 0)), whole, whole],
        out_specs=[pl.BlockSpec((1, triple, count), lambda i: (i, 0, 0)), whole, whole],
        out_shape=[
            jax.ShapeDtypeStruct((steps, triple, count), BF16),
            jax.ShapeDtypeStruct((count, width), BF16),
            jax.ShapeDtypeStruct((count, width), BF16),
        ],
        scratch_shapes=[pltpu.VMEM((count, width), F32), pltpu.VMEM((count, width), F32)],
        compiler_params=pltpu.CompilerParams(vmem_limit_bytes=56 * 1024 * 1024),
        cost_estimate=pl.CostEstimate(
            flops=4 * steps * triple * width * count,
            bytes_accessed=2 * steps * triple * (width + count) + 8 * count * width,
            transcendentals=steps * triple * count // 3,
        ),
        name="feed_forward",
    )(weights, rows, grads)


def ffn_grads_kernel(hidden_ref, rows_ref, grads_ref, out_ref):
    hidden = hidden_ref.shape[1] // 3
    for start, source in ((0, rows_ref), (hidden, rows_ref), (2 * hidden, grads_ref)):
        out_ref[0, start : start + hidden, :] = jnp.dot(
            hidden_ref[0, start : start + hidden, :], source[...], preferred_element_type=F32
        ).astype(BF16)


def ffn_grads(hidden, rows, grads):
    steps, triple, count = hidden.shape
    width = rows.shape[1]
    whole = pl.BlockSpec(memory_space=pltpu.VMEM)
    return pl.pallas_call(
        ffn_grads_kernel,
        grid=(steps,),
        in_specs=[pl.BlockSpec((1, triple, count), lambda i: (i, 0, 0)), whole, whole],
        out_specs=pl.BlockSpec((1, triple, width), lambda i: (i, 0, 0)),
        out_shape=jax.ShapeDtypeStruct((steps, triple, width), BF16),
        compiler_params=pltpu.CompilerParams(vmem_limit_bytes=48 * 1024 * 1024),
        cost_estimate=pl.CostEstimate(
            flops=2 * steps * triple * width * count,
            bytes_accessed=2 * steps * triple * (width + count) + 4 * count * width,
            transcendentals=0,
        ),
        name="ffn_grads",
    )(hidden, rows, grads)


def after(value, *others):
    return lax.optimization_barrier((value,) + others)[0]


def flip(value, count, bits):
    return lax.ppermute(value, "seq", [(i, i ^ bits) for i in range(count)])


def gather_seq(value, count, chip, core, axis=0):
    even = [value] + [flip(value, count, 2 * m) for m in range(1, count // 2)]
    odd = [flip(piece, count, 1) for piece in even]
    shape = value.shape[:axis] + (count // 2, 2) + value.shape[axis:]
    whole = jnp.zeros(shape, value.dtype)
    for pieces, side in ((even, core), (odd, 1 - core)):
        for m, piece in enumerate(pieces):
            start = [0] * len(shape)
            start[axis] = chip ^ m
            start[axis + 1] = side
            whole = lax.dynamic_update_slice(
                whole, jnp.expand_dims(piece, (axis, axis + 1)), start
            )
    return whole


def choose(value, index, axis):
    return lax.dynamic_index_in_dim(value, index, axis, keepdims=False)


def scatter_seq(mine, theirs, count, chip, axis=0):
    half = mine.astype(F32) + flip(theirs.astype(BF16), count, 1).astype(F32)
    total = choose(half, chip, axis)
    half_low = half.astype(BF16)
    for m in range(1, count // 2):
        total = total + flip(choose(half_low, chip ^ m, axis), count, 2 * m).astype(F32)
    return total


def per_device_heads(
    dp_count,
    seq_count,
    layer_input,
    positions,
    attn_gain,
    query_down,
    query_gain,
    query_up,
    latent_down,
    latent_gain,
    latent_up,
    output_proj,
    ffn_gain,
    ffn_gate,
    ffn_up,
    ffn_down,
    cotangent,
):
    tokens, width = layer_input.shape
    query_rank = query_down.shape[1]
    own_rows = query_down.shape[0]
    down_width = query_rank + KV_RANK + ROPE
    heads = HEADS // seq_count
    place = lax.axis_index("dp")
    spot = lax.axis_index("seq")
    chip, core = spot // 2, spot % 2
    chips = seq_count // 2
    both = ("dp", "seq")
    devices = dp_count * seq_count
    length = seq_count * tokens

    def by_core(value):
        value = value.reshape(chips, 2, tokens, value.shape[1])
        return choose(value, core, 1), choose(value, 1 - core, 1)

    def gather_dp_ordered(value):
        whole = jnp.zeros((dp_count,) + value.shape, value.dtype)
        for k, piece in enumerate(gather_dp(value, dp_count)):
            whole = lax.dynamic_update_index_in_dim(whole, piece, (place - k) % dp_count, 0)
        return whole

    def scatter_dp_ordered(blocks):
        return scatter_dp(
            [choose(blocks, (place - k) % dp_count, 0) for k in range(dp_count)], dp_count
        )

    padded_width = down_width + 4 + -(down_width + 4) % HEAD_LANES

    def column(gain):
        return jnp.pad(gain, (0, own_rows - gain.shape[0]))[:, None]

    down_own = jnp.concatenate(
        [
            query_down,
            latent_down,
            column(attn_gain),
            column(ffn_gain),
            column(query_gain),
            column(latent_gain),
            jnp.zeros((own_rows, padded_width - down_width - 4), BF16),
        ],
        1,
    )
    down_plane = gather_dp_ordered(down_own)
    down_full = gather_seq(down_plane, seq_count, chip, core, 1).reshape(width, padded_width)
    gains = down_full[:, down_width : down_width + 4].T.astype(F32)
    attn_gain_full = gains[0]
    ffn_gain_full = gains[1]

    def short_gain(row, own):
        return row.reshape(devices, own_rows)[:, : own.shape[0]].reshape(-1)

    query_gain_full = short_gain(gains[2], query_gain)
    latent_gain_full = short_gain(gains[3], latent_gain)

    def group_rows(rows):
        whole = jnp.zeros((dp_count,) + rows.shape, rows.dtype)
        for k in range(dp_count):
            pairs = [
                (s * dp_count + (z + k) % dp_count, z * seq_count + s)
                for z in range(dp_count)
                for s in range(seq_count)
            ]
            whole = lax.dynamic_update_index_in_dim(
                whole, lax.ppermute(rows, both, pairs), (place + k) % dp_count, 0
            )
        return whole

    to_owner = [
        (z * seq_count + s, s * dp_count + z) for z in range(dp_count) for s in range(seq_count)
    ]

    def group_home(blocks):
        return lax.ppermute(scatter_dp_ordered(blocks).astype(BF16), both, to_owner).astype(F32)

    up_rows = max(query_up.shape[1], latent_up.shape[1])
    up_packed = jnp.concatenate(
        [
            jnp.pad(query_up.T, ((0, up_rows - query_up.shape[1]), (0, 0))),
            jnp.pad(latent_up.T, ((0, up_rows - latent_up.shape[1]), (0, 0))),
        ],
        1,
    )
    up_group = group_rows(after(up_packed, down_plane))
    query_up_padded = jnp.pad(
        up_group[:, : query_up.shape[1], :query_rank].reshape(heads, NOPE + ROPE, query_rank),
        ((0, 0), (0, HEAD_LANES - NOPE - ROPE), (0, 0)),
    ).reshape(heads * HEAD_LANES, query_rank)
    latent_up_group = up_group[:, : latent_up.shape[1], query_rank:].reshape(-1, KV_RANK)

    inputs = layer_input.astype(F32)
    normal_one, inverse_one = norm_parts(inputs)
    normed = (normal_one * attn_gain_full).astype(BF16)
    normed = after(normed, query_up_padded, latent_up_group)
    down_out = jnp.dot(normed, down_full, preferred_element_type=F32)
    normal_query, inverse_query = norm_parts(down_out[:, :query_rank])
    query_normed = (normal_query * query_gain_full).astype(BF16)
    normal_latent, inverse_latent = norm_parts(down_out[:, query_rank : query_rank + KV_RANK])
    latent = (normal_latent * latent_gain_full).astype(BF16)
    cos_table, sin_table = rotary_tables(positions)
    rotary_keys = rotate(
        down_out[:, query_rank + KV_RANK : down_width], cos_table, sin_table
    ).astype(BF16)
    half = ROPE // 2

    def two_parts(table):
        high = table.astype(BF16)
        return [high, (table - high.astype(F32)).astype(BF16)]

    token_message = jnp.concatenate(
        [query_normed, latent, rotary_keys]
        + two_parts(cos_table[:, :half])
        + two_parts(sin_table[:, :half]),
        1,
    )
    token_all = gather_seq(token_message, seq_count, chip, core).reshape(
        length, token_message.shape[1]
    )
    proj_group = group_rows(after(output_proj, down_full)).reshape(-1, width)
    grad_out = cotangent.astype(F32)
    grad_two = (RESIDUAL_SCALE * grad_out).astype(BF16)
    grad_rows = jnp.concatenate(gather_dp(after(grad_two, proj_group), dp_count))
    proj_padded = jnp.pad(
        proj_group.reshape(heads, VDIM, width), ((0, 0), (HEAD_LANES - VDIM, 0), (0, 0))
    ).reshape(heads * HEAD_LANES, width)
    ffn_own = after(jnp.concatenate([ffn_gate.T, ffn_up.T, ffn_down], 0), down_full)
    ffn_full = lax.all_gather(ffn_own, "seq", axis=0)

    query_normed_all = token_all[:, :query_rank]
    latent_all = token_all[:, query_rank : query_rank + KV_RANK]
    rotary_all = token_all[:, query_rank + KV_RANK : down_width]
    angles = token_all[:, down_width:].astype(F32)
    cos_all = angles[:, :half] + angles[:, half : 2 * half]
    sin_all = angles[:, 2 * half : 3 * half] + angles[:, 3 * half :]

    def lanes(start, values):
        return jnp.pad(values, ((0, 0), (start, HEAD_LANES - start - values.shape[1])))

    tables = (
        jnp.concatenate(
            [
                jnp.ones((length, NOPE), F32),
                cos_all,
                cos_all,
                jnp.zeros((length, HEAD_LANES - NOPE - ROPE), F32),
            ],
            1,
        ),
        lanes(NOPE, -sin_all),
        lanes(NOPE + half, sin_all),
    )
    rotary_lanes = lanes(NOPE, rotary_all)
    projected = dot("tq,kq->tk", query_normed_all, query_up_padded)
    pairs = dot("tc,kc->tk", latent_all, latent_up_group).astype(BF16)
    query, attended, logs = attend(projected, pairs, rotary_lanes, tables)

    attended_mine, attended_theirs = by_core(attended)
    branch = scatter_seq(
        dot("mtk,kd->mtd", attended_mine, proj_padded),
        dot("mtk,kd->mtd", attended_theirs, proj_padded),
        seq_count,
        chip,
    )
    middle = inputs + RESIDUAL_SCALE * branch
    normal_two, inverse_two = norm_parts(middle)
    normed_two = (normal_two * ffn_gain_full).astype(BF16)
    normed_two = after(normed_two, grad_rows)

    normed_rows = jnp.concatenate(gather_dp(normed_two, dp_count))
    proj_full = lax.all_gather(after(proj_group, normed_two), "seq", axis=0, tiled=True)
    hidden, grad_part, out_part = feed_forward(ffn_full, normed_rows, grad_rows)
    grad_parts = jnp.split(grad_part, dp_count)
    returned = [
        shift(grad_parts[k], "dp", dp_count, -k).astype(F32) for k in range(1, dp_count)
    ]
    grad_normed_two = sum(returned, grad_parts[0].astype(F32))
    hidden = after(hidden, returned[0])
    ffn_sums = lax.psum_scatter(
        ffn_grads(hidden, normed_rows, grad_rows), "seq", scatter_dimension=0
    ).astype(F32)
    out_part = after(out_part, grad_normed_two)
    layer_output = (
        middle + RESIDUAL_SCALE * scatter_dp(jnp.split(out_part, dp_count), dp_count)
    ).astype(BF16)

    grad_middle_norm, grad_ffn_gain_part = norm_back(
        grad_normed_two, normal_two, inverse_two, ffn_gain_full
    )
    grad_middle = grad_out + grad_middle_norm
    grad_branch = (RESIDUAL_SCALE * grad_middle).astype(BF16)
    grad_attended = dot("td,kd->tk", grad_branch, proj_full).astype(BF16)
    grad_attended = lax.all_to_all(
        grad_attended.reshape(tokens, seq_count, heads * VDIM).transpose(1, 0, 2),
        "seq",
        split_axis=0,
        concat_axis=0,
        tiled=True,
    ).reshape(length, heads, VDIM)
    grad_attended = jnp.pad(
        grad_attended, ((0, 0), (0, 0), (HEAD_LANES - VDIM, 0))
    ).reshape(length, heads * HEAD_LANES)
    grad_projected, grad_pairs, grad_rotary = attend_back(
        query, pairs, rotary_lanes, logs, grad_attended, tables
    )
    token_grads = []
    for projected_part, pairs_part, rotary_part in zip(
        by_core(grad_projected), by_core(grad_pairs), by_core(grad_rotary)
    ):
        token_grads.append(
            jnp.concatenate(
                [
                    dot("mtk,kq->mtq", projected_part, query_up_padded).astype(BF16),
                    dot("mtk,kc->mtc", pairs_part, latent_up_group).astype(BF16),
                    rotary_part[:, :, NOPE : NOPE + ROPE].astype(BF16),
                ],
                2,
            )
        )
    grad_own = scatter_seq(token_grads[0], token_grads[1], seq_count, chip)

    query_up_grads = dot("tk,tq->kq", grad_projected, query_normed_all).astype(BF16)
    query_up_grads = query_up_grads.reshape(heads, HEAD_LANES, query_rank)[:, : NOPE + ROPE]
    query_up_grads = query_up_grads.reshape(dp_count, -1, query_rank)
    latent_up_grads = dot("tk,tc->kc", grad_pairs, latent_all).astype(BF16)
    latent_up_grads = latent_up_grads.reshape(dp_count, -1, KV_RANK)
    up_grads = jnp.concatenate(
        [
            jnp.pad(
                query_up_grads, ((0, 0), (0, up_rows - query_up_grads.shape[1]), (0, 0))
            ),
            jnp.pad(
                latent_up_grads, ((0, 0), (0, up_rows - latent_up_grads.shape[1]), (0, 0))
            ),
        ],
        2,
    )
    sum_up = group_home(up_grads)
    sum_query_up = sum_up[: query_up.shape[1], :query_rank].T
    sum_latent_up = sum_up[: latent_up.shape[1], query_rank:].T

    branch_all = gather_seq(after(grad_branch, grad_attended), seq_count, chip, core)
    proj_grads = dot("tk,td->kd", attended, branch_all.reshape(length, width)).astype(BF16)
    proj_grads = proj_grads.reshape(heads, HEAD_LANES, width)[:, HEAD_LANES - VDIM :]
    sum_out = group_home(proj_grads.reshape(dp_count, -1, width))

    grad_query_latent, grad_query_gain_part = norm_back(
        grad_own[:, :query_rank], normal_query, inverse_query, query_gain_full
    )
    grad_latent_norm, grad_latent_gain_part = norm_back(
        grad_own[:, query_rank : query_rank + KV_RANK],
        normal_latent,
        inverse_latent,
        latent_gain_full,
    )
    grad_down_out = jnp.concatenate(
        [
            grad_query_latent,
            grad_latent_norm,
            rotate_back(grad_own[:, query_rank + KV_RANK :], cos_table, sin_table),
            jnp.zeros((tokens, padded_width - down_width), F32),
        ],
        -1,
    ).astype(BF16)
    grad_normed = dot("tc,dc->td", grad_down_out, down_full)
    grad_input_norm, grad_attn_gain_part = norm_back(
        grad_normed, normal_one, inverse_one, attn_gain_full
    )
    input_grad = grad_middle + grad_input_norm

    def short_column(grads, own):
        blocks = grads.reshape(devices, own.shape[0])
        return jnp.pad(blocks, ((0, 0), (0, own_rows - own.shape[0]))).reshape(-1)

    gain_columns = jnp.stack(
        [
            grad_attn_gain_part,
            grad_ffn_gain_part,
            short_column(grad_query_gain_part, query_gain),
            short_column(grad_latent_gain_part, latent_gain),
        ],
        1,
    )
    down_sums = dot("td,tc->dc", normed, grad_down_out) + jnp.pad(
        gain_columns, ((0, 0), (down_width, padded_width - down_width - 4))
    )
    down_sums = down_sums.astype(BF16).reshape(dp_count, chips, 2, own_rows, padded_width)
    sum_down = scatter_dp_ordered(
        scatter_seq(
            choose(down_sums, core, 2), choose(down_sums, 1 - core, 2), seq_count, chip, 1
        )
    )
    sum_gains = sum_down[:, down_width : down_width + 4].T
    own_hidden = ffn_down.shape[0]
    return (
        layer_output,
        input_grad,
        sum_gains[0],
        sum_down[:, :query_rank],
        sum_gains[2][: query_gain.shape[0]],
        sum_query_up,
        sum_down[:, query_rank:down_width],
        sum_gains[3][: latent_gain.shape[0]],
        sum_latent_up,
        sum_out,
        sum_gains[1],
        ffn_sums[:own_hidden].T,
        ffn_sums[own_hidden : 2 * own_hidden].T,
        ffn_sums[2 * own_hidden :],
    )


def solution(mesh):
    both = ("dp", "seq")
    dp_count = mesh.shape["dp"]

    seq_count = mesh.shape["seq"]
    by_heads = HEADS % seq_count == 0 and seq_count & (seq_count - 1) == 0

    def run(*arrays):
        if by_heads:
            return per_device_heads(dp_count, seq_count, *arrays)
        return per_device_general(dp_count, *arrays)

    in_specs = (
        P(both, None),
        P(both),
        P(both),
        P(both, None),
        P(both),
        P(None, both),
        P(both, None),
        P(both),
        P(None, both),
        P(both, None),
        P(both),
        P(None, both),
        P(None, both),
        P(both, None),
        P(both, None),
    )
    out_specs = (
        P(both, None),
        P(both, None),
        P(both),
        P(both, None),
        P(both),
        P(None, both),
        P(both, None),
        P(both),
        P(None, both),
        P(both, None),
        P(both),
        P(None, both),
        P(None, both),
        P(both, None),
    )
    return jax.shard_map(run, mesh=mesh, in_specs=in_specs, out_specs=out_specs, check_vma=False)
```

time: 2260 us -> 829 us (0.37)
  waiting for transfers between devices: 1730 us -> 288 us
  matrix products: 319 us -> 47.9 us
  starting transfers between devices: 1.52 us -> 213 us
  Pallas kernels: 0 us -> 107 us
  blocking collectives: 102 us -> 0 us
  local copies, waits for them, and re-layouts: 51.6 us -> 110 us
    all_gather x12 -> x2, waiting for transfers between devices: 1180 us -> 0.01 us  [the longest x1 0.01 us: per_device_heads(): ffn_full = lax.all_gather(ffn_own, 'seq', axis=0)]
    reduce_scatter x4 -> x1, waiting for transfers between devices: 485 us -> 0.01 us  [per_device_heads(): lax.psum_scatter(ffn_grads(hidden, normed_rows, grad_rows), 'seq', scatte...]
    ppermute x0 -> x67, waiting for transfers between devices: none -> 276 us  [the longest x24 173 us: shift(): lax.ppermute(value, axis, [(i, (i + step) % count) for i in range(count)])]
    dot_general x94 -> x15, matrix products: 319 us -> 47.9 us  [the longest x14 42.8 us: dot(): return jnp.einsum(spec, left, right, preferred_element_type=F32)]
    ppermute x0 -> x67, starting transfers between devices: none -> 205 us  [the longest x24 114 us: shift(): lax.ppermute(value, axis, [(i, (i + step) % count) for i in range(count)])]
    pallas_call x0 -> x4, Pallas kernels: none -> 107 us  [the longest x1 60.1 us: feed_forward(): pl.pallas_call(ffn_kernel, grid=(steps,), in_specs=[pl.BlockSpec((1, trip...]
    unnamed x2 -> x0, blocking collectives: 83.3 us -> none
    unnamed x20 -> x3, waiting for transfers between devices: 63.7 us -> 0.05 us
  transfers between devices with their start and end apart: 18 -> 71, of which waited for: 18 -> 33; matrix products, arithmetic and copies ran while one was open for 11% -> 22% of each run, Pallas kernels for 0% -> 13%
where the time goes in v1:
time: 829 us; the launch traced here: 816 us
  waiting for transfers between devices  288 us (35%)
  starting transfers between devices  213 us (26%)
  local copies, waits for them, and re-layouts  110 us (13%)
  Pallas kernels  107 us (13%)
  matrix products  47.9 us (6%)
  other arithmetic  34.6 us (4%)
  between operations  16 us (2%)
    ppermute x24, waiting for transfers between devices, shift(): lax.ppermute(value, axis, [(i, (i + step) % count) for i in range(count)])  173 us
    ppermute x24, starting transfers between devices, shift(): lax.ppermute(value, axis, [(i, (i + step) % count) for i in range(count)])  114 us
    ppermute x33, waiting for transfers between devices, flip(): return lax.ppermute(value, 'seq', [(i, i ^ bits) for i in range(count)])  63.1 us
    pallas_call x1, Pallas kernels, feed_forward(): pl.pallas_call(ffn_kernel, grid=(steps,), in_specs=[pl.BlockSpec((1, trip...  60.1 us
    ppermute x33, starting transfers between devices, flip(): return lax.ppermute(value, 'seq', [(i, i ^ bits) for i in range(count)])  51.3 us
    dot_general x14, matrix products, dot(): return jnp.einsum(spec, left, right, preferred_element_type=F32)  42.8 us
    dynamic_update_slice x24, local copies, waits for them, and re-layouts, gather_seq(): lax.dynamic_update_slice(whole, jnp.expand_dims(piece, (axis, axis + 1)),...  27.6 us
    ppermute x8, starting transfers between devices, group_rows(): lax.ppermute(rows, both, pairs)  25.8 us
  transfers between devices with their start and end apart: 71, of which 33 were waited for; matrix products, arithmetic and copies ran while one was open for 22% of the time, Pallas kernels for 13%

profile of v1, /device:TPU:2, one launch (start us, length us, event | category | flops | bytes accessed | tf_op | source)
XLA Modules:
  0.0 816.1 jit_solution(1179826043543808958)
XLA Ops:
  47.4 14.0 %collective-permute-done.4 = bf16[4,80,1152]{2,1,0:T(8,128)(2,1)} collective-permute-done((bf16[4,80,1152]{2,1,0:T(8,128)(2,1)S(1)}, bf16[4,80,1152]{2,1,0:T(8,128)(2,1)}, u32[]{:S(2)}, u32[]{:S(2)}) %collective-permute-start.4) | collective-permute-done | bytes 737312 | tf_op jit(solution)/shard_map/ppermute | solution.py:649
  117.6 15.9 %collective-permute-start.15 = (bf16[128,1120]{0,1:T(8,128)(2,1)}, bf16[128,1120]{0,1:T(8,128)(2,1)}, u32[]{:S(2)}, u32[]{:S(2)}) collective-permute-start(bf16[128,1120]{0,1:T(8,128)(2,1)} %constant_dynamic-update-slice_fusion), channel_id=1, source_target_pairs={{0,4},{1,5},{2,6},{3,7},{4,0},{5,1},{6,2},{7,3},{8,12},{9,13},{10,... | collective-permute-start | bytes 860168 | tf_op jit(solution)/shard_map/ppermute | solution.py:649
  153.5 16.8 %collective-permute-done.16 = bf16[128,1120]{0,1:T(8,128)(2,1)} collective-permute-done((bf16[128,1120]{0,1:T(8,128)(2,1)}, bf16[128,1120]{0,1:T(8,128)(2,1)}, u32[]{:S(2)}, u32[]{:S(2)}) %collective-permute-start.16) | collective-permute-done | bytes 286752 | tf_op jit(solution)/shard_map/ppermute | solution.py:649
  202.9 12.7 %attend.1 = (bf16[1024,640]{1,0:T(8,128)(2,1)S(1)}, bf16[1024,640]{1,0:T(8,128)(2,1)S(1)}, f32[1024,640]{1,0:T(8,128)S(1)}) custom-call(f32[1024,640]{1,0:T(8,128)S(1)} %fusion.9.projected_ref, bf16[1024,640]{1,0:T(8,128)(2,1)S(1)} %convolution_convert_fusion.3.pairs_ref, bf16[1024,128]{1,0:T(8,128)(2,1)S(1)} %pad.56.rotary_ref, ...), custom_call_target="tpu_custom_call" | custom-call | flops 2013265920 | bytes 7864320 | tf_op jit(solution)/shard_map/attend/pallas_call | solution.py:448
  226.7 14.8 %collective-permute-done.29 = bf16[128,2560]{1,0:T(8,128)(2,1)S(1)} collective-permute-done((bf16[128,2560]{1,0:T(8,128)(2,1)}, bf16[128,2560]{1,0:T(8,128)(2,1)S(1)}, u32[]{:S(2)}, u32[]{:S(2)}) %collective-permute-start.29) | collective-permute-done | bytes 655392 | tf_op jit(solution)/shard_map/ppermute | solution.py:82
  250.5 18.0 %collective-permute-done.30 = bf16[128,2560]{1,0:T(8,128)(2,1)S(1)} collective-permute-done((bf16[128,2560]{1,0:T(8,128)(2,1)}, bf16[128,2560]{1,0:T(8,128)(2,1)S(1)}, u32[]{:S(2)}, u32[]{:S(2)}) %collective-permute-start.30) | collective-permute-done | bytes 655392 | tf_op jit(solution)/shard_map/ppermute | solution.py:82
  290.7 10.7 %collective-permute-done.32 = bf16[128,2560]{1,0:T(8,128)(2,1)S(1)} collective-permute-done((bf16[128,2560]{1,0:T(8,128)(2,1)}, bf16[128,2560]{1,0:T(8,128)(2,1)S(1)}, u32[]{:S(2)}, u32[]{:S(2)}) %collective-permute-start.32) | collective-permute-done | bytes 655392 | tf_op jit(solution)/shard_map/ppermute | solution.py:82
  302.3 24.4 %collective-permute-done.33 = bf16[128,2560]{1,0:T(8,128)(2,1)S(1)} collective-permute-done((bf16[128,2560]{1,0:T(8,128)(2,1)}, bf16[128,2560]{1,0:T(8,128)(2,1)S(1)}, u32[]{:S(2)}, u32[]{:S(2)}) %collective-permute-start.33) | collective-permute-done | bytes 655392 | tf_op jit(solution)/shard_map/ppermute | solution.py:82
  328.6 60.1 %feed_forward.1 = (bf16[8,600,512]{2,1,0:T(8,128)(2,1)}, bf16[512,2560]{1,0:T(8,128)(2,1)}, bf16[512,2560]{1,0:T(8,128)(2,1)}) custom-call(bf16[8,600,2560]{2,1,0:T(8,128)(2,1)} %bitcast.314, bf16[512,2560]{1,0:T(8,128)(2,1)} %constant_dynamic-update-slice_fusion.9.rows_ref, bf16[512,2560]{1,0:T(8,128)(2,1)} %copy-done.3), custom_call_target="tpu_custom_call" | custom-call | flops 25165824000 | bytes 39976960 | tf_op jit(solution)/shard_map/feed_forward/pallas_call | solution.py:595
  388.7 18.4 %ffn_grads.1 = bf16[8,600,2560]{2,1,0:T(8,128)(2,1)} custom-call(bf16[8,600,512]{2,1,0:T(8,128)(2,1)} %get-tuple-element.51.hidden_ref, bf16[512,2560]{1,0:T(8,128)(2,1)} %constant_dynamic-update-slice_fusion.9.rows_ref, bf16[512,2560]{1,0:T(8,128)(2,1)S(1)} %copy-done.4), custom_call_target="tpu_custom_call" | custom-call | flops 12582912000 | bytes 34734080 | tf_op jit(solution)/shard_map/ffn_grads/pallas_call | solution.py:628
  408.9 15.1 %collective-permute-start.37 = (bf16[128,2560]{1,0:T(8,128)(2,1)S(1)}, bf16[128,2560]{1,0:T(8,128)(2,1)S(1)}, u32[]{:S(2)}, u32[]{:S(2)}) collective-permute-start(bf16[128,2560]{1,0:T(8,128)(2,1)S(1)} %get-tuple-element.83), channel_id=1, source_target_pairs={{0,8},{8,16},{16,24},{24,0},{1,9},{9,17},{17,25},{25,1},{2,10},{10... | collective-permute-start | bytes 1966088 | tf_op jit(solution)/shard_map/ppermute | solution.py:82
  428.1 14.3 %collective-permute-done.37 = bf16[128,2560]{1,0:T(8,128)(2,1)S(1)} collective-permute-done((bf16[128,2560]{1,0:T(8,128)(2,1)S(1)}, bf16[128,2560]{1,0:T(8,128)(2,1)S(1)}, u32[]{:S(2)}, u32[]{:S(2)}) %collective-permute-start.37) | collective-permute-done | bytes 655392 | tf_op jit(solution)/shard_map/ppermute | solution.py:82
  442.4 25.9 %collective-permute-done.36 = bf16[128,2560]{1,0:T(8,128)(2,1)S(1)} collective-permute-done((bf16[128,2560]{1,0:T(8,128)(2,1)S(1)}, bf16[128,2560]{1,0:T(8,128)(2,1)S(1)}, u32[]{:S(2)}, u32[]{:S(2)}) %collective-permute-start.36) | collective-permute-done | bytes 655392 | tf_op jit(solution)/shard_map/ppermute | solution.py:82
  472.5 10.6 %convolution_convert_fusion.2 = bf16[128,2560]{1,0:T(8,128)(2,1)} fusion(bf16[128,2560]{1,0:T(8,128)(2,1)} %multiply_convert_fusion, bf16[2560,2560]{1,0:T(8,128)(2,1)} %all-gather.4.cloned.1.call-done), kind=kOutput, calls=%fused_computation.6 | convolution fusion | flops 1678049280 | bytes 14417920 | tf_op jit(solution)/shard_map/td,kd->tk/dot_general | solution.py:78
  496.5 12.4 %all-to-all-done = bf16[8,128,320]{1,2,0:T(8,128)(2,1)} async-done(((bf16[8,128,320]{1,2,0:T(8,128)(2,1)}), bf16[8,128,320]{1,2,0:T(8,128)(2,1)}, u32[]{:S(2)}, u32[]{:S(2)}) %all-to-all-start) | async-done | bytes 655392 | tf_op jit(solution)/shard_map/all_to_all | solution.py:893
  521.6 15.5 %attend_back.1 = (bf16[1024,640]{1,0:T(8,128)(2,1)S(1)}, bf16[1024,640]{1,0:T(8,128)(2,1)S(1)}, f32[1024,128]{1,0:T(8,128)S(1)}) custom-call(bf16[1024,640]{1,0:T(8,128)(2,1)} %copy-done.8, bf16[1024,640]{1,0:T(8,128)(2,1)} %copy-done, bf16[1024,128]{1,0:T(8,128)(2,1)S(1)} %pad.56.rotary_ref, f32[1024,640]{1,0:T(8,128)} %copy-done.7, ...), custom_call_target="tpu_custom_call" | custom-call | flops 5368709120 | bytes 9175040 | tf_op jit(solution)/shard_map/attend_back/pallas_call | solution.py:516
  541.1 14.8 %collective-permute-start.54 = (bf16[160,1024]{1,0:T(8,128)(2,1)}, bf16[160,1024]{1,0:T(8,128)(2,1)}, u32[]{:S(2)}, u32[]{:S(2)}) collective-permute-start(bf16[160,1024]{1,0:T(8,128)(2,1)} %get-tuple-element.97), channel_id=1, source_target_pairs={{0,8},{8,16},{16,24},{24,0},{1,9},{9,17},{17,25},{25,1},{2,10},{10... | collective-permute-start | bytes 983048 | tf_op jit(solution)/shard_map/ppermute | solution.py:82
  576.5 10.2 %collective-permute-start.55 = (bf16[160,1024]{1,0:T(8,128)(2,1)S(1)}, bf16[160,1024]{1,0:T(8,128)(2,1)S(1)}, u32[]{:S(2)}, u32[]{:S(2)}) collective-permute-start(bf16[160,1024]{1,0:T(8,128)(2,1)S(1)} %fusion.28), channel_id=1, source_target_pairs={{0,0},{1,4},{2,8},{3,12},{4,16},{5,20},{6,24},{7,28},{8,1},{9,5},{... | collective-permute-start | bytes 983048 | tf_op jit(solution)/shard_map/ppermute | solution.py:775
  660.3 12.3 %collective-permute-start.65 = (bf16[80,2560]{1,0:T(8,128)(2,1)S(1)}, bf16[80,2560]{1,0:T(8,128)(2,1)S(1)}, u32[]{:S(2)}, u32[]{:S(2)}) collective-permute-start(bf16[80,2560]{1,0:T(8,128)(2,1)S(1)} %get-tuple-element.91), channel_id=1, source_target_pairs={{0,8},{8,16},{16,24},{24,0},{1,9},{9,17},{17,25},{25,1},{2,10},{10... | collective-permute-start | bytes 1228808 | tf_op jit(solution)/shard_map/ppermute | solution.py:82
  683.4 11.1 %collective-permute-done.64 = bf16[80,2560]{1,0:T(8,128)(2,1)S(1)} collective-permute-done((bf16[80,2560]{1,0:T(8,128)(2,1)S(1)}, bf16[80,2560]{1,0:T(8,128)(2,1)S(1)}, u32[]{:S(2)}, u32[]{:S(2)}) %collective-permute-start.64) | collective-permute-done | bytes 409632 | tf_op jit(solution)/shard_map/ppermute | solution.py:82
  694.6 16.5 %collective-permute-start.40 = (bf16[128,2560]{1,0:T(8,128)(2,1)S(1)}, bf16[128,2560]{1,0:T(8,128)(2,1)S(1)}, u32[]{:S(2)}, u32[]{:S(2)}) collective-permute-start(bf16[128,2560]{1,0:T(8,128)(2,1)S(1)} %copy-done.41), channel_id=1, source_target_pairs={{0,8},{8,16},{16,24},{24,0},{1,9},{9,17},{17,25},{25,1},{2,10},{10... | collective-permute-start | bytes 1966088 | tf_op jit(solution)/shard_map/ppermute | solution.py:82
  730.8 26.8 %collective-permute-done.39 = bf16[128,2560]{1,0:T(8,128)(2,1)S(1)} collective-permute-done((bf16[128,2560]{1,0:T(8,128)(2,1)S(1)}, bf16[128,2560]{1,0:T(8,128)(2,1)S(1)}, u32[]{:S(2)}, u32[]{:S(2)}) %collective-permute-start.39) | collective-permute-done | bytes 655392 | tf_op jit(solution)/shard_map/ppermute | solution.py:82
  757.7 19.4 %collective-permute-start.49 = (bf16[80,1152]{1,0:T(8,128)(2,1)S(1)}, bf16[80,1152]{1,0:T(8,128)(2,1)S(1)}, u32[]{:S(2)}, u32[]{:S(2)}) collective-permute-start(bf16[80,1152]{1,0:T(8,128)(2,1)S(1)} %get-tuple-element.93), channel_id=1, source_target_pairs={{0,24},{8,0},{16,8},{24,16},{1,25},{9,1},{17,9},{25,17},{2,26},{10... | collective-permute-start | bytes 552968 | tf_op jit(solution)/shard_map/ppermute | solution.py:82
  780.7 14.9 %collective-permute-done.66 = bf16[80,2560]{1,0:T(8,128)(2,1)S(1)} collective-permute-done((bf16[80,2560]{1,0:T(8,128)(2,1)S(1)}, bf16[80,2560]{1,0:T(8,128)(2,1)S(1)}, u32[]{:S(2)}, u32[]{:S(2)}) %collective-permute-start.66) | collective-permute-done | bytes 409632 | tf_op jit(solution)/shard_map/ppermute | solution.py:775
  (462 shorter events, 374.5 us)
Async XLA Ops:
  7.2 321.4 %all-gather.6.cloned.1.call-start = ((), (), s32[]{:S(2)}) async-start(), calls=%async_computation.4 | async-start | bytes 27648000 | tf_op jit(solution)/shard_map/all_gather | solution.py:828
  71.8 400.7 %all-gather.4.cloned.1.call-start = ((), (), s32[]{:S(2)}) async-start(), calls=%async_computation.2 | async-start | bytes 14745600 | tf_op jit(solution)/shard_map/all_gather | solution.py:871
  133.5 36.7 %collective-permute-start.16 = (bf16[128,1120]{0,1:T(8,128)(2,1)}, bf16[128,1120]{0,1:T(8,128)(2,1)}, u32[]{:S(2)}, u32[]{:S(2)}) collective-permute-start(bf16[128,1120]{0,1:T(8,128)(2,1)} %constant_dynamic-update-slice_fusion), channel_id=1, source_target_pairs={{0,6},{1,7},{2,4},{3,5},{4,2},{5,3},{6,0},{7,1},{8,14},{9,15},{10,... | collective-permute-start | bytes 860168 | tf_op jit(solution)/shard_map/ppermute | solution.py:649
  133.5 40.7 %collective-permute-start.17 = (bf16[128,1120]{0,1:T(8,128)(2,1)}, bf16[128,1120]{0,1:T(8,128)(2,1)}, u32[]{:S(2)}, u32[]{:S(2)}) collective-permute-start(bf16[128,1120]{0,1:T(8,128)(2,1)} %constant_dynamic-update-slice_fusion), channel_id=1, source_target_pairs={{0,1},{1,0},{2,3},{3,2},{4,5},{5,4},{6,7},{7,6},{8,9},{9,8},{10,11... | collective-permute-start | bytes 860168 | tf_op jit(solution)/shard_map/ppermute | solution.py:649
  134.8 43.4 %collective-permute-start.21 = (bf16[80,2560]{1,0:T(8,128)(2,1)}, bf16[80,2560]{1,0:T(8,128)(2,1)}, u32[]{:S(2)}, u32[]{:S(2)}) collective-permute-start(bf16[80,2560]{1,0:T(8,128)(2,1)} %param.24), channel_id=1, source_target_pairs={{0,0},{4,1},{8,2},{12,3},{16,4},{20,5},{24,6},{28,7},{1,8},{5,9},{... | collective-permute-start | bytes 1228808 | tf_op jit(solution)/shard_map/ppermute | solution.py:766
  138.7 41.3 %collective-permute-start.22 = (bf16[80,2560]{1,0:T(8,128)(2,1)}, bf16[80,2560]{1,0:T(8,128)(2,1)}, u32[]{:S(2)}, u32[]{:S(2)}) collective-permute-start(bf16[80,2560]{1,0:T(8,128)(2,1)} %param.24), channel_id=1, source_target_pairs={{1,0},{5,1},{9,2},{13,3},{17,4},{21,5},{25,6},{29,7},{2,8},{6,9},{... | collective-permute-start | bytes 1228808 | tf_op jit(solution)/shard_map/ppermute | solution.py:766
  221.7 46.8 %collective-permute-start.30 = (bf16[128,2560]{1,0:T(8,128)(2,1)}, bf16[128,2560]{1,0:T(8,128)(2,1)S(1)}, u32[]{:S(2)}, u32[]{:S(2)}) collective-permute-start(bf16[128,2560]{1,0:T(8,128)(2,1)} %fusion.11), channel_id=1, source_target_pairs={{0,16},{8,24},{16,0},{24,8},{1,17},{9,25},{17,1},{25,9},{2,18},{10... | collective-permute-start | bytes 1966088 | tf_op jit(solution)/shard_map/ppermute | solution.py:82
  221.7 46.9 %collective-permute-start.31 = (bf16[128,2560]{1,0:T(8,128)(2,1)}, bf16[128,2560]{1,0:T(8,128)(2,1)S(1)}, u32[]{:S(2)}, u32[]{:S(2)}) collective-permute-start(bf16[128,2560]{1,0:T(8,128)(2,1)} %fusion.11), channel_id=1, source_target_pairs={{0,24},{8,0},{16,8},{24,16},{1,25},{9,1},{17,9},{25,17},{2,26},{10... | collective-permute-start | bytes 1966088 | tf_op jit(solution)/shard_map/ppermute | solution.py:82
  279.9 523.8 %reduce-scatter.2.cloned.1.call-start = ((), (), s32[]{:S(2)}) async-start(), calls=%async_computation.3 | async-start | bytes 27648000 | tf_op jit(solution)/shard_map/reduce_scatter | solution.py:879
  285.9 40.8 %collective-permute-start.33 = (bf16[128,2560]{1,0:T(8,128)(2,1)}, bf16[128,2560]{1,0:T(8,128)(2,1)S(1)}, u32[]{:S(2)}, u32[]{:S(2)}) collective-permute-start(bf16[128,2560]{1,0:T(8,128)(2,1)} %multiply_convert_fusion.1), channel_id=1, source_target_pairs={{0,16},{8,24},{16,0},{24,8},{1,17},{9,25},{17,1},{25,9},{2,18},{10... | collective-permute-start | bytes 1966088 | tf_op jit(solution)/shard_map/ppermute | solution.py:82
  285.9 41.8 %collective-permute-start.34 = (bf16[128,2560]{1,0:T(8,128)(2,1)}, bf16[128,2560]{1,0:T(8,128)(2,1)S(1)}, u32[]{:S(2)}, u32[]{:S(2)}) collective-permute-start(bf16[128,2560]{1,0:T(8,128)(2,1)} %multiply_convert_fusion.1), channel_id=1, source_target_pairs={{0,24},{8,0},{16,8},{24,16},{1,25},{9,1},{17,9},{25,17},{2,26},{10... | collective-permute-start | bytes 1966088 | tf_op jit(solution)/shard_map/ppermute | solution.py:82
  424.0 44.4 %collective-permute-start.36 = (bf16[128,2560]{1,0:T(8,128)(2,1)S(1)}, bf16[128,2560]{1,0:T(8,128)(2,1)S(1)}, u32[]{:S(2)}, u32[]{:S(2)}) collective-permute-start(bf16[128,2560]{1,0:T(8,128)(2,1)S(1)} %get-tuple-element.84), channel_id=1, source_target_pairs={{0,16},{8,24},{16,0},{24,8},{1,17},{9,25},{17,1},{25,9},{2,18},{10... | collective-permute-start | bytes 1966088 | tf_op jit(solution)/shard_map/ppermute | solution.py:82
  427.3 41.1 %collective-permute-start.35 = (bf16[128,2560]{1,0:T(8,128)(2,1)S(1)}, bf16[128,2560]{1,0:T(8,128)(2,1)S(1)}, u32[]{:S(2)}, u32[]{:S(2)}) collective-permute-start(bf16[128,2560]{1,0:T(8,128)(2,1)S(1)} %get-tuple-element.82), channel_id=1, source_target_pairs={{0,24},{8,0},{16,8},{24,16},{1,25},{9,1},{17,9},{25,17},{2,26},{10... | collective-permute-start | bytes 1966088 | tf_op jit(solution)/shard_map/ppermute | solution.py:82
  518.2 58.4 %collective-permute-start.56 = (bf16[128,2560]{1,0:T(8,128)(2,1)}, bf16[128,2560]{1,0:T(8,128)(2,1)}, u32[]{:S(2)}, u32[]{:S(2)}) collective-permute-start(bf16[128,2560]{1,0:T(8,128)(2,1)} %multiply_convert_fusion), channel_id=1, source_target_pairs={{0,2},{1,3},{2,0},{3,1},{4,6},{5,7},{6,4},{7,5},{8,10},{9,11},{10,... | collective-permute-start | bytes 1966088 | tf_op jit(solution)/shard_map/ppermute | solution.py:649
  521.0 67.8 %collective-permute-start.57 = (bf16[128,2560]{1,0:T(8,128)(2,1)}, bf16[128,2560]{1,0:T(8,128)(2,1)}, u32[]{:S(2)}, u32[]{:S(2)}) collective-permute-start(bf16[128,2560]{1,0:T(8,128)(2,1)} %multiply_convert_fusion), channel_id=1, source_target_pairs={{0,4},{1,5},{2,6},{3,7},{4,0},{5,1},{6,2},{7,3},{8,12},{9,13},{10,... | collective-permute-start | bytes 1966088 | tf_op jit(solution)/shard_map/ppermute | solution.py:649
  574.3 51.2 %collective-permute-start.59 = (bf16[128,2560]{1,0:T(8,128)(2,1)S(1)}, bf16[128,2560]{1,0:T(8,128)(2,1)}, u32[]{:S(2)}, u32[]{:S(2)}) collective-permute-start(bf16[128,2560]{1,0:T(8,128)(2,1)S(1)} %copy-done.21), channel_id=1, source_target_pairs={{0,1},{1,0},{2,3},{3,2},{4,5},{5,4},{6,7},{7,6},{8,9},{9,8},{10,11... | collective-permute-start | bytes 1966088 | tf_op jit(solution)/shard_map/ppermute | solution.py:649
  588.7 59.2 %collective-permute-start.60 = (bf16[128,2560]{1,0:T(8,128)(2,1)}, bf16[128,2560]{1,0:T(8,128)(2,1)}, u32[]{:S(2)}, u32[]{:S(2)}) collective-permute-start(bf16[128,2560]{1,0:T(8,128)(2,1)} %collective-permute-done.56), channel_id=1, source_target_pairs={{0,1},{1,0},{2,3},{3,2},{4,5},{5,4},{6,7},{7,6},{8,9},{9,8},{10,11... | collective-permute-start | bytes 1966088 | tf_op jit(solution)/shard_map/ppermute | solution.py:649
  600.7 49.3 %collective-permute-start.61 = (bf16[128,2560]{1,0:T(8,128)(2,1)}, bf16[128,2560]{1,0:T(8,128)(2,1)}, u32[]{:S(2)}, u32[]{:S(2)}) collective-permute-start(bf16[128,2560]{1,0:T(8,128)(2,1)} %collective-permute-done.57), channel_id=1, source_target_pairs={{0,1},{1,0},{2,3},{3,2},{4,5},{5,4},{6,7},{7,6},{8,9},{9,8},{10,11... | collective-permute-start | bytes 1966088 | tf_op jit(solution)/shard_map/ppermute | solution.py:649
  711.0 46.6 %collective-permute-start.39 = (bf16[128,2560]{1,0:T(8,128)(2,1)S(1)}, bf16[128,2560]{1,0:T(8,128)(2,1)S(1)}, u32[]{:S(2)}, u32[]{:S(2)}) collective-permute-start(bf16[128,2560]{1,0:T(8,128)(2,1)S(1)} %copy-done.40), channel_id=1, source_target_pairs={{0,16},{8,24},{16,0},{24,8},{1,17},{9,25},{17,1},{25,9},{2,18},{10... | collective-permute-start | bytes 1966088 | tf_op jit(solution)/shard_map/ppermute | solution.py:82
  714.6 62.4 %collective-permute-start.38 = (bf16[128,2560]{1,0:T(8,128)(2,1)S(1)}, bf16[128,2560]{1,0:T(8,128)(2,1)S(1)}, u32[]{:S(2)}, u32[]{:S(2)}) collective-permute-start(bf16[128,2560]{1,0:T(8,128)(2,1)S(1)} %copy-done.39), channel_id=1, source_target_pairs={{0,24},{8,0},{16,8},{24,16},{1,25},{9,1},{17,9},{25,17},{2,26},{10... | collective-permute-start | bytes 1966088 | tf_op jit(solution)/shard_map/ppermute | solution.py:82
  714.7 80.9 %collective-permute-start.66 = (bf16[80,2560]{1,0:T(8,128)(2,1)S(1)}, bf16[80,2560]{1,0:T(8,128)(2,1)S(1)}, u32[]{:S(2)}, u32[]{:S(2)}) collective-permute-start(bf16[80,2560]{1,0:T(8,128)(2,1)S(1)} %fusion.25), channel_id=1, source_target_pairs={{0,0},{1,4},{2,8},{3,12},{4,16},{5,20},{6,24},{7,28},{8,1},{9,5},{... | collective-permute-start | bytes 1228808 | tf_op jit(solution)/shard_map/ppermute | solution.py:775
  718.6 78.0 %collective-permute-start.51 = (bf16[80,1152]{1,0:T(8,128)(2,1)S(1)}, bf16[80,1152]{1,0:T(8,128)(2,1)S(1)}, u32[]{:S(2)}, u32[]{:S(2)}) collective-permute-start(bf16[80,1152]{1,0:T(8,128)(2,1)S(1)} %get-tuple-element.94), channel_id=1, source_target_pairs={{0,8},{8,16},{16,24},{24,0},{1,9},{9,17},{17,25},{25,1},{2,10},{10... | collective-permute-start | bytes 552968 | tf_op jit(solution)/shard_map/ppermute | solution.py:82
  729.6 70.5 %collective-permute-start.50 = (bf16[80,1152]{1,0:T(8,128)(2,1)S(1)}, bf16[80,1152]{1,0:T(8,128)(2,1)S(1)}, u32[]{:S(2)}, u32[]{:S(2)}) collective-permute-start(bf16[80,1152]{1,0:T(8,128)(2,1)S(1)} %get-tuple-element.95), channel_id=1, source_target_pairs={{0,16},{8,24},{16,0},{24,8},{1,17},{9,25},{17,1},{25,9},{2,18},{10... | collective-permute-start | bytes 552968 | tf_op jit(solution)/shard_map/ppermute | solution.py:82
  757.7 42.4 %collective-permute-start.49 = (bf16[80,1152]{1,0:T(8,128)(2,1)S(1)}, bf16[80,1152]{1,0:T(8,128)(2,1)S(1)}, u32[]{:S(2)}, u32[]{:S(2)}) collective-permute-start(bf16[80,1152]{1,0:T(8,128)(2,1)S(1)} %get-tuple-element.93), channel_id=1, source_target_pairs={{0,24},{8,0},{16,8},{24,16},{1,25},{9,1},{17,9},{25,17},{2,26},{10... | collective-permute-start | bytes 552968 | tf_op jit(solution)/shard_map/ppermute | solution.py:82
  (116 other events, 2874.7 us)
Sparse Core Ops, SparseCore 0:
  71.9 167.4 all-gather.5
  280.0 78.2 all-gather.3
  407.3 216.2 reduce-scatter.1

commit v2 on v1

--- a/solution.py
+++ b/solution.py
@@ -537,145 +537,111 @@
     )(query, pairs, rotary, logs, grad, *tables)
 
 
-def ffn_kernel(
-    weights_ref, rows_ref, grads_ref,
-    hidden_ref, grad_rows_ref, out_rows_ref, grad_sum_ref, out_sum_ref,
-):
-    step = pl.program_id(0)
-    hidden = weights_ref.shape[1] // 3
-
-    def against(rows, start):
+def ffn_kernel(weights_ref, rows_ref, grads_ref, both_ref, act_ref):
+    def against(index, rows):
         return lax.dot_general(
-            rows[...], weights_ref[0, start : start + hidden, :], (((1,), (1,)), ((), ())),
-            preferred_element_type=F32,
+            weights_ref[index], rows[...], (((1,), (1,)), ((), ())), preferred_element_type=F32
         )
 
-    gate_values = against(rows_ref, 0)
-    upward = against(rows_ref, hidden)
-    grad_activated = against(grads_ref, 2 * hidden)
+    gate_values = against(0, rows_ref)
+    upward = against(1, rows_ref)
+    grad_activated = against(2, grads_ref)
     sigmoid_gate = jax.nn.sigmoid(gate_values)
-    activated = gate_values * sigmoid_gate * upward
-    grad_upward = grad_activated * gate_values * sigmoid_gate
-    grad_gate = (
+    swish = gate_values * sigmoid_gate
+    act_ref[...] = (swish * upward).astype(BF16)
+    both_ref[1] = (grad_activated * swish).astype(BF16)
+    both_ref[0] = (
         grad_activated * upward * sigmoid_gate * (1.0 + gate_values * (1.0 - sigmoid_gate))
-    )
-    hidden_ref[0, 0:hidden, :] = grad_gate.T.astype(BF16)
-    hidden_ref[0, hidden : 2 * hidden, :] = grad_upward.T.astype(BF16)
-    hidden_ref[0, 2 * hidden : 3 * hidden, :] = activated.T.astype(BF16)
-
-    def through(values, start):
-        return jnp.dot(
-            values.astype(BF16), weights_ref[0, start : start + hidden, :],
-            preferred_element_type=F32,
-        )
-
-    grad_part = through(grad_gate, 0) + through(grad_upward, hidden)
-    out_part = through(activated, 2 * hidden)
-
-    @pl.when(step == 0)
-    def _():
-        grad_sum_ref[...] = grad_part
-        out_sum_ref[...] = out_part
-
-    @pl.when(step > 0)
-    def _():
-        grad_sum_ref[...] += grad_part
-        out_sum_ref[...] += out_part
-
-    @pl.when(step == pl.num_programs(0) - 1)
-    def _():
-        grad_rows_ref[...] = grad_sum_ref[...].astype(BF16)
-        out_rows_ref[...] = out_sum_ref[...].astype(BF16)
-
-
-def feed_forward(weights, rows, grads):
-    steps, triple, width = weights.shape
+    ).astype(BF16)
+
+
+def ffn_hidden(weights, rows, grads):
+    _, hidden, width = weights.shape
     count = rows.shape[0]
+    block = hidden // 4
     whole = pl.BlockSpec(memory_space=pltpu.VMEM)
+    own = pl.BlockSpec((block, count), lambda i: (i, 0))
     return pl.pallas_call(
         ffn_kernel,
-        grid=(steps,),
-        in_specs=[pl.BlockSpec((1, triple, width), lambda i: (i, 0, 0)), whole, whole],
-        out_specs=[pl.BlockSpec((1, triple, count), lambda i: (i, 0, 0)), whole, whole],
+        grid=(hidden // block,),
+        in_specs=[pl.BlockSpec((3, block, width), lambda i: (0, i, 0)), whole, whole],
+        out_specs=[pl.BlockSpec((2, block, count), lambda i: (0, i, 0)), own],
         out_shape=[
-            jax.ShapeDtypeStruct((steps, triple, count), BF16),
-            jax.ShapeDtypeStruct((count, width), BF16),
-            jax.ShapeDtypeStruct((count, width), BF16),
-        ],
-        scratch_shapes=[pltpu.VMEM((count, width), F32), pltpu.VMEM((count, width), F32)],
-        compiler_params=pltpu.CompilerParams(vmem_limit_bytes=56 * 1024 * 1024),
+            jax.ShapeDtypeStruct((2, hidden, count), BF16),
+            jax.ShapeDtypeStruct((hidden, count), BF16),
+        ],
+        compiler_params=pltpu.CompilerParams(vmem_limit_bytes=48 * 1024 * 1024),
         cost_estimate=pl.CostEstimate(
-            flops=4 * steps * triple * width * count,
-            bytes_accessed=2 * steps * triple * (width + count) + 8 * count * width,
-            transcendentals=steps * triple * count // 3,
+            flops=6 * hidden * width * count,
+            bytes_accessed=6 * hidden * (width + count) + 4 * count * width,
+            transcendentals=hidden * count,
         ),
-        name="feed_forward",
+        name="ffn_hidden",
     )(weights, rows, grads)
 
 
-def ffn_grads_kernel(hidden_ref, rows_ref, grads_ref, out_ref):
-    hidden = hidden_ref.shape[1] // 3
-    for start, source in ((0, rows_ref), (hidden, rows_ref), (2 * hidden, grads_ref)):
-        out_ref[0, start : start + hidden, :] = jnp.dot(
-            hidden_ref[0, start : start + hidden, :], source[...], preferred_element_type=F32
+def ffn_grads_kernel(both_ref, act_ref, rows_ref, grads_ref, earlier_ref, out_ref):
+    hidden = act_ref.shape[1]
+    parts = ((both_ref[0, 0], rows_ref), (both_ref[1, 0], rows_ref), (act_ref[0], grads_ref))
+    for place, (left, right) in enumerate(parts):
+        out_ref[0, place * hidden : (place + 1) * hidden, :] = jnp.dot(
+            left, right[...], preferred_element_type=F32
         ).astype(BF16)
 
 
-def ffn_grads(hidden, rows, grads):
-    steps, triple, count = hidden.shape
+def ffn_grads(grad_both, activated, rows, grads, earlier):
+    steps, hidden, count = activated.shape
     width = rows.shape[1]
     whole = pl.BlockSpec(memory_space=pltpu.VMEM)
+    own = pl.BlockSpec((1, hidden, count), lambda i: (i, 0, 0))
     return pl.pallas_call(
         ffn_grads_kernel,
         grid=(steps,),
-        in_specs=[pl.BlockSpec((1, triple, count), lambda i: (i, 0, 0)), whole, whole],
-        out_specs=pl.BlockSpec((1, triple, width), lambda i: (i, 0, 0)),
-        out_shape=jax.ShapeDtypeStruct((steps, triple, width), BF16),
+        in_specs=[
+            pl.BlockSpec((2, 1, hidden, count), lambda i: (0, i, 0, 0)),
+            own,
+            whole,
+            whole,
+            pl.BlockSpec(memory_space=pl.ANY),
+        ],
+        out_specs=pl.BlockSpec((1, 3 * hidden, width), lambda i: (i, 0, 0)),
+        out_shape=jax.ShapeDtypeStruct((steps, 3 * hidden, width), BF16),
         compiler_params=pltpu.CompilerParams(vmem_limit_bytes=48 * 1024 * 1024),
         cost_estimate=pl.CostEstimate(
-            flops=2 * steps * triple * width * count,
-            bytes_accessed=2 * steps * triple * (width + count) + 4 * count * width,
+            flops=6 * steps * hidden * width * count,
+            bytes_accessed=6 * steps * hidden * (width + count) + 4 * count * width,
             transcendentals=0,
         ),
         name="ffn_grads",
-    )(hidden, rows, grads)
-
-
-def after(value, *others):
-    return lax.optimization_barrier((value,) + others)[0]
-
-
-def flip(value, count, bits):
-    return lax.ppermute(value, "seq", [(i, i ^ bits) for i in range(count)])
-
-
-def gather_seq(value, count, chip, core, axis=0):
-    even = [value] + [flip(value, count, 2 * m) for m in range(1, count // 2)]
-    odd = [flip(piece, count, 1) for piece in even]
-    shape = value.shape[:axis] + (count // 2, 2) + value.shape[axis:]
-    whole = jnp.zeros(shape, value.dtype)
-    for pieces, side in ((even, core), (odd, 1 - core)):
-        for m, piece in enumerate(pieces):
-            start = [0] * len(shape)
-            start[axis] = chip ^ m
-            start[axis + 1] = side
-            whole = lax.dynamic_update_slice(
-                whole, jnp.expand_dims(piece, (axis, axis + 1)), start
-            )
-    return whole
+    )(grad_both, activated, rows, grads, earlier)
+
+
+def done(value):
+    first = value[(0,) * value.ndim].astype(F32)
+    return (first != first).astype(jnp.int32)
+
+
+def hold(value, token):
+    return jnp.where(token == 0, value, jnp.zeros_like(value))
+
+
+def flip(value):
+    count = lax.axis_size("seq")
+    return lax.ppermute(value, "seq", [(i, i ^ 1) for i in range(count)])
+
+
+def exchange(blocks, axis, groups=None):
+    return lax.all_to_all(
+        blocks, axis, split_axis=0, concat_axis=0, axis_index_groups=groups, tiled=True
+    )
+
+
+def repeat(value, count):
+    return jnp.broadcast_to(value[None], (count,) + value.shape)
 
 
 def choose(value, index, axis):
     return lax.dynamic_index_in_dim(value, index, axis, keepdims=False)
-
-
-def scatter_seq(mine, theirs, count, chip, axis=0):
-    half = mine.astype(F32) + flip(theirs.astype(BF16), count, 1).astype(F32)
-    total = choose(half, chip, axis)
-    half_low = half.astype(BF16)
-    for m in range(1, count // 2):
-        total = total + flip(choose(half_low, chip ^ m, axis), count, 2 * m).astype(F32)
-    return total
 
 
 def per_device_heads(
@@ -702,28 +668,63 @@
     own_rows = query_down.shape[0]
     down_width = query_rank + KV_RANK + ROPE
     heads = HEADS // seq_count
-    place = lax.axis_index("dp")
-    spot = lax.axis_index("seq")
-    chip, core = spot // 2, spot % 2
+    core = lax.axis_index("seq") % 2
     chips = seq_count // 2
     both = ("dp", "seq")
     devices = dp_count * seq_count
     length = seq_count * tokens
-
-    def by_core(value):
-        value = value.reshape(chips, 2, tokens, value.shape[1])
-        return choose(value, core, 1), choose(value, 1 - core, 1)
-
-    def gather_dp_ordered(value):
+    place = lax.axis_index("dp")
+    chip = lax.axis_index("seq") // 2
+    same_core = [[2 * j + c for j in range(chips)] for c in range(2)]
+
+    def across(value, steps):
+        return lax.ppermute(value, "seq", [(i, i ^ (2 * steps)) for i in range(seq_count)])
+
+    def place_in(whole, piece, index, axis):
+        return lax.dynamic_update_slice_in_dim(whole, jnp.expand_dims(piece, axis), index, axis)
+
+    def gather_plane(value, token=0, axis=0):
+        shape = value.shape[:axis] + (chips,) + value.shape[axis:]
+        whole = jnp.zeros(shape, value.dtype)
+        for m in range(chips):
+            piece = across(value, m) if m else value
+            index = chip ^ m if m < chips - 1 else (chip ^ m) + token
+            whole = place_in(whole, piece, index, axis)
+        return whole
+
+    def with_other_core(mine, axis=1):
+        shape = mine.shape[:axis] + (2,) + mine.shape[axis:]
+        whole = place_in(jnp.zeros(shape, mine.dtype), mine, core, axis)
+        return place_in(whole, flip(mine), 1 - core, axis)
+
+    def gather_seq(value, token=0, axis=0):
+        return with_other_core(gather_plane(value, token, axis), axis + 1)
+
+    def scatter_seq(mine, theirs, token=0):
+        half = mine.astype(F32) + flip(theirs.astype(BF16)).astype(F32)
+        half = half.astype(BF16)
+        total = choose(half, chip, 0).astype(F32)
+        for m in range(1, chips):
+            total = total + across(choose(half, (chip ^ m) + token, 0), m).astype(F32)
+        return total
+
+    def gather_z(value):
         whole = jnp.zeros((dp_count,) + value.shape, value.dtype)
         for k, piece in enumerate(gather_dp(value, dp_count)):
             whole = lax.dynamic_update_index_in_dim(whole, piece, (place - k) % dp_count, 0)
         return whole
 
-    def scatter_dp_ordered(blocks):
-        return scatter_dp(
-            [choose(blocks, (place - k) % dp_count, 0) for k in range(dp_count)], dp_count
-        )
+    def scatter_z(blocks):
+        blocks = blocks.astype(BF16)
+        total = choose(blocks, place, 0).astype(F32)
+        for k in range(1, dp_count):
+            block = choose(blocks, (place - k) % dp_count, 0)
+            total = total + shift(block, "dp", dp_count, -k).astype(F32)
+        return total
+
+    def by_core(value, token=0):
+        value = value.reshape(chips, 2, tokens, value.shape[1])
+        return choose(value, core, 1), choose(value, 1 - core + token, 1)
 
     padded_width = down_width + 4 + -(down_width + 4) % HEAD_LANES
 
@@ -742,38 +743,11 @@
         ],
         1,
     )
-    down_plane = gather_dp_ordered(down_own)
-    down_full = gather_seq(down_plane, seq_count, chip, core, 1).reshape(width, padded_width)
-    gains = down_full[:, down_width : down_width + 4].T.astype(F32)
-    attn_gain_full = gains[0]
-    ffn_gain_full = gains[1]
-
-    def short_gain(row, own):
-        return row.reshape(devices, own_rows)[:, : own.shape[0]].reshape(-1)
-
-    query_gain_full = short_gain(gains[2], query_gain)
-    latent_gain_full = short_gain(gains[3], latent_gain)
-
-    def group_rows(rows):
-        whole = jnp.zeros((dp_count,) + rows.shape, rows.dtype)
-        for k in range(dp_count):
-            pairs = [
-                (s * dp_count + (z + k) % dp_count, z * seq_count + s)
-                for z in range(dp_count)
-                for s in range(seq_count)
-            ]
-            whole = lax.dynamic_update_index_in_dim(
-                whole, lax.ppermute(rows, both, pairs), (place + k) % dp_count, 0
-            )
-        return whole
-
+    down_plane = gather_z(down_own)
     to_owner = [
         (z * seq_count + s, s * dp_count + z) for z in range(dp_count) for s in range(seq_count)
     ]
-
-    def group_home(blocks):
-        return lax.ppermute(scatter_dp_ordered(blocks).astype(BF16), both, to_owner).astype(F32)
-
+    to_group = [(owner, holder) for holder, owner in to_owner]
     up_rows = max(query_up.shape[1], latent_up.shape[1])
     up_packed = jnp.concatenate(
         [
@@ -782,7 +756,21 @@
         ],
         1,
     )
-    up_group = group_rows(after(up_packed, down_plane))
+    up_moved = lax.ppermute(up_packed, both, to_group)
+    up_group = gather_z(hold(up_moved, done(down_plane)))
+    proj_moved = lax.ppermute(output_proj, both, to_group)
+    proj_group = gather_z(hold(proj_moved, done(up_group))).reshape(-1, width)
+    down_full = gather_seq(down_plane, done(up_group), 1).reshape(width, padded_width)
+    gains = down_full[:, down_width : down_width + 4].T.astype(F32)
+    attn_gain_full = gains[0]
+    ffn_gain_full = gains[1]
+
+    def short_gain(row, own):
+        return row.reshape(devices, own_rows)[:, : own.shape[0]].reshape(-1)
+
+    query_gain_full = short_gain(gains[2], query_gain)
+    latent_gain_full = short_gain(gains[3], latent_gain)
+
     query_up_padded = jnp.pad(
         up_group[:, : query_up.shape[1], :query_rank].reshape(heads, NOPE + ROPE, query_rank),
         ((0, 0), (0, HEAD_LANES - NOPE - ROPE), (0, 0)),
@@ -792,7 +780,6 @@
     inputs = layer_input.astype(F32)
     normal_one, inverse_one = norm_parts(inputs)
     normed = (normal_one * attn_gain_full).astype(BF16)
-    normed = after(normed, query_up_padded, latent_up_group)
     down_out = jnp.dot(normed, down_full, preferred_element_type=F32)
     normal_query, inverse_query = norm_parts(down_out[:, :query_rank])
     query_normed = (normal_query * query_gain_full).astype(BF16)
@@ -814,18 +801,17 @@
         + two_parts(sin_table[:, :half]),
         1,
     )
-    token_all = gather_seq(token_message, seq_count, chip, core).reshape(
+    token_all = gather_seq(token_message, done(proj_group)).reshape(
         length, token_message.shape[1]
     )
-    proj_group = group_rows(after(output_proj, down_full)).reshape(-1, width)
     grad_out = cotangent.astype(F32)
     grad_two = (RESIDUAL_SCALE * grad_out).astype(BF16)
-    grad_rows = jnp.concatenate(gather_dp(after(grad_two, proj_group), dp_count))
+    grad_rows = gather_z(hold(grad_two, done(proj_group))).reshape(-1, width)
     proj_padded = jnp.pad(
         proj_group.reshape(heads, VDIM, width), ((0, 0), (HEAD_LANES - VDIM, 0), (0, 0))
     ).reshape(heads * HEAD_LANES, width)
-    ffn_own = after(jnp.concatenate([ffn_gate.T, ffn_up.T, ffn_down], 0), down_full)
-    ffn_full = lax.all_gather(ffn_own, "seq", axis=0)
+    ffn_own = hold(jnp.stack([ffn_gate.T, ffn_up.T, ffn_down]), done(down_full))
+    ffn_full = lax.all_gather(ffn_own, "seq", axis=1, tiled=True)
 
     query_normed_all = token_all[:, :query_rank]
     latent_all = token_all[:, query_rank : query_rank + KV_RANK]
@@ -855,34 +841,41 @@
     pairs = dot("tc,kc->tk", latent_all, latent_up_group).astype(BF16)
     query, attended, logs = attend(projected, pairs, rotary_lanes, tables)
 
-    attended_mine, attended_theirs = by_core(attended)
+    attended_mine, attended_theirs = by_core(attended, done(grad_rows))
     branch = scatter_seq(
         dot("mtk,kd->mtd", attended_mine, proj_padded),
         dot("mtk,kd->mtd", attended_theirs, proj_padded),
-        seq_count,
-        chip,
     )
     middle = inputs + RESIDUAL_SCALE * branch
     normal_two, inverse_two = norm_parts(middle)
     normed_two = (normal_two * ffn_gain_full).astype(BF16)
-    normed_two = after(normed_two, grad_rows)
-
-    normed_rows = jnp.concatenate(gather_dp(normed_two, dp_count))
-    proj_full = lax.all_gather(after(proj_group, normed_two), "seq", axis=0, tiled=True)
-    hidden, grad_part, out_part = feed_forward(ffn_full, normed_rows, grad_rows)
-    grad_parts = jnp.split(grad_part, dp_count)
+
+    normed_rows = gather_z(normed_two).reshape(-1, width)
+    proj_full = lax.all_gather(hold(proj_group, done(normed_two)), "seq", axis=0, tiled=True)
+    own_hidden = ffn_down.shape[0]
+    count = dp_count * tokens
+    grad_both, activated = ffn_hidden(ffn_full, normed_rows, grad_rows)
+    grad_part = dot("gft,gfd->td", grad_both, ffn_full[:2])
+    grad_parts = grad_part.astype(BF16).reshape(dp_count, tokens, width)
     returned = [
-        shift(grad_parts[k], "dp", dp_count, -k).astype(F32) for k in range(1, dp_count)
+        shift(choose(grad_parts, (place - k) % dp_count, 0), "dp", dp_count, -k)
+        for k in range(1, dp_count)
     ]
-    grad_normed_two = sum(returned, grad_parts[0].astype(F32))
-    hidden = after(hidden, returned[0])
+    grad_normed_two = choose(grad_parts, place, 0).astype(F32)
+    for piece in returned:
+        grad_normed_two = grad_normed_two + piece.astype(F32)
     ffn_sums = lax.psum_scatter(
-        ffn_grads(hidden, normed_rows, grad_rows), "seq", scatter_dimension=0
+        ffn_grads(
+            grad_both.reshape(2, seq_count, own_hidden, count),
+            activated.reshape(seq_count, own_hidden, count),
+            normed_rows,
+            grad_rows,
+            returned[0],
+        ),
+        "seq",
+        scatter_dimension=0,
     ).astype(F32)
-    out_part = after(out_part, grad_normed_two)
-    layer_output = (
-        middle + RESIDUAL_SCALE * scatter_dp(jnp.split(out_part, dp_count), dp_count)
-    ).astype(BF16)
+    out_part = dot("ft,fd->td", activated, ffn_full[2]).astype(BF16)
 
     grad_middle_norm, grad_ffn_gain_part = norm_back(
         grad_normed_two, normal_two, inverse_two, ffn_gain_full
@@ -890,12 +883,8 @@
     grad_middle = grad_out + grad_middle_norm
     grad_branch = (RESIDUAL_SCALE * grad_middle).astype(BF16)
     grad_attended = dot("td,kd->tk", grad_branch, proj_full).astype(BF16)
-    grad_attended = lax.all_to_all(
-        grad_attended.reshape(tokens, seq_count, heads * VDIM).transpose(1, 0, 2),
-        "seq",
-        split_axis=0,
-        concat_axis=0,
-        tiled=True,
+    grad_attended = exchange(
+        grad_attended.reshape(tokens, seq_count, heads * VDIM).transpose(1, 0, 2), "seq"
     ).reshape(length, heads, VDIM)
     grad_attended = jnp.pad(
         grad_attended, ((0, 0), (0, 0), (HEAD_LANES - VDIM, 0))
@@ -917,7 +906,11 @@
                 2,
             )
         )
-    grad_own = scatter_seq(token_grads[0], token_grads[1], seq_count, chip)
+    branch_plane = gather_plane(grad_branch)
+    grad_own = scatter_seq(token_grads[0], token_grads[1], done(branch_plane))
+    out_parts = hold(out_part.reshape(dp_count, tokens, width), done(grad_attended))
+    out_sum = jnp.sum(exchange(out_parts, "dp").astype(F32), 0)
+    layer_output = (middle + RESIDUAL_SCALE * out_sum).astype(BF16)
 
     query_up_grads = dot("tk,tq->kq", grad_projected, query_normed_all).astype(BF16)
     query_up_grads = query_up_grads.reshape(heads, HEAD_LANES, query_rank)[:, : NOPE + ROPE]
@@ -935,14 +928,17 @@
         ],
         2,
     )
-    sum_up = group_home(up_grads)
-    sum_query_up = sum_up[: query_up.shape[1], :query_rank].T
-    sum_latent_up = sum_up[: latent_up.shape[1], query_rank:].T
-
-    branch_all = gather_seq(after(grad_branch, grad_attended), seq_count, chip, core)
+    branch_all = with_other_core(branch_plane)
     proj_grads = dot("tk,td->kd", attended, branch_all.reshape(length, width)).astype(BF16)
     proj_grads = proj_grads.reshape(heads, HEAD_LANES, width)[:, HEAD_LANES - VDIM :]
-    sum_out = group_home(proj_grads.reshape(dp_count, -1, width))
+    group_grads = jnp.concatenate(
+        [up_grads, proj_grads.reshape(dp_count, -1, up_grads.shape[2])], 1
+    )
+    group_sums = jnp.sum(exchange(hold(group_grads, done(grad_own)), "dp").astype(F32), 0)
+    group_sums = lax.ppermute(group_sums.astype(BF16), both, to_owner).astype(F32)
+    sum_query_up = group_sums[: query_up.shape[1], :query_rank].T
+    sum_latent_up = group_sums[: latent_up.shape[1], query_rank:].T
+    sum_out = group_sums[up_rows:].reshape(-1, width)
 
     grad_query_latent, grad_query_gain_part = norm_back(
         grad_own[:, :query_rank], normal_query, inverse_query, query_gain_full
@@ -985,13 +981,11 @@
         gain_columns, ((0, 0), (down_width, padded_width - down_width - 4))
     )
     down_sums = down_sums.astype(BF16).reshape(dp_count, chips, 2, own_rows, padded_width)
-    sum_down = scatter_dp_ordered(
-        scatter_seq(
-            choose(down_sums, core, 2), choose(down_sums, 1 - core, 2), seq_count, chip, 1
-        )
+    down_sums = down_sums.transpose(1, 2, 0, 3, 4)
+    sum_down = scatter_z(
+        scatter_seq(choose(down_sums, core, 1), choose(down_sums, 1 - core, 1))
     )
     sum_gains = sum_down[:, down_width : down_width + 4].T
-    own_hidden = ffn_down.shape[0]
     return (
         layer_output,
         input_grad,

time: 829 us -> 799 us (0.964)
  the two profiles are of different devices: /device:TPU:2 before, /device:TPU:1 now
where the time goes in v2:
time: 799 us; the launch traced here: 792 us
  waiting for transfers between devices  330 us (41%)
  starting transfers between devices  159 us (20%)
  local copies, waits for them, and re-layouts  103 us (13%)
  matrix products  71.3 us (9%)
  Pallas kernels  65.7 us (8%)
  other arithmetic  34.7 us (4%)
  between operations  27.6 us (3%)
    ppermute x21, waiting for transfers between devices, shift(): lax.ppermute(value, axis, [(i, (i + step) % count) for i in range(count)])  140 us
    ppermute x21, starting transfers between devices, shift(): lax.ppermute(value, axis, [(i, (i + step) % count) for i in range(count)])  102 us
    ppermute x18, waiting for transfers between devices, across(): lax.ppermute(value, 'seq', [(i, i ^ 2 * steps) for i in range(seq_count)])  92.9 us
    dot_general x16, matrix products, dot(): return jnp.einsum(spec, left, right, preferred_element_type=F32)  67.6 us
    ppermute x1, waiting for transfers between devices, per_device_heads(): lax.ppermute(group_sums.astype(BF16), both, to_owner).astype(F32)  44 us
    all_to_all x3, waiting for transfers between devices, exchange(): lax.all_to_all(blocks, axis, split_axis=0, concat_axis=0, axis_index_grou...  39.9 us
    dynamic_update_slice x17, local copies, waits for them, and re-layouts, place_in(): lax.dynamic_update_slice_in_dim(whole, jnp.expand_dims(piece, axis), inde...  23.1 us
    pallas_call x1, Pallas kernels, ffn_hidden(): pl.pallas_call(ffn_kernel, grid=(hidden // block,), in_specs=[pl.BlockSpe...  19.2 us
  transfers between devices with their start and end apart: 54, of which 27 were waited for; matrix products, arithmetic and copies ran while one was open for 23% of the time, Pallas kernels for 8%

profile of v2, /device:TPU:1, one launch (start us, length us, event | category | flops | bytes accessed | tf_op | source)
XLA Modules:
  0.0 792.2 jit_solution(7177883625788487771)
XLA Ops:
  52.9 15.9 %collective-permute-done.8 = bf16[160,1024]{1,0:T(8,128)(2,1)S(1)} collective-permute-done((bf16[160,1024]{1,0:T(8,128)(2,1)S(1)}, bf16[160,1024]{1,0:T(8,128)(2,1)S(1)}, u32[]{:S(2)}, u32[]{:S(2)}) %collective-permute-start.8) | collective-permute-done | bytes 327712 | tf_op jit(solution)/shard_map/ppermute | solution.py:82
  105.9 12.0 %collective-permute-start.15 = (bf16[80,2560]{1,0:T(8,128)(2,1)S(1)}, bf16[80,2560]{1,0:T(8,128)(2,1)S(1)}, u32[]{:S(2)}, u32[]{:S(2)}) collective-permute-start(bf16[80,2560]{1,0:T(8,128)(2,1)S(1)} %get-tuple-element.56), channel_id=1, source_target_pairs={{0,8},{8,16},{16,24},{24,0},{1,9},{9,17},{17,25},{25,1},{2,10},{10... | collective-permute-start | bytes 1228808 | tf_op jit(solution)/shard_map/ppermute | solution.py:82
  120.3 11.9 %collective-permute-start.16 = (bf16[80,2560]{1,0:T(8,128)(2,1)S(1)}, bf16[80,2560]{1,0:T(8,128)(2,1)S(1)}, u32[]{:S(2)}, u32[]{:S(2)}) collective-permute-start(bf16[80,2560]{1,0:T(8,128)(2,1)S(1)} %get-tuple-element.56), channel_id=1, source_target_pairs={{0,16},{8,24},{16,0},{24,8},{1,17},{9,25},{17,1},{25,9},{2,18},{10... | collective-permute-start | bytes 1228808 | tf_op jit(solution)/shard_map/ppermute | solution.py:82
  135.8 15.0 %collective-permute-done.16 = bf16[80,2560]{1,0:T(8,128)(2,1)S(1)} collective-permute-done((bf16[80,2560]{1,0:T(8,128)(2,1)S(1)}, bf16[80,2560]{1,0:T(8,128)(2,1)S(1)}, u32[]{:S(2)}, u32[]{:S(2)}) %collective-permute-start.16) | collective-permute-done | bytes 409632 | tf_op jit(solution)/shard_map/ppermute | solution.py:82
  155.5 13.7 %collective-permute-start.19 = (bf16[128,2560]{1,0:T(8,128)(2,1)}, bf16[128,2560]{1,0:T(8,128)(2,1)}, u32[]{:S(2)}, u32[]{:S(2)}) collective-permute-start(bf16[128,2560]{1,0:T(8,128)(2,1)} %get-tuple-element.52), channel_id=1, source_target_pairs={{0,8},{8,16},{16,24},{24,0},{1,9},{9,17},{17,25},{25,1},{2,10},{10... | collective-permute-start | bytes 1966088 | tf_op jit(solution)/shard_map/ppermute | solution.py:82
  236.8 12.7 %attend.1 = (bf16[1024,640]{1,0:T(8,128)(2,1)S(1)}, bf16[1024,640]{1,0:T(8,128)(2,1)S(1)}, f32[1024,640]{1,0:T(8,128)S(1)}) custom-call(f32[1024,640]{1,0:T(8,128)S(1)} %fusion.23.projected_ref, bf16[1024,640]{1,0:T(8,128)(2,1)S(1)} %convolution_convert_fusion.3.pairs_ref, bf16[1024,128]{1,0:T(8,128)(2,1)S(1)} %pad.56.rotary_ref, ...), custom_call_target="tpu_custom_call" | custom-call | flops 2013265920 | bytes 7864320 | tf_op jit(solution)/shard_map/attend/pallas_call | solution.py:448
  266.6 14.2 %collective-permute-done.25 = bf16[128,2560]{1,0:T(8,128)(2,1)S(1)} collective-permute-done((bf16[128,2560]{1,0:T(8,128)(2,1)S(1)}, bf16[128,2560]{1,0:T(8,128)(2,1)S(1)}, u32[]{:S(2)}, u32[]{:S(2)}) %collective-permute-start.25) | collective-permute-done | bytes 655392 | tf_op jit(solution)/shard_map/ppermute | solution.py:681
  280.7 14.7 %collective-permute-done.24 = bf16[128,2560]{1,0:T(8,128)(2,1)S(1)} collective-permute-done((bf16[128,2560]{1,0:T(8,128)(2,1)S(1)}, bf16[128,2560]{1,0:T(8,128)(2,1)S(1)}, u32[]{:S(2)}, u32[]{:S(2)}) %collective-permute-start.24) | collective-permute-done | bytes 655392 | tf_op jit(solution)/shard_map/ppermute | solution.py:681
  300.5 11.4 %collective-permute-start.26 = (bf16[128,2560]{1,0:T(8,128)(2,1)S(1)}, bf16[128,2560]{1,0:T(8,128)(2,1)S(1)}, u32[]{:S(2)}, u32[]{:S(2)}) collective-permute-start(bf16[128,2560]{1,0:T(8,128)(2,1)S(1)} %get-tuple-element.48), channel_id=1, source_target_pairs={{0,8},{8,16},{16,24},{24,0},{1,9},{9,17},{17,25},{25,1},{2,10},{10... | collective-permute-start | bytes 1966088 | tf_op jit(solution)/shard_map/ppermute | solution.py:82
  326.3 29.1 %collective-permute-done.27 = bf16[128,2560]{1,0:T(8,128)(2,1)S(1)} collective-permute-done((bf16[128,2560]{1,0:T(8,128)(2,1)S(1)}, bf16[128,2560]{1,0:T(8,128)(2,1)S(1)}, u32[]{:S(2)}, u32[]{:S(2)}) %collective-permute-start.27) | collective-permute-done | bytes 655392 | tf_op jit(solution)/shard_map/ppermute | solution.py:82
  355.5 19.2 %ffn_hidden.1 = (bf16[2,1600,512]{2,1,0:T(8,128)(2,1)}, bf16[1600,512]{1,0:T(8,128)(2,1)S(1)}) custom-call(bf16[3,1600,2560]{2,1,0:T(8,128)(2,1)} %all-gather.3.cloned.1.call-done.weights_ref, bf16[512,2560]{1,0:T(8,128)(2,1)S(1)} %bitcast.280, bf16[512,2560]{1,0:T(8,128)(2,1)} %bitcast.310), custom_call_target="tpu_custom_call" | custom-call | flops 12582912000 | bytes 34734080 | tf_op jit(solution)/shard_map/ffn_hidden/pallas_call | solution.py:564
  374.7 14.2 %bitcast_convert_fusion = bf16[512,2560]{1,0:T(8,128)(2,1)S(1)} fusion(bf16[2,1600,512]{2,1,0:T(8,128)(2,1)} %get-tuple-element.23, bf16[3,1600,2560]{2,1,0:T(8,128)(2,1)} %all-gather.3.cloned.1.call-done.weights_ref), kind=kOutput, calls=%fused_computation.13 | convolution fusion | flops 8389918720 | bytes 22282240 | tf_op jit(solution)/shard_map/gft,gfd->td/dot_general | solution.py:78
  391.0 16.5 %collective-permute-start.29 = (bf16[128,2560]{1,0:T(8,128)(2,1)S(1)}, bf16[128,2560]{1,0:T(8,128)(2,1)S(1)}, u32[]{:S(2)}, u32[]{:S(2)}) collective-permute-start(bf16[128,2560]{1,0:T(8,128)(2,1)S(1)} %get-tuple-element.67), channel_id=1, source_target_pairs={{0,24},{8,0},{16,8},{24,16},{1,25},{9,1},{17,9},{25,17},{2,26},{10... | collective-permute-start | bytes 1966088 | tf_op jit(solution)/shard_map/ppermute | solution.py:82
  407.5 12.2 %collective-permute-done.29.earlier_ref = bf16[128,2560]{1,0:T(8,128)(2,1)S(1)} collective-permute-done((bf16[128,2560]{1,0:T(8,128)(2,1)S(1)}, bf16[128,2560]{1,0:T(8,128)(2,1)S(1)}, u32[]{:S(2)}, u32[]{:S(2)}) %collective-permute-start.29) | collective-permute-done | bytes 655392 | tf_op jit(solution)/shard_map/ppermute | solution.py:82
  419.7 18.3 %ffn_grads.1 = bf16[8,600,2560]{2,1,0:T(8,128)(2,1)} custom-call(bf16[2,8,200,512]{3,2,1,0:T(8,128)(2,1)} %bitcast.330, bf16[8,200,512]{2,1,0:T(8,128)(2,1)S(1)} %bitcast.285, bf16[512,2560]{1,0:T(8,128)(2,1)S(1)} %bitcast.281, bf16[512,2560]{1,0:T(8,128)(2,1)} %bitcast.311, bf16[128,2560]{1,0:T(8,128)(2,1)S(1)} %collective-permute-done.29.earlier_ref), custom_call_target="tpu_custom_call" | custom-call | flops 12582912000 | bytes 34734080 | tf_op jit(solution)/shard_map/ffn_grads/pallas_call | solution.py:597
  442.4 12.3 %collective-permute-done.31 = bf16[128,2560]{1,0:T(8,128)(2,1)S(1)} collective-permute-done((bf16[128,2560]{1,0:T(8,128)(2,1)}, bf16[128,2560]{1,0:T(8,128)(2,1)S(1)}, u32[]{:S(2)}, u32[]{:S(2)}) %collective-permute-start.31) | collective-permute-done | bytes 655392 | tf_op jit(solution)/shard_map/ppermute | solution.py:82
  454.7 30.9 %collective-permute-done.30 = bf16[128,2560]{1,0:T(8,128)(2,1)S(1)} collective-permute-done((bf16[128,2560]{1,0:T(8,128)(2,1)}, bf16[128,2560]{1,0:T(8,128)(2,1)S(1)}, u32[]{:S(2)}, u32[]{:S(2)}) %collective-permute-start.30) | collective-permute-done | bytes 655392 | tf_op jit(solution)/shard_map/ppermute | solution.py:82
  509.7 11.5 %all-to-all-done = bf16[8,128,320]{1,2,0:T(8,128)(2,1)S(1)} async-done(((bf16[8,128,320]{1,2,0:T(8,128)(2,1)}), bf16[8,128,320]{1,2,0:T(8,128)(2,1)S(1)}, u32[]{:S(2)}, u32[]{:S(2)}) %all-to-all-start) | async-done | bytes 655392 | tf_op jit(solution)/shard_map/all_to_all | solution.py:634
  524.8 15.5 %attend_back.1 = (bf16[1024,640]{1,0:T(8,128)(2,1)S(1)}, bf16[1024,640]{1,0:T(8,128)(2,1)S(1)}, f32[1024,128]{1,0:T(8,128)S(1)}) custom-call(bf16[1024,640]{1,0:T(8,128)(2,1)} %copy-done.14, bf16[1024,640]{1,0:T(8,128)(2,1)} %copy-done, bf16[1024,128]{1,0:T(8,128)(2,1)S(1)} %pad.56.rotary_ref, f32[1024,640]{1,0:T(8,128)} %copy-done.13, ...), custom_call_target="tpu_custom_call" | custom-call | flops 5368709120 | bytes 9175040 | tf_op jit(solution)/shard_map/attend_back/pallas_call | solution.py:516
  596.7 11.7 %collective-permute-done.37 = bf16[128,1056]{1,0:T(8,128)(2,1)S(1)} collective-permute-done((bf16[128,1056]{1,0:T(8,128)(2,1)S(1)}, bf16[128,1056]{1,0:T(8,128)(2,1)S(1)}, u32[]{:S(2)}, u32[]{:S(2)}) %collective-permute-start.37) | collective-permute-done | bytes 270368 | tf_op jit(solution)/shard_map/ppermute | solution.py:681
  656.7 14.0 %collective-permute-done.42 = bf16[4,80,1152]{2,1,0:T(8,128)(2,1)S(1)} collective-permute-done((bf16[4,80,1152]{2,1,0:T(8,128)(2,1)S(1)}, bf16[4,80,1152]{2,1,0:T(8,128)(2,1)S(1)}, u32[]{:S(2)}, u32[]{:S(2)}) %collective-permute-start.42) | collective-permute-done | bytes 737312 | tf_op jit(solution)/shard_map/ppermute | solution.py:681
  670.7 16.3 %collective-permute-done.41 = bf16[4,80,1152]{2,1,0:T(8,128)(2,1)S(1)} collective-permute-done((bf16[4,80,1152]{2,1,0:T(8,128)(2,1)S(1)}, bf16[4,80,1152]{2,1,0:T(8,128)(2,1)S(1)}, u32[]{:S(2)}, u32[]{:S(2)}) %collective-permute-start.41) | collective-permute-done | bytes 737312 | tf_op jit(solution)/shard_map/ppermute | solution.py:681
  694.2 28.4 %all-to-all-done.2 = bf16[4,360,1024]{2,1,0:T(8,128)(2,1)} async-done(((bf16[4,360,1024]{2,1,0:T(8,128)(2,1)}), bf16[4,360,1024]{2,1,0:T(8,128)(2,1)}, u32[]{:S(2)}, u32[]{:S(2)}) %all-to-all-start.2) | async-done | bytes 2949152 | tf_op jit(solution)/shard_map/all_to_all | solution.py:634
  733.1 44.0 %collective-permute-done.47 = bf16[360,1024]{1,0:T(8,128)(2,1)S(1)} collective-permute-done((bf16[360,1024]{1,0:T(8,128)(2,1)S(1)}, bf16[360,1024]{1,0:T(8,128)(2,1)S(1)}, u32[]{:S(2)}, u32[]{:S(2)}) %collective-permute-start.47) | collective-permute-done | bytes 737312 | tf_op jit(solution)/shard_map/ppermute | solution.py:938
  (432 shorter events, 349.1 us)
Async XLA Ops:
  7.2 348.3 %all-gather.3.cloned.1.call-start = ((), (), s32[]{:S(2)}) async-start(), calls=%async_computation.4 | async-start | bytes 27648000 | tf_op jit(solution)/shard_map/all_gather | solution.py:814
  30.7 41.0 %collective-permute-start.3 = (bf16[4,80,1152]{2,1,0:T(8,128)(2,1)}, bf16[4,80,1152]{2,1,0:T(8,128)(2,1)}, u32[]{:S(2)}, u32[]{:S(2)}) collective-permute-start(bf16[4,80,1152]{2,1,0:T(8,128)(2,1)} %bitcast_dynamic-update-slice_fusion.28), channel_id=1, source_target_pairs={{0,2},{1,3},{2,0},{3,1},{4,6},{5,7},{6,4},{7,5},{8,10},{9,11},{10,... | collective-permute-start | bytes 2211848 | tf_op jit(solution)/shard_map/ppermute | solution.py:681
  31.2 41.8 %collective-permute-start.4 = (bf16[4,80,1152]{2,1,0:T(8,128)(2,1)}, bf16[4,80,1152]{2,1,0:T(8,128)(2,1)}, u32[]{:S(2)}, u32[]{:S(2)}) collective-permute-start(bf16[4,80,1152]{2,1,0:T(8,128)(2,1)} %bitcast_dynamic-update-slice_fusion.28), channel_id=1, source_target_pairs={{0,4},{1,5},{2,6},{3,7},{4,0},{5,1},{6,2},{7,3},{8,12},{9,13},{10,... | collective-permute-start | bytes 2211848 | tf_op jit(solution)/shard_map/ppermute | solution.py:681
  33.6 40.6 %collective-permute-start.5 = (bf16[4,80,1152]{2,1,0:T(8,128)(2,1)}, bf16[4,80,1152]{2,1,0:T(8,128)(2,1)}, u32[]{:S(2)}, u32[]{:S(2)}) collective-permute-start(bf16[4,80,1152]{2,1,0:T(8,128)(2,1)} %bitcast_dynamic-update-slice_fusion.28), channel_id=1, source_target_pairs={{0,6},{1,7},{2,4},{3,5},{4,2},{5,3},{6,0},{7,1},{8,14},{9,15},{10,... | collective-permute-start | bytes 2211848 | tf_op jit(solution)/shard_map/ppermute | solution.py:681
  95.4 396.2 %all-gather.5.cloned.1.call-start = ((), (), s32[]{:S(2)}) async-start(), calls=%async_computation.5 | async-start | bytes 14745600 | tf_op jit(solution)/shard_map/all_gather | solution.py:854
  169.1 46.0 %collective-permute-start.20 = (bf16[128,2560]{1,0:T(8,128)(2,1)}, bf16[128,2560]{1,0:T(8,128)(2,1)}, u32[]{:S(2)}, u32[]{:S(2)}) collective-permute-start(bf16[128,2560]{1,0:T(8,128)(2,1)} %get-tuple-element.52), channel_id=1, source_target_pairs={{0,16},{8,24},{16,0},{24,8},{1,17},{9,25},{17,1},{25,9},{2,18},{10... | collective-permute-start | bytes 1966088 | tf_op jit(solution)/shard_map/ppermute | solution.py:82
  172.0 45.1 %collective-permute-start.21 = (bf16[128,2560]{1,0:T(8,128)(2,1)}, bf16[128,2560]{1,0:T(8,128)(2,1)S(1)}, u32[]{:S(2)}, u32[]{:S(2)}) collective-permute-start(bf16[128,2560]{1,0:T(8,128)(2,1)} %get-tuple-element.52), channel_id=1, source_target_pairs={{0,24},{8,0},{16,8},{24,16},{1,25},{9,1},{17,9},{25,17},{2,26},{10... | collective-permute-start | bytes 1966088 | tf_op jit(solution)/shard_map/ppermute | solution.py:82
  300.4 479.5 %reduce-scatter.2.cloned.1.call-start = ((), (), s32[]{:S(2)}) async-start(), calls=%async_computation.6 | async-start | bytes 27648000 | tf_op jit(solution)/shard_map/reduce_scatter | solution.py:867
  311.9 43.4 %collective-permute-start.27 = (bf16[128,2560]{1,0:T(8,128)(2,1)S(1)}, bf16[128,2560]{1,0:T(8,128)(2,1)S(1)}, u32[]{:S(2)}, u32[]{:S(2)}) collective-permute-start(bf16[128,2560]{1,0:T(8,128)(2,1)S(1)} %get-tuple-element.48), channel_id=1, source_target_pairs={{0,16},{8,24},{16,0},{24,8},{1,17},{9,25},{17,1},{25,9},{2,18},{10... | collective-permute-start | bytes 1966088 | tf_op jit(solution)/shard_map/ppermute | solution.py:82
  313.8 41.5 %collective-permute-start.28 = (bf16[128,2560]{1,0:T(8,128)(2,1)S(1)}, bf16[128,2560]{1,0:T(8,128)(2,1)S(1)}, u32[]{:S(2)}, u32[]{:S(2)}) collective-permute-start(bf16[128,2560]{1,0:T(8,128)(2,1)S(1)} %get-tuple-element.48), channel_id=1, source_target_pairs={{0,24},{8,0},{16,8},{24,16},{1,25},{9,1},{17,9},{25,17},{2,26},{10... | collective-permute-start | bytes 1966088 | tf_op jit(solution)/shard_map/ppermute | solution.py:82
  438.4 47.2 %collective-permute-start.30 = (bf16[128,2560]{1,0:T(8,128)(2,1)}, bf16[128,2560]{1,0:T(8,128)(2,1)S(1)}, u32[]{:S(2)}, u32[]{:S(2)}) collective-permute-start(bf16[128,2560]{1,0:T(8,128)(2,1)} %get-tuple-element.69), channel_id=1, source_target_pairs={{0,16},{8,24},{16,0},{24,8},{1,17},{9,25},{17,1},{25,9},{2,18},{10... | collective-permute-start | bytes 1966088 | tf_op jit(solution)/shard_map/ppermute | solution.py:82
  506.4 68.0 %collective-permute-start.33 = (bf16[128,2560]{1,0:T(8,128)(2,1)}, bf16[128,2560]{1,0:T(8,128)(2,1)}, u32[]{:S(2)}, u32[]{:S(2)}) collective-permute-start(bf16[128,2560]{1,0:T(8,128)(2,1)} %get-tuple-element.45), channel_id=1, source_target_pairs={{0,2},{1,3},{2,0},{3,1},{4,6},{5,7},{6,4},{7,5},{8,10},{9,11},{10,... | collective-permute-start | bytes 1966088 | tf_op jit(solution)/shard_map/ppermute | solution.py:681
  507.8 68.6 %collective-permute-start.34 = (bf16[128,2560]{1,0:T(8,128)(2,1)}, bf16[128,2560]{1,0:T(8,128)(2,1)}, u32[]{:S(2)}, u32[]{:S(2)}) collective-permute-start(bf16[128,2560]{1,0:T(8,128)(2,1)} %get-tuple-element.45), channel_id=1, source_target_pairs={{0,4},{1,5},{2,6},{3,7},{4,0},{5,1},{6,2},{7,3},{8,12},{9,13},{10,... | collective-permute-start | bytes 1966088 | tf_op jit(solution)/shard_map/ppermute | solution.py:681
  509.0 71.3 %collective-permute-start.35 = (bf16[128,2560]{1,0:T(8,128)(2,1)}, bf16[128,2560]{1,0:T(8,128)(2,1)}, u32[]{:S(2)}, u32[]{:S(2)}) collective-permute-start(bf16[128,2560]{1,0:T(8,128)(2,1)} %get-tuple-element.45), channel_id=1, source_target_pairs={{0,6},{1,7},{2,4},{3,5},{4,2},{5,3},{6,0},{7,1},{8,14},{9,15},{10,... | collective-permute-start | bytes 1966088 | tf_op jit(solution)/shard_map/ppermute | solution.py:681
  546.3 38.5 %collective-permute-start.32 = (bf16[4,128,1056]{1,2,0:T(8,128)(2,1)}, bf16[4,128,1056]{1,2,0:T(8,128)(2,1)}, u32[]{:S(2)}, u32[]{:S(2)}) collective-permute-start(bf16[4,128,1056]{1,2,0:T(8,128)(2,1)} %copy.148), channel_id=1, source_target_pairs={{0,1},{1,0},{2,3},{3,2},{4,5},{5,4},{6,7},{7,6},{8,9},{9,8},{10,11... | collective-permute-start | bytes 3244040 | tf_op jit(solution)/shard_map/ppermute | solution.py:630
  565.3 77.8 %all-to-all-start.1 = ((bf16[4,128,2560]{2,1,0:T(8,128)(2,1)}), bf16[4,128,2560]{2,1,0:T(8,128)(2,1)}, u32[]{:S(2)}, u32[]{:S(2)}) async-start(bf16[4,128,2560]{2,1,0:T(8,128)(2,1)} %bitcast.308), calls=%async_computation.1 | async-start | bytes 5242880 | tf_op jit(solution)/shard_map/all_to_all | solution.py:634
  592.4 38.4 %collective-permute-start.46 = (bf16[4,128,2560]{2,1,0:T(8,128)(2,1)}, bf16[4,128,2560]{2,1,0:T(8,128)(2,1)}, u32[]{:S(2)}, u32[]{:S(2)}) collective-permute-start(bf16[4,128,2560]{2,1,0:T(8,128)(2,1)} %bitcast_dynamic-update-slice_fusion.8), channel_id=1, source_target_pairs={{0,1},{1,0},{2,3},{3,2},{4,5},{5,4},{6,7},{7,6},{8,9},{9,8},{10,11... | collective-permute-start | bytes 7864328 | tf_op jit(solution)/shard_map/ppermute | solution.py:630
  643.1 79.4 %all-to-all-start.2 = ((bf16[4,360,1024]{2,1,0:T(8,128)(2,1)}), bf16[4,360,1024]{2,1,0:T(8,128)(2,1)}, u32[]{:S(2)}, u32[]{:S(2)}) async-start(bf16[4,360,1024]{2,1,0:T(8,128)(2,1)} %fusion.14), calls=%async_computation.2 | async-start | bytes 5898240 | tf_op jit(solution)/shard_map/all_to_all | solution.py:634
  653.0 34.0 %collective-permute-start.41 = (bf16[4,80,1152]{2,1,0:T(8,128)(2,1)S(1)}, bf16[4,80,1152]{2,1,0:T(8,128)(2,1)S(1)}, u32[]{:S(2)}, u32[]{:S(2)}) collective-permute-start(bf16[4,80,1152]{2,1,0:T(8,128)(2,1)S(1)} %get-tuple-element.66), channel_id=1, source_target_pairs={{0,4},{1,5},{2,6},{3,7},{4,0},{5,1},{6,2},{7,3},{8,12},{9,13},{10,... | collective-permute-start | bytes 2211848 | tf_op jit(solution)/shard_map/ppermute | solution.py:681
  653.0 34.0 %collective-permute-start.40 = (bf16[4,80,1152]{2,1,0:T(8,128)(2,1)S(1)}, bf16[4,80,1152]{2,1,0:T(8,128)(2,1)S(1)}, u32[]{:S(2)}, u32[]{:S(2)}) collective-permute-start(bf16[4,80,1152]{2,1,0:T(8,128)(2,1)S(1)} %get-tuple-element.64), channel_id=1, source_target_pairs={{0,2},{1,3},{2,0},{3,1},{4,6},{5,7},{6,4},{7,5},{8,10},{9,11},{10,... | collective-permute-start | bytes 2211848 | tf_op jit(solution)/shard_map/ppermute | solution.py:681
  687.4 42.0 %collective-permute-start.45 = (bf16[80,1152]{1,0:T(8,128)(2,1)S(1)}, bf16[80,1152]{1,0:T(8,128)(2,1)S(1)}, u32[]{:S(2)}, u32[]{:S(2)}) collective-permute-start(bf16[80,1152]{1,0:T(8,128)(2,1)S(1)} %get-tuple-element.79), channel_id=1, source_target_pairs={{0,8},{8,16},{16,24},{24,0},{1,9},{9,17},{17,25},{25,1},{2,10},{10... | collective-permute-start | bytes 552968 | tf_op jit(solution)/shard_map/ppermute | solution.py:82
  688.9 40.6 %collective-permute-start.44 = (bf16[80,1152]{1,0:T(8,128)(2,1)S(1)}, bf16[80,1152]{1,0:T(8,128)(2,1)S(1)}, u32[]{:S(2)}, u32[]{:S(2)}) collective-permute-start(bf16[80,1152]{1,0:T(8,128)(2,1)S(1)} %get-tuple-element.80), channel_id=1, source_target_pairs={{0,16},{8,24},{16,0},{24,8},{1,17},{9,25},{17,1},{25,9},{2,18},{10... | collective-permute-start | bytes 552968 | tf_op jit(solution)/shard_map/ppermute | solution.py:82
  690.9 38.6 %collective-permute-start.43 = (bf16[80,1152]{1,0:T(8,128)(2,1)S(1)}, bf16[80,1152]{1,0:T(8,128)(2,1)S(1)}, u32[]{:S(2)}, u32[]{:S(2)}) collective-permute-start(bf16[80,1152]{1,0:T(8,128)(2,1)S(1)} %get-tuple-element.78), channel_id=1, source_target_pairs={{0,24},{8,0},{16,8},{24,16},{1,25},{9,1},{17,9},{25,17},{2,26},{10... | collective-permute-start | bytes 552968 | tf_op jit(solution)/shard_map/ppermute | solution.py:82
  725.0 52.0 %collective-permute-start.47 = (bf16[360,1024]{1,0:T(8,128)(2,1)S(1)}, bf16[360,1024]{1,0:T(8,128)(2,1)S(1)}, u32[]{:S(2)}, u32[]{:S(2)}) collective-permute-start(bf16[360,1024]{1,0:T(8,128)(2,1)S(1)} %reduce_sum.142), channel_id=1, source_target_pairs={{0,0},{1,4},{2,8},{3,12},{4,16},{5,20},{6,24},{7,28},{8,1},{9,5},{... | collective-permute-start | bytes 2211848 | tf_op jit(solution)/shard_map/ppermute | solution.py:938
  (103 other events, 1423.3 us)
Sparse Core Ops, SparseCore 0:
  95.4 144.0 all-gather.2
  300.5 84.3 all-gather.4
  438.2 200.3 reduce-scatter.1

commit v3 on v2

--- a/solution.py
+++ b/solution.py
@@ -467,7 +467,7 @@
 
 def attend_back_kernel(
     query_ref, pairs_ref, rotary_ref, log_ref, grad_ref, cos_ref, left_ref, right_ref,
-    grad_query_ref, grad_pairs_ref, grad_rotary_ref, keys_ref, grad_keys_ref, grad_values_ref,
+    earlier_ref, grad_query_ref, grad_pairs_ref, grad_rotary_ref, keys_ref, grad_keys_ref, grad_values_ref,
 ):
     length = query_ref.shape[0]
     block = min(QUERY_BLOCK, length)
@@ -509,14 +509,15 @@
     grad_rotary_ref[...] += grad_keys
 
 
-def attend_back(query, pairs, rotary, logs, grad, tables):
+def attend_back(query, pairs, rotary, logs, grad, tables, earlier):
     length, lanes = query.shape
     own = pl.BlockSpec((length, HEAD_LANES), lambda h: (0, h))
     shared = pl.BlockSpec((length, HEAD_LANES), lambda h: (0, 0))
     return pl.pallas_call(
         attend_back_kernel,
         grid=(lanes // HEAD_LANES,),
-        in_specs=[own, own, shared, own, own, shared, shared, shared],
+        in_specs=[own, own, shared, own, own, shared, shared, shared]
+        + [pl.BlockSpec(memory_space=pl.ANY)],
         out_specs=[own, own, shared],
         out_shape=[
             jax.ShapeDtypeStruct((length, lanes), BF16),
@@ -534,7 +535,7 @@
             transcendentals=length * length * lanes // HEAD_LANES,
         ),
         name="attend_back",
-    )(query, pairs, rotary, logs, grad, *tables)
+    )(query, pairs, rotary, logs, grad, *tables, earlier)
 
 
 def ffn_kernel(weights_ref, rows_ref, grads_ref, both_ref, act_ref):
@@ -744,8 +745,11 @@
         1,
     )
     down_plane = gather_z(down_own)
+    group_of = [s if s % 2 == 0 else (s + 2) % seq_count for s in range(seq_count)]
     to_owner = [
-        (z * seq_count + s, s * dp_count + z) for z in range(dp_count) for s in range(seq_count)
+        (z * seq_count + s, group_of[s] * dp_count + z)
+        for z in range(dp_count)
+        for s in range(seq_count)
     ]
     to_group = [(owner, holder) for holder, owner in to_owner]
     up_rows = max(query_up.shape[1], latent_up.shape[1])
@@ -758,8 +762,6 @@
     )
     up_moved = lax.ppermute(up_packed, both, to_group)
     up_group = gather_z(hold(up_moved, done(down_plane)))
-    proj_moved = lax.ppermute(output_proj, both, to_group)
-    proj_group = gather_z(hold(proj_moved, done(up_group))).reshape(-1, width)
     down_full = gather_seq(down_plane, done(up_group), 1).reshape(width, padded_width)
     gains = down_full[:, down_width : down_width + 4].T.astype(F32)
     attn_gain_full = gains[0]
@@ -801,6 +803,8 @@
         + two_parts(sin_table[:, :half]),
         1,
     )
+    proj_moved = lax.ppermute(output_proj, both, to_group)
+    proj_group = gather_z(hold(proj_moved, done(token_message))).reshape(-1, width)
     token_all = gather_seq(token_message, done(proj_group)).reshape(
         length, token_message.shape[1]
     )
@@ -841,14 +845,14 @@
     pairs = dot("tc,kc->tk", latent_all, latent_up_group).astype(BF16)
     query, attended, logs = attend(projected, pairs, rotary_lanes, tables)
 
-    attended_mine, attended_theirs = by_core(attended, done(grad_rows))
+    attended_mine, attended_theirs = by_core(attended)
     branch = scatter_seq(
         dot("mtk,kd->mtd", attended_mine, proj_padded),
         dot("mtk,kd->mtd", attended_theirs, proj_padded),
     )
     middle = inputs + RESIDUAL_SCALE * branch
     normal_two, inverse_two = norm_parts(middle)
-    normed_two = (normal_two * ffn_gain_full).astype(BF16)
+    normed_two = hold((normal_two * ffn_gain_full).astype(BF16), done(grad_rows))
 
     normed_rows = gather_z(normed_two).reshape(-1, width)
     proj_full = lax.all_gather(hold(proj_group, done(normed_two)), "seq", axis=0, tiled=True)
@@ -864,25 +868,25 @@
     grad_normed_two = choose(grad_parts, place, 0).astype(F32)
     for piece in returned:
         grad_normed_two = grad_normed_two + piece.astype(F32)
+    out_part = dot("ft,fd->td", activated, ffn_full[2]).astype(BF16)
+
+    grad_middle_norm, grad_ffn_gain_part = norm_back(
+        grad_normed_two, normal_two, inverse_two, ffn_gain_full
+    )
+    grad_middle = grad_out + grad_middle_norm
+    grad_branch = (RESIDUAL_SCALE * grad_middle).astype(BF16)
+    grad_attended = dot("td,kd->tk", grad_branch, proj_full).astype(BF16)
     ffn_sums = lax.psum_scatter(
         ffn_grads(
             grad_both.reshape(2, seq_count, own_hidden, count),
             activated.reshape(seq_count, own_hidden, count),
             normed_rows,
             grad_rows,
-            returned[0],
+            grad_attended,
         ),
         "seq",
         scatter_dimension=0,
     ).astype(F32)
-    out_part = dot("ft,fd->td", activated, ffn_full[2]).astype(BF16)
-
-    grad_middle_norm, grad_ffn_gain_part = norm_back(
-        grad_normed_two, normal_two, inverse_two, ffn_gain_full
-    )
-    grad_middle = grad_out + grad_middle_norm
-    grad_branch = (RESIDUAL_SCALE * grad_middle).astype(BF16)
-    grad_attended = dot("td,kd->tk", grad_branch, proj_full).astype(BF16)
     grad_attended = exchange(
         grad_attended.reshape(tokens, seq_count, heads * VDIM).transpose(1, 0, 2), "seq"
     ).reshape(length, heads, VDIM)
@@ -890,7 +894,7 @@
         grad_attended, ((0, 0), (0, 0), (HEAD_LANES - VDIM, 0))
     ).reshape(length, heads * HEAD_LANES)
     grad_projected, grad_pairs, grad_rotary = attend_back(
-        query, pairs, rotary_lanes, logs, grad_attended, tables
+        query, pairs, rotary_lanes, logs, grad_attended, tables, out_part
     )
     token_grads = []
     for projected_part, pairs_part, rotary_part in zip(
@@ -912,10 +916,11 @@
     out_sum = jnp.sum(exchange(out_parts, "dp").astype(F32), 0)
     layer_output = (middle + RESIDUAL_SCALE * out_sum).astype(BF16)
 
-    query_up_grads = dot("tk,tq->kq", grad_projected, query_normed_all).astype(BF16)
+    home = done(grad_own)
+    query_up_grads = dot("tk,tq->kq", hold(grad_projected, home), query_normed_all).astype(BF16)
     query_up_grads = query_up_grads.reshape(heads, HEAD_LANES, query_rank)[:, : NOPE + ROPE]
     query_up_grads = query_up_grads.reshape(dp_count, -1, query_rank)
-    latent_up_grads = dot("tk,tc->kc", grad_pairs, latent_all).astype(BF16)
+    latent_up_grads = dot("tk,tc->kc", hold(grad_pairs, home), latent_all).astype(BF16)
     latent_up_grads = latent_up_grads.reshape(dp_count, -1, KV_RANK)
     up_grads = jnp.concatenate(
         [
@@ -934,7 +939,7 @@
     group_grads = jnp.concatenate(
         [up_grads, proj_grads.reshape(dp_count, -1, up_grads.shape[2])], 1
     )
-    group_sums = jnp.sum(exchange(hold(group_grads, done(grad_own)), "dp").astype(F32), 0)
+    group_sums = jnp.sum(exchange(group_grads, "dp").astype(F32), 0)
     group_sums = lax.ppermute(group_sums.astype(BF16), both, to_owner).astype(F32)
     sum_query_up = group_sums[: query_up.shape[1], :query_rank].T
     sum_latent_up = group_sums[: latent_up.shape[1], query_rank:].T

time: 799 us -> 789 us (0.987)
  the two profiles are of different devices: /device:TPU:1 before, /device:TPU:2 now
where the time goes in v3:
time: 789 us; the launch traced here: 780 us
  waiting for transfers between devices  318 us (40%)
  starting transfers between devices  137 us (17%)
  local copies, waits for them, and re-layouts  114 us (14%)
  matrix products  76.3 us (10%)
  Pallas kernels  65.8 us (8%)
  other arithmetic  39.6 us (5%)
  between operations  29.8 us (4%)
    ppermute x21, waiting for transfers between devices, shift(): lax.ppermute(value, axis, [(i, (i + step) % count) for i in range(count)])  158 us
    ppermute x18, waiting for transfers between devices, across(): lax.ppermute(value, 'seq', [(i, i ^ 2 * steps) for i in range(seq_count)])  92.4 us
    ppermute x21, starting transfers between devices, shift(): lax.ppermute(value, axis, [(i, (i + step) % count) for i in range(count)])  77.3 us
    dot_general x16, matrix products, dot(): return jnp.einsum(spec, left, right, preferred_element_type=F32)  71.9 us
    all_to_all x3, waiting for transfers between devices, exchange(): lax.all_to_all(blocks, axis, split_axis=0, concat_axis=0, axis_index_grou...  31.7 us
    ppermute x1, waiting for transfers between devices, per_device_heads(): lax.ppermute(group_sums.astype(BF16), both, to_owner).astype(F32)  31 us
    all_to_all x3, starting transfers between devices, exchange(): lax.all_to_all(blocks, axis, split_axis=0, concat_axis=0, axis_index_grou...  27.5 us
    dynamic_update_slice x17, local copies, waits for them, and re-layouts, place_in(): lax.dynamic_update_slice_in_dim(whole, jnp.expand_dims(piece, axis), inde...  23.1 us
  transfers between devices with their start and end apart: 54, of which 25 were waited for; matrix products, arithmetic and copies ran while one was open for 25% of the time, Pallas kernels for 6%

profile of v3, /device:TPU:2, one launch (start us, length us, event | category | flops | bytes accessed | tf_op | source)
XLA Modules:
  0.0 779.8 jit_solution(1870488155274903639)
XLA Ops:
  57.3 14.5 %collective-permute-done.8 = bf16[160,1024]{1,0:T(8,128)(2,1)S(1)} collective-permute-done((bf16[160,1024]{1,0:T(8,128)(2,1)S(1)}, bf16[160,1024]{1,0:T(8,128)(2,1)S(1)}, u32[]{:S(2)}, u32[]{:S(2)}) %collective-permute-start.8) | collective-permute-done | bytes 327712 | tf_op jit(solution)/shard_map/ppermute | solution.py:82
  131.6 12.0 %collective-permute-done.13 = bf16[128,1120]{1,0:T(8,128)(2,1)S(1)} collective-permute-done((bf16[128,1120]{1,0:T(8,128)(2,1)S(1)}, bf16[128,1120]{1,0:T(8,128)(2,1)S(1)}, u32[]{:S(2)}, u32[]{:S(2)}) %collective-permute-start.13) | collective-permute-done | bytes 286752 | tf_op jit(solution)/shard_map/ppermute | solution.py:682
  180.2 12.7 %attend.1 = (bf16[1024,640]{1,0:T(8,128)(2,1)S(1)}, bf16[1024,640]{1,0:T(8,128)(2,1)S(1)}, f32[1024,640]{1,0:T(8,128)S(1)}) custom-call(f32[1024,640]{1,0:T(8,128)S(1)} %fusion.21.projected_ref, bf16[1024,640]{1,0:T(8,128)(2,1)S(1)} %convolution_convert_fusion.3.pairs_ref, bf16[1024,128]{1,0:T(8,128)(2,1)S(1)} %pad.56.rotary_ref, ...), custom_call_target="tpu_custom_call" | custom-call | flops 2013265920 | bytes 7864320 | tf_op jit(solution)/shard_map/attend/pallas_call | solution.py:448
  210.9 12.9 %collective-permute-done.23 = bf16[128,2560]{1,0:T(8,128)(2,1)S(1)} collective-permute-done((bf16[128,2560]{1,0:T(8,128)(2,1)S(1)}, bf16[128,2560]{1,0:T(8,128)(2,1)S(1)}, u32[]{:S(2)}, u32[]{:S(2)}) %collective-permute-start.23) | collective-permute-done | bytes 655392 | tf_op jit(solution)/shard_map/ppermute | solution.py:82
  224.7 27.0 %collective-permute-done.24 = bf16[128,2560]{1,0:T(8,128)(2,1)S(1)} collective-permute-done((bf16[128,2560]{1,0:T(8,128)(2,1)S(1)}, bf16[128,2560]{1,0:T(8,128)(2,1)S(1)}, u32[]{:S(2)}, u32[]{:S(2)}) %collective-permute-start.24) | collective-permute-done | bytes 655392 | tf_op jit(solution)/shard_map/ppermute | solution.py:82
  264.6 11.7 %collective-permute-done.22 = bf16[128,2560]{1,0:T(8,128)(2,1)S(1)} collective-permute-done((bf16[128,2560]{1,0:T(8,128)(2,1)S(1)}, bf16[128,2560]{1,0:T(8,128)(2,1)S(1)}, u32[]{:S(2)}, u32[]{:S(2)}) %collective-permute-start.22) | collective-permute-done | bytes 655392 | tf_op jit(solution)/shard_map/ppermute | solution.py:682
  276.3 13.0 %collective-permute-done.21 = bf16[128,2560]{1,0:T(8,128)(2,1)S(1)} collective-permute-done((bf16[128,2560]{1,0:T(8,128)(2,1)S(1)}, bf16[128,2560]{1,0:T(8,128)(2,1)S(1)}, u32[]{:S(2)}, u32[]{:S(2)}) %collective-permute-start.21) | collective-permute-done | bytes 655392 | tf_op jit(solution)/shard_map/ppermute | solution.py:682
  295.5 11.9 %collective-permute-start.26 = (bf16[128,2560]{1,0:T(8,128)(2,1)S(1)}, bf16[128,2560]{1,0:T(8,128)(2,1)S(1)}, u32[]{:S(2)}, u32[]{:S(2)}) collective-permute-start(bf16[128,2560]{1,0:T(8,128)(2,1)S(1)} %get-tuple-element.48), channel_id=1, source_target_pairs={{0,8},{8,16},{16,24},{24,0},{1,9},{9,17},{17,25},{25,1},{2,10},{10... | collective-permute-start | bytes 1966088 | tf_op jit(solution)/shard_map/ppermute | solution.py:82
  310.8 15.2 %collective-permute-done.26 = bf16[128,2560]{1,0:T(8,128)(2,1)S(1)} collective-permute-done((bf16[128,2560]{1,0:T(8,128)(2,1)S(1)}, bf16[128,2560]{1,0:T(8,128)(2,1)S(1)}, u32[]{:S(2)}, u32[]{:S(2)}) %collective-permute-start.26) | collective-permute-done | bytes 655392 | tf_op jit(solution)/shard_map/ppermute | solution.py:82
  326.1 26.4 %collective-permute-done.27 = bf16[128,2560]{1,0:T(8,128)(2,1)S(1)} collective-permute-done((bf16[128,2560]{1,0:T(8,128)(2,1)S(1)}, bf16[128,2560]{1,0:T(8,128)(2,1)S(1)}, u32[]{:S(2)}, u32[]{:S(2)}) %collective-permute-start.27) | collective-permute-done | bytes 655392 | tf_op jit(solution)/shard_map/ppermute | solution.py:82
  352.6 18.8 %ffn_hidden.1 = (bf16[2,1600,512]{2,1,0:T(8,128)(2,1)}, bf16[1600,512]{1,0:T(8,128)(2,1)S(1)}) custom-call(bf16[3,1600,2560]{2,1,0:T(8,128)(2,1)} %all-gather.3.cloned.1.call-done.weights_ref, bf16[512,2560]{1,0:T(8,128)(2,1)S(1)} %bitcast.279, bf16[512,2560]{1,0:T(8,128)(2,1)} %bitcast.309), custom_call_target="tpu_custom_call" | custom-call | flops 12582912000 | bytes 34734080 | tf_op jit(solution)/shard_map/ffn_hidden/pallas_call | solution.py:565
  371.4 14.2 %bitcast_convert_fusion = bf16[512,2560]{1,0:T(8,128)(2,1)S(1)} fusion(bf16[2,1600,512]{2,1,0:T(8,128)(2,1)} %get-tuple-element.23, bf16[3,1600,2560]{2,1,0:T(8,128)(2,1)} %all-gather.3.cloned.1.call-done.weights_ref), kind=kOutput, calls=%fused_computation.13 | convolution fusion | flops 8389918720 | bytes 22282240 | tf_op jit(solution)/shard_map/gft,gfd->td/dot_general | solution.py:78
  387.8 14.3 %collective-permute-start.31 = (bf16[128,2560]{1,0:T(8,128)(2,1)}, bf16[128,2560]{1,0:T(8,128)(2,1)S(1)}, u32[]{:S(2)}, u32[]{:S(2)}) collective-permute-start(bf16[128,2560]{1,0:T(8,128)(2,1)} %get-tuple-element.68), channel_id=1, source_target_pairs={{0,8},{8,16},{16,24},{24,0},{1,9},{9,17},{17,25},{25,1},{2,10},{10... | collective-permute-start | bytes 1966088 | tf_op jit(solution)/shard_map/ppermute | solution.py:82
  404.6 12.9 %collective-permute-done.31 = bf16[128,2560]{1,0:T(8,128)(2,1)S(1)} collective-permute-done((bf16[128,2560]{1,0:T(8,128)(2,1)}, bf16[128,2560]{1,0:T(8,128)(2,1)S(1)}, u32[]{:S(2)}, u32[]{:S(2)}) %collective-permute-start.31) | collective-permute-done | bytes 655392 | tf_op jit(solution)/shard_map/ppermute | solution.py:82
  417.5 25.7 %collective-permute-done.30 = bf16[128,2560]{1,0:T(8,128)(2,1)} collective-permute-done((bf16[128,2560]{1,0:T(8,128)(2,1)}, bf16[128,2560]{1,0:T(8,128)(2,1)}, u32[]{:S(2)}, u32[]{:S(2)}) %collective-permute-start.30) | collective-permute-done | bytes 655392 | tf_op jit(solution)/shard_map/ppermute | solution.py:82
  461.7 18.5 %ffn_grads.1 = bf16[8,600,2560]{2,1,0:T(8,128)(2,1)} custom-call(bf16[2,8,200,512]{3,2,1,0:T(8,128)(2,1)} %bitcast.330, bf16[8,200,512]{2,1,0:T(8,128)(2,1)S(1)} %bitcast.284, bf16[512,2560]{1,0:T(8,128)(2,1)S(1)} %bitcast.280, bf16[512,2560]{1,0:T(8,128)(2,1)} %bitcast.310, bf16[128,2560]{1,0:T(8,128)(2,1)S(1)} %convolution_convert_fusion.2.earlier_ref), custom_call_target="tpu_custom_call" | custom-call | flops 12582912000 | bytes 34734080 | tf_op jit(solution)/shard_map/ffn_grads/pallas_call | solution.py:598
  502.5 12.3 %broadcast_select_fusion = (bf16[512,2560]{1,0:T(8,128)(2,1)}, bf16[512,2560]{1,0:T(8,128)(2,1)}) fusion(pred[]{:T(512)} %bitcast.83, bf16[1600,512]{1,0:T(8,128)(2,1)S(1)} %copy-done.9, bf16[3,1600,2560]{2,1,0:T(8,128)(2,1)} %all-gather.3.cloned.1.call-done.weights_ref), kind=kOutput, calls=%fused_computation.28 | convolution fusion | flops 4196925440 | bytes 15073792 | tf_op jit(solution)/shard_map/ft,fd->td/dot_general | solution.py:78
  514.8 15.8 %attend_back.1 = (bf16[1024,640]{1,0:T(8,128)(2,1)S(1)}, bf16[1024,640]{1,0:T(8,128)(2,1)S(1)}, f32[1024,128]{1,0:T(8,128)S(1)}) custom-call(bf16[1024,640]{1,0:T(8,128)(2,1)} %copy-done.13, bf16[1024,640]{1,0:T(8,128)(2,1)} %copy-done, bf16[1024,128]{1,0:T(8,128)(2,1)S(1)} %pad.56.rotary_ref, f32[1024,640]{1,0:T(8,128)} %copy-done.12, ...), custom_call_target="tpu_custom_call" | custom-call | flops 5368709120 | bytes 9175040 | tf_op jit(solution)/shard_map/attend_back/pallas_call | solution.py:516
  536.4 18.4 %all-to-all-start.1 = ((bf16[4,128,2560]{2,1,0:T(8,128)(2,1)}), bf16[4,128,2560]{2,1,0:T(8,128)(2,1)}, u32[]{:S(2)}, u32[]{:S(2)}) async-start(bf16[4,128,2560]{2,1,0:T(8,128)(2,1)} %bitcast.307), calls=%async_computation.1 | async-start | bytes 5242880 | tf_op jit(solution)/shard_map/all_to_all | solution.py:635
  577.1 11.0 %collective-permute-done.38 = bf16[128,1056]{1,0:T(8,128)(2,1)S(1)} collective-permute-done((bf16[128,1056]{1,0:T(8,128)(2,1)S(1)}, bf16[128,1056]{1,0:T(8,128)(2,1)S(1)}, u32[]{:S(2)}, u32[]{:S(2)}) %collective-permute-start.38) | collective-permute-done | bytes 270368 | tf_op jit(solution)/shard_map/ppermute | solution.py:682
  659.3 16.8 %collective-permute-done.42 = bf16[4,80,1152]{2,1,0:T(8,128)(2,1)S(1)} collective-permute-done((bf16[4,80,1152]{2,1,0:T(8,128)(2,1)S(1)}, bf16[4,80,1152]{2,1,0:T(8,128)(2,1)S(1)}, u32[]{:S(2)}, u32[]{:S(2)}) %collective-permute-start.42) | collective-permute-done | bytes 737312 | tf_op jit(solution)/shard_map/ppermute | solution.py:682
  676.1 15.4 %collective-permute-done.41 = bf16[4,80,1152]{2,1,0:T(8,128)(2,1)S(1)} collective-permute-done((bf16[4,80,1152]{2,1,0:T(8,128)(2,1)S(1)}, bf16[4,80,1152]{2,1,0:T(8,128)(2,1)S(1)}, u32[]{:S(2)}, u32[]{:S(2)}) %collective-permute-start.41) | collective-permute-done | bytes 737312 | tf_op jit(solution)/shard_map/ppermute | solution.py:682
  699.4 26.0 %all-to-all-done.2 = bf16[4,360,1024]{2,1,0:T(8,128)(2,1)} async-done(((bf16[4,360,1024]{2,1,0:T(8,128)(2,1)}), bf16[4,360,1024]{2,1,0:T(8,128)(2,1)}, u32[]{:S(2)}, u32[]{:S(2)}) %all-to-all-start.2) | async-done | bytes 2949152 | tf_op jit(solution)/shard_map/all_to_all | solution.py:635
  733.5 31.0 %collective-permute-done.47 = bf16[360,1024]{1,0:T(8,128)(2,1)S(1)} collective-permute-done((bf16[360,1024]{1,0:T(8,128)(2,1)S(1)}, bf16[360,1024]{1,0:T(8,128)(2,1)S(1)}, u32[]{:S(2)}, u32[]{:S(2)}) %collective-permute-start.47) | collective-permute-done | bytes 737312 | tf_op jit(solution)/shard_map/ppermute | solution.py:943
  (430 shorter events, 341.7 us)
Async XLA Ops:
  7.2 345.4 %all-gather.3.cloned.1.call-start = ((), (), s32[]{:S(2)}) async-start(), calls=%async_computation.4 | async-start | bytes 27648000 | tf_op jit(solution)/shard_map/all_gather | solution.py:818
  29.0 48.2 %collective-permute-start.3 = (bf16[4,80,1152]{2,1,0:T(8,128)(2,1)}, bf16[4,80,1152]{2,1,0:T(8,128)(2,1)}, u32[]{:S(2)}, u32[]{:S(2)}) collective-permute-start(bf16[4,80,1152]{2,1,0:T(8,128)(2,1)} %bitcast_dynamic-update-slice_fusion.28), channel_id=1, source_target_pairs={{0,2},{1,3},{2,0},{3,1},{4,6},{5,7},{6,4},{7,5},{8,10},{9,11},{10,... | collective-permute-start | bytes 2211848 | tf_op jit(solution)/shard_map/ppermute | solution.py:682
  30.4 48.0 %collective-permute-start.4 = (bf16[4,80,1152]{2,1,0:T(8,128)(2,1)}, bf16[4,80,1152]{2,1,0:T(8,128)(2,1)}, u32[]{:S(2)}, u32[]{:S(2)}) collective-permute-start(bf16[4,80,1152]{2,1,0:T(8,128)(2,1)} %bitcast_dynamic-update-slice_fusion.28), channel_id=1, source_target_pairs={{0,4},{1,5},{2,6},{3,7},{4,0},{5,1},{6,2},{7,3},{8,12},{9,13},{10,... | collective-permute-start | bytes 2211848 | tf_op jit(solution)/shard_map/ppermute | solution.py:682
  33.4 46.2 %collective-permute-start.5 = (bf16[4,80,1152]{2,1,0:T(8,128)(2,1)}, bf16[4,80,1152]{2,1,0:T(8,128)(2,1)}, u32[]{:S(2)}, u32[]{:S(2)}) collective-permute-start(bf16[4,80,1152]{2,1,0:T(8,128)(2,1)} %bitcast_dynamic-update-slice_fusion.28), channel_id=1, source_target_pairs={{0,6},{1,7},{2,4},{3,5},{4,2},{5,3},{6,0},{7,1},{8,14},{9,15},{10,... | collective-permute-start | bytes 2211848 | tf_op jit(solution)/shard_map/ppermute | solution.py:682
  95.1 357.3 %all-gather.5.cloned.1.call-start = ((), (), s32[]{:S(2)}) async-start(), calls=%async_computation.5 | async-start | bytes 14745600 | tf_op jit(solution)/shard_map/all_gather | solution.py:858
  196.8 55.7 %collective-permute-start.19 = (bf16[4,128,2560]{2,1,0:T(8,128)(2,1)}, bf16[4,128,2560]{2,1,0:T(8,128)(2,1)}, u32[]{:S(2)}, u32[]{:S(2)}) collective-permute-start(bf16[4,128,2560]{2,1,0:T(8,128)(2,1)} %convolution_convert_fusion.1), channel_id=1, source_target_pairs={{0,1},{1,0},{2,3},{3,2},{4,5},{5,4},{6,7},{7,6},{8,9},{9,8},{10,11... | collective-permute-start | bytes 7864328 | tf_op jit(solution)/shard_map/ppermute | solution.py:631
  208.2 43.5 %collective-permute-start.24 = (bf16[128,2560]{1,0:T(8,128)(2,1)S(1)}, bf16[128,2560]{1,0:T(8,128)(2,1)S(1)}, u32[]{:S(2)}, u32[]{:S(2)}) collective-permute-start(bf16[128,2560]{1,0:T(8,128)(2,1)S(1)} %get-tuple-element.50), channel_id=1, source_target_pairs={{0,16},{8,24},{16,0},{24,8},{1,17},{9,25},{17,1},{25,9},{2,18},{10... | collective-permute-start | bytes 1966088 | tf_op jit(solution)/shard_map/ppermute | solution.py:82
  208.6 52.6 %collective-permute-start.25 = (bf16[128,2560]{1,0:T(8,128)(2,1)S(1)}, bf16[128,2560]{1,0:T(8,128)(2,1)S(1)}, u32[]{:S(2)}, u32[]{:S(2)}) collective-permute-start(bf16[128,2560]{1,0:T(8,128)(2,1)S(1)} %get-tuple-element.50), channel_id=1, source_target_pairs={{0,24},{8,0},{16,8},{24,16},{1,25},{9,1},{17,9},{25,17},{2,26},{10... | collective-permute-start | bytes 1966088 | tf_op jit(solution)/shard_map/ppermute | solution.py:82
  295.5 471.8 %reduce-scatter.2.cloned.1.call-start = ((), (), s32[]{:S(2)}) async-start(), calls=%async_computation.6 | async-start | bytes 27648000 | tf_op jit(solution)/shard_map/reduce_scatter | solution.py:879
  307.4 45.1 %collective-permute-start.27 = (bf16[128,2560]{1,0:T(8,128)(2,1)S(1)}, bf16[128,2560]{1,0:T(8,128)(2,1)S(1)}, u32[]{:S(2)}, u32[]{:S(2)}) collective-permute-start(bf16[128,2560]{1,0:T(8,128)(2,1)S(1)} %get-tuple-element.48), channel_id=1, source_target_pairs={{0,16},{8,24},{16,0},{24,8},{1,17},{9,25},{17,1},{25,9},{2,18},{10... | collective-permute-start | bytes 1966088 | tf_op jit(solution)/shard_map/ppermute | solution.py:82
  310.8 41.7 %collective-permute-start.28 = (bf16[128,2560]{1,0:T(8,128)(2,1)S(1)}, bf16[128,2560]{1,0:T(8,128)(2,1)S(1)}, u32[]{:S(2)}, u32[]{:S(2)}) collective-permute-start(bf16[128,2560]{1,0:T(8,128)(2,1)S(1)} %get-tuple-element.48), channel_id=1, source_target_pairs={{0,24},{8,0},{16,8},{24,16},{1,25},{9,1},{17,9},{25,17},{2,26},{10... | collective-permute-start | bytes 1966088 | tf_op jit(solution)/shard_map/ppermute | solution.py:82
  402.1 41.1 %collective-permute-start.30 = (bf16[128,2560]{1,0:T(8,128)(2,1)}, bf16[128,2560]{1,0:T(8,128)(2,1)}, u32[]{:S(2)}, u32[]{:S(2)}) collective-permute-start(bf16[128,2560]{1,0:T(8,128)(2,1)} %get-tuple-element.69), channel_id=1, source_target_pairs={{0,16},{8,24},{16,0},{24,8},{1,17},{9,25},{17,1},{25,9},{2,18},{10... | collective-permute-start | bytes 1966088 | tf_op jit(solution)/shard_map/ppermute | solution.py:82
  402.1 42.7 %collective-permute-start.29 = (bf16[128,2560]{1,0:T(8,128)(2,1)}, bf16[128,2560]{1,0:T(8,128)(2,1)}, u32[]{:S(2)}, u32[]{:S(2)}) collective-permute-start(bf16[128,2560]{1,0:T(8,128)(2,1)} %get-tuple-element.67), channel_id=1, source_target_pairs={{0,24},{8,0},{16,8},{24,16},{1,25},{9,1},{17,9},{25,17},{2,26},{10... | collective-permute-start | bytes 1966088 | tf_op jit(solution)/shard_map/ppermute | solution.py:82
  485.7 72.3 %collective-permute-start.33 = (bf16[128,2560]{1,0:T(8,128)(2,1)}, bf16[128,2560]{1,0:T(8,128)(2,1)}, u32[]{:S(2)}, u32[]{:S(2)}) collective-permute-start(bf16[128,2560]{1,0:T(8,128)(2,1)} %get-tuple-element.45), channel_id=1, source_target_pairs={{0,2},{1,3},{2,0},{3,1},{4,6},{5,7},{6,4},{7,5},{8,10},{9,11},{10,... | collective-permute-start | bytes 1966088 | tf_op jit(solution)/shard_map/ppermute | solution.py:682
  485.9 74.1 %collective-permute-start.34 = (bf16[128,2560]{1,0:T(8,128)(2,1)}, bf16[128,2560]{1,0:T(8,128)(2,1)}, u32[]{:S(2)}, u32[]{:S(2)}) collective-permute-start(bf16[128,2560]{1,0:T(8,128)(2,1)} %get-tuple-element.45), channel_id=1, source_target_pairs={{0,4},{1,5},{2,6},{3,7},{4,0},{5,1},{6,2},{7,3},{8,12},{9,13},{10,... | collective-permute-start | bytes 1966088 | tf_op jit(solution)/shard_map/ppermute | solution.py:682
  487.8 74.2 %collective-permute-start.35 = (bf16[128,2560]{1,0:T(8,128)(2,1)}, bf16[128,2560]{1,0:T(8,128)(2,1)}, u32[]{:S(2)}, u32[]{:S(2)}) collective-permute-start(bf16[128,2560]{1,0:T(8,128)(2,1)} %get-tuple-element.45), channel_id=1, source_target_pairs={{0,6},{1,7},{2,4},{3,5},{4,2},{5,3},{6,0},{7,1},{8,14},{9,15},{10,... | collective-permute-start | bytes 1966088 | tf_op jit(solution)/shard_map/ppermute | solution.py:682
  536.4 108.4 %all-to-all-start.1 = ((bf16[4,128,2560]{2,1,0:T(8,128)(2,1)}), bf16[4,128,2560]{2,1,0:T(8,128)(2,1)}, u32[]{:S(2)}, u32[]{:S(2)}) async-start(bf16[4,128,2560]{2,1,0:T(8,128)(2,1)} %bitcast.307), calls=%async_computation.1 | async-start | bytes 5242880 | tf_op jit(solution)/shard_map/all_to_all | solution.py:635
  566.5 65.7 %collective-permute-start.46 = (bf16[4,128,2560]{2,1,0:T(8,128)(2,1)}, bf16[4,128,2560]{2,1,0:T(8,128)(2,1)}, u32[]{:S(2)}, u32[]{:S(2)}) collective-permute-start(bf16[4,128,2560]{2,1,0:T(8,128)(2,1)} %bitcast_dynamic-update-slice_fusion.8), channel_id=1, source_target_pairs={{0,1},{1,0},{2,3},{3,2},{4,5},{5,4},{6,7},{7,6},{8,9},{9,8},{10,11... | collective-permute-start | bytes 7864328 | tf_op jit(solution)/shard_map/ppermute | solution.py:631
  644.8 80.6 %all-to-all-start.2 = ((bf16[4,360,1024]{2,1,0:T(8,128)(2,1)}), bf16[4,360,1024]{2,1,0:T(8,128)(2,1)}, u32[]{:S(2)}, u32[]{:S(2)}) async-start(bf16[4,360,1024]{2,1,0:T(8,128)(2,1)} %fusion.12), calls=%async_computation.2 | async-start | bytes 5898240 | tf_op jit(solution)/shard_map/all_to_all | solution.py:635
  655.6 35.9 %collective-permute-start.41 = (bf16[4,80,1152]{2,1,0:T(8,128)(2,1)S(1)}, bf16[4,80,1152]{2,1,0:T(8,128)(2,1)S(1)}, u32[]{:S(2)}, u32[]{:S(2)}) collective-permute-start(bf16[4,80,1152]{2,1,0:T(8,128)(2,1)S(1)} %get-tuple-element.66), channel_id=1, source_target_pairs={{0,4},{1,5},{2,6},{3,7},{4,0},{5,1},{6,2},{7,3},{8,12},{9,13},{10,... | collective-permute-start | bytes 2211848 | tf_op jit(solution)/shard_map/ppermute | solution.py:682
  656.2 35.4 %collective-permute-start.40 = (bf16[4,80,1152]{2,1,0:T(8,128)(2,1)S(1)}, bf16[4,80,1152]{2,1,0:T(8,128)(2,1)S(1)}, u32[]{:S(2)}, u32[]{:S(2)}) collective-permute-start(bf16[4,80,1152]{2,1,0:T(8,128)(2,1)S(1)} %get-tuple-element.64), channel_id=1, source_target_pairs={{0,2},{1,3},{2,0},{3,1},{4,6},{5,7},{6,4},{7,5},{8,10},{9,11},{10,... | collective-permute-start | bytes 2211848 | tf_op jit(solution)/shard_map/ppermute | solution.py:682
  692.0 37.8 %collective-permute-start.45 = (bf16[80,1152]{1,0:T(8,128)(2,1)S(1)}, bf16[80,1152]{1,0:T(8,128)(2,1)S(1)}, u32[]{:S(2)}, u32[]{:S(2)}) collective-permute-start(bf16[80,1152]{1,0:T(8,128)(2,1)S(1)} %get-tuple-element.79), channel_id=1, source_target_pairs={{0,8},{8,16},{16,24},{24,0},{1,9},{9,17},{17,25},{25,1},{2,10},{10... | collective-permute-start | bytes 552968 | tf_op jit(solution)/shard_map/ppermute | solution.py:82
  693.5 36.3 %collective-permute-start.44 = (bf16[80,1152]{1,0:T(8,128)(2,1)S(1)}, bf16[80,1152]{1,0:T(8,128)(2,1)S(1)}, u32[]{:S(2)}, u32[]{:S(2)}) collective-permute-start(bf16[80,1152]{1,0:T(8,128)(2,1)S(1)} %get-tuple-element.80), channel_id=1, source_target_pairs={{0,16},{8,24},{16,0},{24,8},{1,17},{9,25},{17,1},{25,9},{2,18},{10... | collective-permute-start | bytes 552968 | tf_op jit(solution)/shard_map/ppermute | solution.py:82
  727.9 36.6 %collective-permute-start.47 = (bf16[360,1024]{1,0:T(8,128)(2,1)S(1)}, bf16[360,1024]{1,0:T(8,128)(2,1)S(1)}, u32[]{:S(2)}, u32[]{:S(2)}) collective-permute-start(bf16[360,1024]{1,0:T(8,128)(2,1)S(1)} %reduce_sum.142), channel_id=1, source_target_pairs={{0,0},{1,12},{2,8},{3,20},{4,16},{5,28},{6,24},{7,4},{8,1},{9,13},... | collective-permute-start | bytes 2211848 | tf_op jit(solution)/shard_map/ppermute | solution.py:943
  (101 other events, 1486.3 us)
Sparse Core Ops, SparseCore 0:
  95.2 140.7 all-gather.2
  295.6 86.4 all-gather.4
  480.4 199.8 reduce-scatter.1

commit v4 on v3

--- a/solution.py
+++ b/solution.py
@@ -393,41 +393,64 @@
 QUERY_BLOCK = 256
 
 
-def head_keys(pairs, rotary):
-    lane = lax.broadcasted_iota(jnp.int32, pairs.shape, 1)
-    return jnp.where(lane < NOPE, pairs, rotary)
+def lane_of(values):
+    return lax.broadcasted_iota(jnp.int32, values.shape, 1)
+
+
+def dot_rows(left, right):
+    return lax.dot_general(left, right, (((1,), (1,)), ((), ())), preferred_element_type=F32)
 
 
 def block_scores(query, keys, start):
-    scores = lax.dot_general(
-        query, keys, (((1,), (1,)), ((), ())), preferred_element_type=F32
-    )
+    scores = dot_rows(query, keys)
     row = start + lax.broadcasted_iota(jnp.int32, scores.shape, 0)
-    column = lax.broadcasted_iota(jnp.int32, scores.shape, 1)
-    return jnp.where(row >= column, scores * SCORE_SCALE, -1e30)
-
-
-def turn(values, cos_ref, left_ref, right_ref, sign):
+    return jnp.where(row >= lane_of(scores), scores * SCORE_SCALE, -1e30)
+
+
+def write_tables(tail, cos_ref, left_ref, right_ref):
+    half = ROPE // 2
+    lane = lane_of(tail)
+    sums = tail + pltpu.roll(tail, HEAD_LANES - half, 1)
+    upper = (lane >= NOPE + half) & (lane < NOPE + ROPE)
+    lower = (lane >= NOPE) & (lane < NOPE + half)
+    cos = jnp.where(lower, pltpu.roll(sums, NOPE, 1), pltpu.roll(sums, NOPE + half, 1))
+    cos_ref[...] = jnp.where(lane < NOPE, 1.0, jnp.where(lower | upper, cos, 0.0))
+    left_ref[...] = jnp.where(lower, -pltpu.roll(sums, NOPE - 2 * half, 1), 0.0)
+    right_ref[...] = jnp.where(upper, pltpu.roll(sums, NOPE - half, 1), 0.0)
+
+
+def turn(values, cos, left, right, sign):
     half = ROPE // 2
     return (
-        values * cos_ref
-        + sign * (pltpu.roll(values, HEAD_LANES - half, 1) * left_ref)
-        + sign * (pltpu.roll(values, half, 1) * right_ref)
+        values * cos
+        + sign * (pltpu.roll(values, HEAD_LANES - half, 1) * left)
+        + sign * (pltpu.roll(values, half, 1) * right)
     )
 
 
 def attend_kernel(
-    projected_ref, pairs_ref, rotary_ref, cos_ref, left_ref, right_ref,
-    query_ref, attended_ref, log_ref, keys_ref,
+    tokens_ref, query_up_ref, pair_up_ref,
+    query_ref, pairs_ref, attended_ref, log_ref, keys_ref, cos_ref, left_ref, right_ref,
 ):
-    length = projected_ref.shape[0]
+    length = tokens_ref.shape[0]
+    rank = query_up_ref.shape[1]
+    tail_start = rank + pair_up_ref.shape[1]
     block = min(QUERY_BLOCK, length)
-    keys_ref[...] = head_keys(pairs_ref[...], rotary_ref[...])
+    head = pl.program_id(0)
+
+    @pl.when(head == 0)
+    def _():
+        write_tables(tokens_ref[:, tail_start:].astype(F32), cos_ref, left_ref, right_ref)
+
+    pairs = dot_rows(tokens_ref[:, rank:tail_start], pair_up_ref[...]).astype(BF16)
+    pairs_ref[...] = pairs
+    keys_ref[...] = jnp.where(lane_of(pairs) < NOPE, pairs, tokens_ref[:, tail_start:])
     for start in range(0, length, block):
         rows = pl.ds(start, block)
         stop = start + block
+        projected = dot_rows(tokens_ref[rows, 0:rank], query_up_ref[...])
         query = turn(
-            projected_ref[rows, :], cos_ref[rows, :], left_ref[rows, :], right_ref[rows, :], 1.0
+            projected, cos_ref[rows, :], left_ref[rows, :], right_ref[rows, :], 1.0
         ).astype(BF16)
         query_ref[rows, :] = query
         scores = block_scores(query, keys_ref[0:stop, :], start)
@@ -436,106 +459,165 @@
         totals = jnp.sum(terms, axis=-1, keepdims=True)
         probs = (terms / totals).astype(BF16)
         mixed = jnp.dot(probs, pairs_ref[0:stop, :], preferred_element_type=F32)
-        lane = lax.broadcasted_iota(jnp.int32, mixed.shape, 1)
-        attended_ref[rows, :] = jnp.where(lane >= NOPE, mixed, 0.0).astype(BF16)
         log_ref[rows, :] = jnp.broadcast_to(peak + jnp.log(totals), mixed.shape)
-
-
-def attend(projected, pairs, rotary, tables):
-    length, lanes = projected.shape
+        lane = lane_of(mixed)
+
+        @pl.when(head % 2 == 0)
+        def _():
+            attended_ref[rows, :] = jnp.where(
+                lane < NOPE, pltpu.roll(mixed, NOPE, 1), 0.0
+            ).astype(BF16)
+
+        @pl.when(head % 2 == 1)
+        def _():
+            attended_ref[rows, :] = jnp.where(
+                lane < NOPE, attended_ref[rows, :].astype(F32), mixed
+            ).astype(BF16)
+
+
+def attend(tokens, query_up, pair_up):
+    length = tokens.shape[0]
+    lanes = query_up.shape[0]
+    heads = lanes // HEAD_LANES
+    whole = pl.BlockSpec(memory_space=pltpu.VMEM)
     own = pl.BlockSpec((length, HEAD_LANES), lambda h: (0, h))
-    shared = pl.BlockSpec((length, HEAD_LANES), lambda h: (0, 0))
+    table = pltpu.VMEM((length, HEAD_LANES), F32)
     return pl.pallas_call(
         attend_kernel,
-        grid=(lanes // HEAD_LANES,),
-        in_specs=[own, own, shared, shared, shared, shared],
-        out_specs=[own, own, own],
+        grid=(heads,),
+        in_specs=[
+            whole,
+            pl.BlockSpec((HEAD_LANES, query_up.shape[1]), lambda h: (h, 0)),
+            pl.BlockSpec((HEAD_LANES, pair_up.shape[1]), lambda h: (h, 0)),
+        ],
+        out_specs=[
+            own, own, pl.BlockSpec((length, HEAD_LANES), lambda h: (0, h // 2)), own
+        ],
         out_shape=[
             jax.ShapeDtypeStruct((length, lanes), BF16),
             jax.ShapeDtypeStruct((length, lanes), BF16),
+            jax.ShapeDtypeStruct((length, (heads + 1) // 2 * HEAD_LANES), BF16),
             jax.ShapeDtypeStruct((length, lanes), F32),
         ],
-        scratch_shapes=[pltpu.VMEM((length, HEAD_LANES), BF16)],
+        scratch_shapes=[pltpu.VMEM((length, HEAD_LANES), BF16), table, table, table],
         compiler_params=pltpu.CompilerParams(vmem_limit_bytes=40 * 1024 * 1024),
         cost_estimate=pl.CostEstimate(
             flops=3 * lanes * length * length, bytes_accessed=12 * lanes * length,
-            transcendentals=length * length * lanes // HEAD_LANES,
+            transcendentals=length * length * heads,
         ),
         name="attend",
-    )(projected, pairs, rotary, *tables)
+    )(tokens, query_up, pair_up)
 
 
 def attend_back_kernel(
-    query_ref, pairs_ref, rotary_ref, log_ref, grad_ref, cos_ref, left_ref, right_ref,
-    earlier_ref, grad_query_ref, grad_pairs_ref, grad_rotary_ref, keys_ref, grad_keys_ref, grad_values_ref,
+    tokens_ref, query_up_ref, pair_up_ref, query_ref, pairs_ref, log_ref, grad_ref,
+    first_ref, second_ref,
+    grad_query_ref, grad_pairs_ref, grad_tokens_ref,
+    keys_ref, cos_ref, left_ref, right_ref, grad_ready_ref, grad_keys_ref, grad_values_ref,
+    sum_ref,
 ):
-    length = query_ref.shape[0]
+    length = tokens_ref.shape[0]
+    rank = query_up_ref.shape[1]
+    tail_start = rank + pair_up_ref.shape[1]
     block = min(QUERY_BLOCK, length)
-    keys_ref[...] = head_keys(pairs_ref[...], rotary_ref[...])
+    head = pl.program_id(0)
+
+    @pl.when(head == 0)
+    def _():
+        write_tables(tokens_ref[:, tail_start:].astype(F32), cos_ref, left_ref, right_ref)
+        sum_ref[...] = jnp.zeros_like(sum_ref)
+
+    pairs = pairs_ref[...]
+    lane = lane_of(pairs)
+    keys_ref[...] = jnp.where(lane < NOPE, pairs, tokens_ref[:, tail_start:])
+    shared = grad_ref[...].astype(F32)
+    shared = jnp.where(head % 2 == 0, pltpu.roll(shared, NOPE, 1), shared)
+    grad_ready_ref[...] = jnp.where(lane >= NOPE, shared, 0.0).astype(BF16)
     grad_keys_ref[...] = jnp.zeros_like(grad_keys_ref)
     grad_values_ref[...] = jnp.zeros_like(grad_values_ref)
     for start in range(0, length, block):
         rows = pl.ds(start, block)
         stop = start + block
         query = query_ref[rows, :]
-        grad = grad_ref[rows, :]
+        grad = grad_ready_ref[rows, :]
         scores = block_scores(query, keys_ref[0:stop, :], start)
         probs = jnp.exp(scores - log_ref[rows, 0:1])
-        grad_probs = lax.dot_general(
-            grad, pairs_ref[0:stop, :], (((1,), (1,)), ((), ())), preferred_element_type=F32
-        )
+        grad_probs = dot_rows(grad, pairs_ref[0:stop, :])
         delta = jnp.sum(probs * grad_probs, axis=-1, keepdims=True)
         grad_scores = (probs * (grad_probs - delta)).astype(BF16)
         grad_query = (
             jnp.dot(grad_scores, keys_ref[0:stop, :], preferred_element_type=F32) * SCORE_SCALE
         )
-        grad_query_ref[rows, :] = turn(
+        grad_query = turn(
             grad_query, cos_ref[rows, :], left_ref[rows, :], right_ref[rows, :], -1.0
         ).astype(BF16)
-        grad_keys_ref[:, 0:stop] += jnp.dot(
-            query.T, grad_scores, preferred_element_type=F32
+        grad_query_ref[rows, :] = grad_query
+        sum_ref[rows, 0:rank] += jnp.dot(
+            grad_query, query_up_ref[...], preferred_element_type=F32
         )
+        grad_keys_ref[:, 0:stop] += jnp.dot(query.T, grad_scores, preferred_element_type=F32)
         grad_values_ref[:, 0:stop] += jnp.dot(
             grad.T, probs.astype(BF16), preferred_element_type=F32
         )
     grad_keys = grad_keys_ref[...].T * SCORE_SCALE
-    lane = lax.broadcasted_iota(jnp.int32, grad_keys.shape, 1)
-    grad_pairs_ref[...] = jnp.where(lane < NOPE, grad_keys, grad_values_ref[...].T).astype(BF16)
-
-    @pl.when(pl.program_id(0) == 0)
+    grad_pairs = jnp.where(lane < NOPE, grad_keys, grad_values_ref[...].T).astype(BF16)
+    grad_pairs_ref[...] = grad_pairs
+    sum_ref[:, rank:tail_start] += jnp.dot(
+        grad_pairs, pair_up_ref[...], preferred_element_type=F32
+    )
+    sum_ref[:, tail_start:] += jnp.where((lane >= NOPE) & (lane < NOPE + ROPE), grad_keys, 0.0)
+
+    @pl.when(head == pl.num_programs(0) - 1)
     def _():
-        grad_rotary_ref[...] = jnp.zeros_like(grad_rotary_ref)
-
-    grad_rotary_ref[...] += grad_keys
-
-
-def attend_back(query, pairs, rotary, logs, grad, tables, earlier):
-    length, lanes = query.shape
+        grad_tokens_ref[...] = sum_ref[...].astype(BF16)
+
+
+def attend_back(tokens, query_up, pair_up, query, pairs, logs, grad, first, second):
+    length, width = tokens.shape
+    lanes = query.shape[1]
+    heads = lanes // HEAD_LANES
+    whole = pl.BlockSpec(memory_space=pltpu.VMEM)
+    anywhere = pl.BlockSpec(memory_space=pl.ANY)
     own = pl.BlockSpec((length, HEAD_LANES), lambda h: (0, h))
-    shared = pl.BlockSpec((length, HEAD_LANES), lambda h: (0, 0))
+    table = pltpu.VMEM((length, HEAD_LANES), F32)
+    turned = pltpu.VMEM((HEAD_LANES, length), F32)
     return pl.pallas_call(
         attend_back_kernel,
-        grid=(lanes // HEAD_LANES,),
-        in_specs=[own, own, shared, own, own, shared, shared, shared]
-        + [pl.BlockSpec(memory_space=pl.ANY)],
-        out_specs=[own, own, shared],
+        grid=(heads,),
+        in_specs=[
+            whole,
+            pl.BlockSpec((HEAD_LANES, query_up.shape[1]), lambda h: (h, 0)),
+            pl.BlockSpec((HEAD_LANES, pair_up.shape[1]), lambda h: (h, 0)),
+            own,
+            own,
+            own,
+            pl.BlockSpec((length, HEAD_LANES), lambda h: (0, h // 2)),
+            anywhere,
+            anywhere,
+        ],
+        out_specs=[own, own, pl.BlockSpec((length, width), lambda h: (0, 0))],
         out_shape=[
             jax.ShapeDtypeStruct((length, lanes), BF16),
             jax.ShapeDtypeStruct((length, lanes), BF16),
-            jax.ShapeDtypeStruct((length, HEAD_LANES), F32),
+            jax.ShapeDtypeStruct((length, width), BF16),
         ],
         scratch_shapes=[
             pltpu.VMEM((length, HEAD_LANES), BF16),
-            pltpu.VMEM((HEAD_LANES, length), F32),
-            pltpu.VMEM((HEAD_LANES, length), F32),
+            table,
+            table,
+            table,
+            pltpu.VMEM((length, HEAD_LANES), BF16),
+            turned,
+            turned,
+            pltpu.VMEM((length, width), F32),
         ],
         compiler_params=pltpu.CompilerParams(vmem_limit_bytes=48 * 1024 * 1024),
         cost_estimate=pl.CostEstimate(
             flops=8 * lanes * length * length, bytes_accessed=14 * lanes * length,
-            transcendentals=length * length * lanes // HEAD_LANES,
+            transcendentals=length * length * heads,
         ),
         name="attend_back",
-    )(query, pairs, rotary, logs, grad, *tables, earlier)
+    )(tokens, query_up, pair_up, query, pairs, logs, grad, first, second)
 
 
 def ffn_kernel(weights_ref, rows_ref, grads_ref, both_ref, act_ref):
@@ -798,64 +880,32 @@
         return [high, (table - high.astype(F32)).astype(BF16)]
 
     token_message = jnp.concatenate(
-        [query_normed, latent, rotary_keys]
+        [query_normed, latent]
         + two_parts(cos_table[:, :half])
-        + two_parts(sin_table[:, :half]),
+        + two_parts(sin_table[:, :half])
+        + [rotary_keys, jnp.zeros((tokens, HEAD_LANES - NOPE - ROPE), BF16)],
         1,
     )
-    proj_moved = lax.ppermute(output_proj, both, to_group)
-    proj_group = gather_z(hold(proj_moved, done(token_message))).reshape(-1, width)
-    token_all = gather_seq(token_message, done(proj_group)).reshape(
-        length, token_message.shape[1]
-    )
+    tail_start = query_rank + KV_RANK
+    token_all = gather_seq(token_message).reshape(length, token_message.shape[1])
+    proj_full = lax.all_gather(hold(output_proj, done(down_plane)), both, axis=0, tiled=True)
     grad_out = cotangent.astype(F32)
     grad_two = (RESIDUAL_SCALE * grad_out).astype(BF16)
-    grad_rows = gather_z(hold(grad_two, done(proj_group))).reshape(-1, width)
-    proj_padded = jnp.pad(
-        proj_group.reshape(heads, VDIM, width), ((0, 0), (HEAD_LANES - VDIM, 0), (0, 0))
-    ).reshape(heads * HEAD_LANES, width)
+    grad_rows = gather_z(hold(grad_two, done(token_message))).reshape(-1, width)
     ffn_own = hold(jnp.stack([ffn_gate.T, ffn_up.T, ffn_down]), done(down_full))
     ffn_full = lax.all_gather(ffn_own, "seq", axis=1, tiled=True)
 
-    query_normed_all = token_all[:, :query_rank]
-    latent_all = token_all[:, query_rank : query_rank + KV_RANK]
-    rotary_all = token_all[:, query_rank + KV_RANK : down_width]
-    angles = token_all[:, down_width:].astype(F32)
-    cos_all = angles[:, :half] + angles[:, half : 2 * half]
-    sin_all = angles[:, 2 * half : 3 * half] + angles[:, 3 * half :]
-
-    def lanes(start, values):
-        return jnp.pad(values, ((0, 0), (start, HEAD_LANES - start - values.shape[1])))
-
-    tables = (
-        jnp.concatenate(
-            [
-                jnp.ones((length, NOPE), F32),
-                cos_all,
-                cos_all,
-                jnp.zeros((length, HEAD_LANES - NOPE - ROPE), F32),
-            ],
-            1,
-        ),
-        lanes(NOPE, -sin_all),
-        lanes(NOPE + half, sin_all),
-    )
-    rotary_lanes = lanes(NOPE, rotary_all)
-    projected = dot("tq,kq->tk", query_normed_all, query_up_padded)
-    pairs = dot("tc,kc->tk", latent_all, latent_up_group).astype(BF16)
-    query, attended, logs = attend(projected, pairs, rotary_lanes, tables)
-
-    attended_mine, attended_theirs = by_core(attended)
-    branch = scatter_seq(
-        dot("mtk,kd->mtd", attended_mine, proj_padded),
-        dot("mtk,kd->mtd", attended_theirs, proj_padded),
-    )
+    query, pairs, attended, logs = attend(token_all, query_up_padded, latent_up_group)
+    head_width = heads * VDIM
+    group_place = [group_of.index(g) for g in range(seq_count)]
+    attended_own = exchange(attended.reshape(seq_count, tokens, -1), "seq")[:, :, :head_width]
+    attended_own = jnp.concatenate([attended_own[s] for s in group_place], 1)
+    branch = jnp.dot(attended_own, proj_full, preferred_element_type=F32)
     middle = inputs + RESIDUAL_SCALE * branch
     normal_two, inverse_two = norm_parts(middle)
     normed_two = hold((normal_two * ffn_gain_full).astype(BF16), done(grad_rows))
 
     normed_rows = gather_z(normed_two).reshape(-1, width)
-    proj_full = lax.all_gather(hold(proj_group, done(normed_two)), "seq", axis=0, tiled=True)
     own_hidden = ffn_down.shape[0]
     count = dp_count * tokens
     grad_both, activated = ffn_hidden(ffn_full, normed_rows, grad_rows)
@@ -868,7 +918,8 @@
     grad_normed_two = choose(grad_parts, place, 0).astype(F32)
     for piece in returned:
         grad_normed_two = grad_normed_two + piece.astype(F32)
-    out_part = dot("ft,fd->td", activated, ffn_full[2]).astype(BF16)
+    out_part = dot("ft,fd->td", activated, ffn_full[2]).reshape(dp_count, tokens, width)
+    layer_output = (middle + RESIDUAL_SCALE * scatter_z(out_part)).astype(BF16)
 
     grad_middle_norm, grad_ffn_gain_part = norm_back(
         grad_normed_two, normal_two, inverse_two, ffn_gain_full
@@ -887,41 +938,32 @@
         "seq",
         scatter_dimension=0,
     ).astype(F32)
-    grad_attended = exchange(
-        grad_attended.reshape(tokens, seq_count, heads * VDIM).transpose(1, 0, 2), "seq"
-    ).reshape(length, heads, VDIM)
-    grad_attended = jnp.pad(
-        grad_attended, ((0, 0), (0, 0), (HEAD_LANES - VDIM, 0))
-    ).reshape(length, heads * HEAD_LANES)
-    grad_projected, grad_pairs, grad_rotary = attend_back(
-        query, pairs, rotary_lanes, logs, grad_attended, tables, out_part
-    )
-    token_grads = []
-    for projected_part, pairs_part, rotary_part in zip(
-        by_core(grad_projected), by_core(grad_pairs), by_core(grad_rotary)
-    ):
-        token_grads.append(
-            jnp.concatenate(
-                [
-                    dot("mtk,kq->mtq", projected_part, query_up_padded).astype(BF16),
-                    dot("mtk,kc->mtc", pairs_part, latent_up_group).astype(BF16),
-                    rotary_part[:, :, NOPE : NOPE + ROPE].astype(BF16),
-                ],
-                2,
-            )
-        )
+    grad_blocks = jnp.stack(
+        [grad_attended[:, g * head_width : (g + 1) * head_width] for g in group_of]
+    )
+    grad_blocks = jnp.pad(
+        grad_blocks, ((0, 0), (0, 0), (0, attended.shape[1] - head_width))
+    )
+    grad_heads = exchange(grad_blocks, "seq").reshape(length, -1)
     branch_plane = gather_plane(grad_branch)
-    grad_own = scatter_seq(token_grads[0], token_grads[1], done(branch_plane))
-    out_parts = hold(out_part.reshape(dp_count, tokens, width), done(grad_attended))
-    out_sum = jnp.sum(exchange(out_parts, "dp").astype(F32), 0)
-    layer_output = (middle + RESIDUAL_SCALE * out_sum).astype(BF16)
-
-    home = done(grad_own)
-    query_up_grads = dot("tk,tq->kq", hold(grad_projected, home), query_normed_all).astype(BF16)
+    grad_projected, grad_pairs, grad_tokens = attend_back(
+        token_all,
+        query_up_padded,
+        latent_up_group,
+        query,
+        pairs,
+        logs,
+        grad_heads,
+        layer_output,
+        branch_plane,
+    )
+    grad_own = scatter_seq(*by_core(grad_tokens))
+
+    query_up_grads = dot("tk,tq->kq", grad_projected, token_all[:, :query_rank]).astype(BF16)
     query_up_grads = query_up_grads.reshape(heads, HEAD_LANES, query_rank)[:, : NOPE + ROPE]
     query_up_grads = query_up_grads.reshape(dp_count, -1, query_rank)
-    latent_up_grads = dot("tk,tc->kc", hold(grad_pairs, home), latent_all).astype(BF16)
-    latent_up_grads = latent_up_grads.reshape(dp_count, -1, KV_RANK)
+    latent_up_grads = dot("tk,tc->kc", grad_pairs, token_all[:, query_rank:tail_start])
+    latent_up_grads = latent_up_grads.astype(BF16).reshape(dp_count, -1, KV_RANK)
     up_grads = jnp.concatenate(
         [
             jnp.pad(
@@ -935,7 +977,7 @@
     )
     branch_all = with_other_core(branch_plane)
     proj_grads = dot("tk,td->kd", attended, branch_all.reshape(length, width)).astype(BF16)
-    proj_grads = proj_grads.reshape(heads, HEAD_LANES, width)[:, HEAD_LANES - VDIM :]
+    proj_grads = proj_grads[:head_width]
     group_grads = jnp.concatenate(
         [up_grads, proj_grads.reshape(dp_count, -1, up_grads.shape[2])], 1
     )
@@ -958,7 +1000,9 @@
         [
             grad_query_latent,
             grad_latent_norm,
-            rotate_back(grad_own[:, query_rank + KV_RANK :], cos_table, sin_table),
+            rotate_back(
+                grad_own[:, tail_start + NOPE : tail_start + NOPE + ROPE], cos_table, sin_table
+            ),
             jnp.zeros((tokens, padded_width - down_width), F32),
         ],
         -1,
@@ -988,7 +1032,9 @@
     down_sums = down_sums.astype(BF16).reshape(dp_count, chips, 2, own_rows, padded_width)
     down_sums = down_sums.transpose(1, 2, 0, 3, 4)
     sum_down = scatter_z(
-        scatter_seq(choose(down_sums, core, 1), choose(down_sums, 1 - core, 1))
+        scatter_seq(
+            choose(down_sums, core, 1), choose(down_sums, 1 - core + done(group_grads), 1)
+        )
     )
     sum_gains = sum_down[:, down_width : down_width + 4].T
     return (

time: 789 us -> 802 us (1.016)
  waiting for transfers between devices: 318 us -> 373 us
  local copies, waits for them, and re-layouts: 114 us -> 85.8 us
  Pallas kernels: 65.8 us -> 87.5 us
  matrix products: 76.3 us -> 56.9 us
    ppermute x21, waiting for transfers between devices: 158 us -> 202 us  [shift(): lax.ppermute(value, axis, [(i, (i + step) % count) for i in range(count)])]
    dot_general x16 -> x8, matrix products: 71.9 us -> 46.5 us  [dot(): return jnp.einsum(spec, left, right, preferred_element_type=F32)]
    pallas_call x2, Pallas kernels: 28.5 us -> 50.4 us  [the longest x1 26.1 us: attend_back(): pl.pallas_call(attend_back_kernel, grid=(heads,), in_specs=[whole, pl.Blo...]
    ppermute x1, waiting for transfers between devices: 0.01 us -> 10 us  [per_device_heads(): up_moved = lax.ppermute(up_packed, both, to_group)]
    unnamed x143 -> x122, local copies, waits for them, and re-layouts: 12.4 us -> 18.2 us
    ppermute x18 -> x15, starting transfers between devices: 21.2 us -> 17.7 us  [across(): lax.ppermute(value, 'seq', [(i, i ^ 2 * steps) for i in range(seq_count)])]
    ppermute x18 -> x15, waiting for transfers between devices: 92.4 us -> 88.9 us  [across(): lax.ppermute(value, 'seq', [(i, i ^ 2 * steps) for i in range(seq_count)])]
  transfers between devices with their start and end apart: 54 -> 49, of which waited for: 25 -> 27; matrix products, arithmetic and copies ran while one was open for 25% -> 15% of each run, Pallas kernels for 6% -> 6%
where the time goes in v4:
time: 802 us; the launch traced here: 792 us
  waiting for transfers between devices  373 us (47%)
  starting transfers between devices  130 us (16%)
  Pallas kernels  87.5 us (11%)
  local copies, waits for them, and re-layouts  85.8 us (11%)
  matrix products  56.9 us (7%)
  other arithmetic  36.1 us (5%)
  between operations  23.4 us (3%)
    ppermute x21, waiting for transfers between devices, shift(): lax.ppermute(value, axis, [(i, (i + step) % count) for i in range(count)])  202 us
    ppermute x15, waiting for transfers between devices, across(): lax.ppermute(value, 'seq', [(i, i ^ 2 * steps) for i in range(seq_count)])  88.9 us
    ppermute x21, starting transfers between devices, shift(): lax.ppermute(value, axis, [(i, (i + step) % count) for i in range(count)])  69.8 us
    dot_general x8, matrix products, dot(): return jnp.einsum(spec, left, right, preferred_element_type=F32)  46.5 us
    all_to_all x3, waiting for transfers between devices, exchange(): lax.all_to_all(blocks, axis, split_axis=0, concat_axis=0, axis_index_grou...  34 us
    ppermute x1, waiting for transfers between devices, per_device_heads(): lax.ppermute(group_sums.astype(BF16), both, to_owner).astype(F32)  30.8 us
    all_to_all x3, starting transfers between devices, exchange(): lax.all_to_all(blocks, axis, split_axis=0, concat_axis=0, axis_index_grou...  28.3 us
    pallas_call x1, Pallas kernels, attend_back(): pl.pallas_call(attend_back_kernel, grid=(heads,), in_specs=[whole, pl.Blo...  26.1 us
  transfers between devices with their start and end apart: 49, of which 27 were waited for; matrix products, arithmetic and copies ran while one was open for 15% of the time, Pallas kernels for 6%

profile of v4, /device:TPU:2, one launch (start us, length us, event | category | flops | bytes accessed | tf_op | source)
XLA Modules:
  0.0 792.4 jit_solution(7380152188014414075)
XLA Ops:
  40.7 10.0 %collective-permute-done.6 = bf16[160,1024]{1,0:T(8,128)(2,1)S(1)} collective-permute-done((bf16[160,1024]{1,0:T(8,128)(2,1)S(1)}, bf16[160,1024]{1,0:T(8,128)(2,1)S(1)}, u32[]{:S(2)}, u32[]{:S(2)}) %collective-permute-start.6) | collective-permute-done | bytes 327712 | tf_op jit(solution)/shard_map/ppermute | solution.py:845
  73.1 29.0 %collective-permute-done.8 = bf16[160,1024]{1,0:T(8,128)(2,1)S(1)} collective-permute-done((bf16[160,1024]{1,0:T(8,128)(2,1)S(1)}, bf16[160,1024]{1,0:T(8,128)(2,1)S(1)}, u32[]{:S(2)}, u32[]{:S(2)}) %collective-permute-start.8) | collective-permute-done | bytes 327712 | tf_op jit(solution)/shard_map/ppermute | solution.py:82
  160.1 10.9 %collective-permute-done.15 = bf16[128,2560]{1,0:T(8,128)(2,1)S(1)} collective-permute-done((bf16[128,2560]{1,0:T(8,128)(2,1)}, bf16[128,2560]{1,0:T(8,128)(2,1)S(1)}, u32[]{:S(2)}, u32[]{:S(2)}) %collective-permute-start.15) | collective-permute-done | bytes 655392 | tf_op jit(solution)/shard_map/ppermute | solution.py:82
  171.1 26.9 %collective-permute-done.16 = bf16[128,2560]{1,0:T(8,128)(2,1)S(1)} collective-permute-done((bf16[128,2560]{1,0:T(8,128)(2,1)}, bf16[128,2560]{1,0:T(8,128)(2,1)S(1)}, u32[]{:S(2)}, u32[]{:S(2)}) %collective-permute-start.16) | collective-permute-done | bytes 655392 | tf_op jit(solution)/shard_map/ppermute | solution.py:82
  199.6 24.3 %attend.1 = (bf16[1024,640]{1,0:T(8,128)(2,1)S(1)}, bf16[1024,640]{1,0:T(8,128)(2,1)S(1)}, bf16[1024,384]{1,0:T(8,128)(2,1)}, f32[1024,640]{1,0:T(8,128)S(1)}) custom-call(bf16[1024,1152]{1,0:T(8,128)(2,1)S(1)} %bitcast.282, bf16[640,768]{1,0:T(8,128)(2,1)S(1)} %bitcast.286, bf16[640,256]{1,0:T(8,128)(2,1)S(1)} %bitcast.289), custom_call_target="tpu_custom_call" | custom-call | flops 2013265920 | bytes 7864320 | tf_op jit(solution)/shard_map/attend/pallas_call | solution.py:485
  236.3 13.9 %all-to-all-done = bf16[8,128,384]{2,1,0:T(8,128)(2,1)S(1)} async-done(((bf16[8,128,384]{2,1,0:T(8,128)(2,1)}), bf16[8,128,384]{2,1,0:T(8,128)(2,1)S(1)}, u32[]{:S(2)}, u32[]{:S(2)}) %all-to-all-start) | async-done | bytes 786464 | tf_op jit(solution)/shard_map/all_to_all | solution.py:717
  258.5 12.9 %collective-permute-start.18 = (bf16[128,2560]{1,0:T(8,128)(2,1)S(1)}, bf16[128,2560]{1,0:T(8,128)(2,1)S(1)}, u32[]{:S(2)}, u32[]{:S(2)}) collective-permute-start(bf16[128,2560]{1,0:T(8,128)(2,1)S(1)} %get-tuple-element.50), channel_id=1, source_target_pairs={{0,8},{8,16},{16,24},{24,0},{1,9},{9,17},{17,25},{25,1},{2,10},{10... | collective-permute-start | bytes 1966088 | tf_op jit(solution)/shard_map/ppermute | solution.py:82
  275.1 14.8 %collective-permute-done.18 = bf16[128,2560]{1,0:T(8,128)(2,1)S(1)} collective-permute-done((bf16[128,2560]{1,0:T(8,128)(2,1)S(1)}, bf16[128,2560]{1,0:T(8,128)(2,1)S(1)}, u32[]{:S(2)}, u32[]{:S(2)}) %collective-permute-start.18) | collective-permute-done | bytes 655392 | tf_op jit(solution)/shard_map/ppermute | solution.py:82
  290.0 26.4 %collective-permute-done.19 = bf16[128,2560]{1,0:T(8,128)(2,1)S(1)} collective-permute-done((bf16[128,2560]{1,0:T(8,128)(2,1)S(1)}, bf16[128,2560]{1,0:T(8,128)(2,1)S(1)}, u32[]{:S(2)}, u32[]{:S(2)}) %collective-permute-start.19) | collective-permute-done | bytes 655392 | tf_op jit(solution)/shard_map/ppermute | solution.py:82
  316.5 18.6 %ffn_hidden.1 = (bf16[2,1600,512]{2,1,0:T(8,128)(2,1)}, bf16[1600,512]{1,0:T(8,128)(2,1)S(1)}) custom-call(bf16[3,1600,2560]{2,1,0:T(8,128)(2,1)} %all-gather.5.cloned.1.call-done.weights_ref, bf16[512,2560]{1,0:T(8,128)(2,1)S(1)} %bitcast.280, bf16[512,2560]{1,0:T(8,128)(2,1)} %bitcast.304), custom_call_target="tpu_custom_call" | custom-call | flops 12582912000 | bytes 34734080 | tf_op jit(solution)/shard_map/ffn_hidden/pallas_call | solution.py:647
  335.1 14.2 %bitcast_convert_fusion = bf16[512,2560]{1,0:T(8,128)(2,1)S(1)} fusion(bf16[2,1600,512]{2,1,0:T(8,128)(2,1)} %get-tuple-element.25, bf16[3,1600,2560]{2,1,0:T(8,128)(2,1)} %all-gather.5.cloned.1.call-done.weights_ref), kind=kOutput, calls=%fused_computation.13 | convolution fusion | flops 8389918720 | bytes 22282240 | tf_op jit(solution)/shard_map/gft,gfd->td/dot_general | solution.py:78
  350.7 14.4 %collective-permute-start.26 = (bf16[128,2560]{1,0:T(8,128)(2,1)S(1)}, bf16[128,2560]{1,0:T(8,128)(2,1)S(1)}, u32[]{:S(2)}, u32[]{:S(2)}) collective-permute-start(bf16[128,2560]{1,0:T(8,128)(2,1)S(1)} %get-tuple-element.64), channel_id=1, source_target_pairs={{0,8},{8,16},{16,24},{24,0},{1,9},{9,17},{17,25},{25,1},{2,10},{10... | collective-permute-start | bytes 1966088 | tf_op jit(solution)/shard_map/ppermute | solution.py:82
  382.9 25.3 %collective-permute-done.25 = bf16[128,2560]{1,0:T(8,128)(2,1)} collective-permute-done((bf16[128,2560]{1,0:T(8,128)(2,1)}, bf16[128,2560]{1,0:T(8,128)(2,1)}, u32[]{:S(2)}, u32[]{:S(2)}) %collective-permute-start.25) | collective-permute-done | bytes 655392 | tf_op jit(solution)/shard_map/ppermute | solution.py:82
  408.5 14.0 %collective-permute-done.23 = bf16[128,2560]{1,0:T(8,128)(2,1)} collective-permute-done((bf16[128,2560]{1,0:T(8,128)(2,1)}, bf16[128,2560]{1,0:T(8,128)(2,1)}, u32[]{:S(2)}, u32[]{:S(2)}) %collective-permute-start.23) | collective-permute-done | bytes 655392 | tf_op jit(solution)/shard_map/ppermute | solution.py:82
  422.5 39.6 %collective-permute-done.22 = bf16[128,2560]{1,0:T(8,128)(2,1)} collective-permute-done((bf16[128,2560]{1,0:T(8,128)(2,1)}, bf16[128,2560]{1,0:T(8,128)(2,1)}, u32[]{:S(2)}, u32[]{:S(2)}) %collective-permute-start.22) | collective-permute-done | bytes 655392 | tf_op jit(solution)/shard_map/ppermute | solution.py:82
  479.9 18.5 %ffn_grads.1 = bf16[8,600,2560]{2,1,0:T(8,128)(2,1)} custom-call(bf16[2,8,200,512]{3,2,1,0:T(8,128)(2,1)} %bitcast.321, bf16[8,200,512]{2,1,0:T(8,128)(2,1)S(1)} %bitcast.291, bf16[512,2560]{1,0:T(8,128)(2,1)S(1)} %bitcast.281, bf16[512,2560]{1,0:T(8,128)(2,1)} %bitcast.305, bf16[128,2560]{1,0:T(8,128)(2,1)S(1)} %convolution_convert_fusion.earlier_ref), custom_call_target="tpu_custom_call" | custom-call | flops 12582912000 | bytes 34734080 | tf_op jit(solution)/shard_map/ffn_grads/pallas_call | solution.py:680
  518.4 13.7 %collective-permute-done.28 = bf16[128,2560]{1,0:T(8,128)(2,1)} collective-permute-done((bf16[128,2560]{1,0:T(8,128)(2,1)}, bf16[128,2560]{1,0:T(8,128)(2,1)}, u32[]{:S(2)}, u32[]{:S(2)}) %collective-permute-start.28) | collective-permute-done | bytes 655392 | tf_op jit(solution)/shard_map/ppermute | solution.py:764
  537.8 26.1 %attend_back.1 = (bf16[1024,640]{1,0:T(8,128)(2,1)S(1)}, bf16[1024,640]{1,0:T(8,128)(2,1)S(1)}, bf16[1024,1152]{1,0:T(8,128)(2,1)}) custom-call(bf16[1024,1152]{1,0:T(8,128)(2,1)} %bitcast.283, bf16[640,768]{1,0:T(8,128)(2,1)S(1)} %bitcast.287, bf16[640,256]{1,0:T(8,128)(2,1)S(1)} %bitcast.290, bf16[1024,640]{1,0:T(8,128)(2,1)} %copy-done.12, ...), custom_call_target="tpu_custom_call" | custom-call | flops 5368709120 | bytes 9175040 | tf_op jit(solution)/shard_map/attend_back/pallas_call | solution.py:584
  579.6 9.8 %collective-permute-done.33 = bf16[128,1152]{1,0:T(8,128)(2,1)} collective-permute-done((bf16[128,1152]{1,0:T(8,128)(2,1)}, bf16[128,1152]{1,0:T(8,128)(2,1)}, u32[]{:S(2)}, u32[]{:S(2)}) %collective-permute-start.33) | collective-permute-done | bytes 294944 | tf_op jit(solution)/shard_map/ppermute | solution.py:764
  642.0 20.4 %all-to-all-start.2 = ((bf16[4,360,1024]{2,1,0:T(8,128)(2,1)}), bf16[4,360,1024]{2,1,0:T(8,128)(2,1)}, u32[]{:S(2)}, u32[]{:S(2)}) async-start(bf16[4,360,1024]{2,1,0:T(8,128)(2,1)} %fusion.13), calls=%async_computation.2 | async-start | bytes 5898240 | tf_op jit(solution)/shard_map/all_to_all | solution.py:717
  669.6 26.6 %collective-permute-done.37 = bf16[4,80,1152]{2,1,0:T(8,128)(2,1)S(1)} collective-permute-done((bf16[4,80,1152]{2,1,0:T(8,128)(2,1)S(1)}, bf16[4,80,1152]{2,1,0:T(8,128)(2,1)S(1)}, u32[]{:S(2)}, u32[]{:S(2)}) %collective-permute-start.37) | collective-permute-done | bytes 737312 | tf_op jit(solution)/shard_map/ppermute | solution.py:764
  696.2 15.5 %collective-permute-done.36 = bf16[4,80,1152]{2,1,0:T(8,128)(2,1)S(1)} collective-permute-done((bf16[4,80,1152]{2,1,0:T(8,128)(2,1)S(1)}, bf16[4,80,1152]{2,1,0:T(8,128)(2,1)S(1)}, u32[]{:S(2)}, u32[]{:S(2)}) %collective-permute-start.36) | collective-permute-done | bytes 737312 | tf_op jit(solution)/shard_map/ppermute | solution.py:764
  719.5 18.8 %all-to-all-done.2 = bf16[4,360,1024]{2,1,0:T(8,128)(2,1)} async-done(((bf16[4,360,1024]{2,1,0:T(8,128)(2,1)}), bf16[4,360,1024]{2,1,0:T(8,128)(2,1)}, u32[]{:S(2)}, u32[]{:S(2)}) %all-to-all-start.2) | async-done | bytes 2949152 | tf_op jit(solution)/shard_map/all_to_all | solution.py:717
  746.3 30.8 %collective-permute-done.42 = bf16[360,1024]{1,0:T(8,128)(2,1)S(1)} collective-permute-done((bf16[360,1024]{1,0:T(8,128)(2,1)S(1)}, bf16[360,1024]{1,0:T(8,128)(2,1)S(1)}, u32[]{:S(2)}, u32[]{:S(2)}) %collective-permute-start.42) | collective-permute-done | bytes 737312 | tf_op jit(solution)/shard_map/ppermute | solution.py:985
  (359 shorter events, 293.5 us)
Async XLA Ops:
  7.2 243.6 %all-gather.3.cloned.1.call-start = ((), (), s32[]{:S(2)}) async-start(), calls=%async_computation.4 | async-start | bytes 13516800 | tf_op jit(solution)/shard_map/all_gather | solution.py:891
  32.4 284.1 %all-gather.5.cloned.1.call-start = ((), (), s32[]{:S(2)}) async-start(), calls=%async_computation.5 | async-start | bytes 27648000 | tf_op jit(solution)/shard_map/all_gather | solution.py:896
  37.1 68.0 %collective-permute-start.3 = (bf16[4,80,1152]{2,1,0:T(8,128)(2,1)}, bf16[4,80,1152]{2,1,0:T(8,128)(2,1)}, u32[]{:S(2)}, u32[]{:S(2)}) collective-permute-start(bf16[4,80,1152]{2,1,0:T(8,128)(2,1)} %bitcast_dynamic-update-slice_fusion.30), channel_id=1, source_target_pairs={{0,2},{1,3},{2,0},{3,1},{4,6},{5,7},{6,4},{7,5},{8,10},{9,11},{10,... | collective-permute-start | bytes 2211848 | tf_op jit(solution)/shard_map/ppermute | solution.py:764
  37.2 69.1 %collective-permute-start.4 = (bf16[4,80,1152]{2,1,0:T(8,128)(2,1)}, bf16[4,80,1152]{2,1,0:T(8,128)(2,1)}, u32[]{:S(2)}, u32[]{:S(2)}) collective-permute-start(bf16[4,80,1152]{2,1,0:T(8,128)(2,1)} %bitcast_dynamic-update-slice_fusion.30), channel_id=1, source_target_pairs={{0,4},{1,5},{2,6},{3,7},{4,0},{5,1},{6,2},{7,3},{8,12},{9,13},{10,... | collective-permute-start | bytes 2211848 | tf_op jit(solution)/shard_map/ppermute | solution.py:764
  38.4 69.1 %collective-permute-start.5 = (bf16[4,80,1152]{2,1,0:T(8,128)(2,1)}, bf16[4,80,1152]{2,1,0:T(8,128)(2,1)}, u32[]{:S(2)}, u32[]{:S(2)}) collective-permute-start(bf16[4,80,1152]{2,1,0:T(8,128)(2,1)} %bitcast_dynamic-update-slice_fusion.30), channel_id=1, source_target_pairs={{0,6},{1,7},{2,4},{3,5},{4,2},{5,3},{6,0},{7,1},{8,14},{9,15},{10,... | collective-permute-start | bytes 2211848 | tf_op jit(solution)/shard_map/ppermute | solution.py:764
  60.6 41.6 %collective-permute-start.8 = (bf16[160,1024]{1,0:T(8,128)(2,1)S(1)}, bf16[160,1024]{1,0:T(8,128)(2,1)S(1)}, u32[]{:S(2)}, u32[]{:S(2)}) collective-permute-start(bf16[160,1024]{1,0:T(8,128)(2,1)S(1)} %get-tuple-element.54), channel_id=1, source_target_pairs={{0,16},{8,24},{16,0},{24,8},{1,17},{9,25},{17,1},{25,9},{2,18},{10... | collective-permute-start | bytes 983048 | tf_op jit(solution)/shard_map/ppermute | solution.py:82
  151.8 46.2 %collective-permute-start.16 = (bf16[128,2560]{1,0:T(8,128)(2,1)}, bf16[128,2560]{1,0:T(8,128)(2,1)S(1)}, u32[]{:S(2)}, u32[]{:S(2)}) collective-permute-start(bf16[128,2560]{1,0:T(8,128)(2,1)} %get-tuple-element.52), channel_id=1, source_target_pairs={{0,16},{8,24},{16,0},{24,8},{1,17},{9,25},{17,1},{25,9},{2,18},{10... | collective-permute-start | bytes 1966088 | tf_op jit(solution)/shard_map/ppermute | solution.py:82
  154.4 77.3 %collective-permute-start.17 = (bf16[128,2560]{1,0:T(8,128)(2,1)}, bf16[128,2560]{1,0:T(8,128)(2,1)}, u32[]{:S(2)}, u32[]{:S(2)}) collective-permute-start(bf16[128,2560]{1,0:T(8,128)(2,1)} %get-tuple-element.52), channel_id=1, source_target_pairs={{0,24},{8,0},{16,8},{24,16},{1,25},{9,1},{17,9},{25,17},{2,26},{10... | collective-permute-start | bytes 1966088 | tf_op jit(solution)/shard_map/ppermute | solution.py:82
  159.6 38.5 %collective-permute-start.14 = (bf16[4,128,1152]{2,1,0:T(8,128)(2,1)S(1)}, bf16[4,128,1152]{2,1,0:T(8,128)(2,1)S(1)}, u32[]{:S(2)}, u32[]{:S(2)}) collective-permute-start(bf16[4,128,1152]{2,1,0:T(8,128)(2,1)S(1)} %bitcast_dynamic-update-slice_fusion.26), channel_id=1, source_target_pairs={{0,1},{1,0},{2,3},{3,2},{4,5},{5,4},{6,7},{7,6},{8,9},{9,8},{10,11... | collective-permute-start | bytes 3538952 | tf_op jit(solution)/shard_map/ppermute | solution.py:713
  231.7 548.3 %reduce-scatter.2.cloned.1.call-start = ((), (), s32[]{:S(2)}) async-start(), calls=%async_computation.6 | async-start | bytes 27648000 | tf_op jit(solution)/shard_map/reduce_scatter | solution.py:930
  271.4 44.9 %collective-permute-start.19 = (bf16[128,2560]{1,0:T(8,128)(2,1)S(1)}, bf16[128,2560]{1,0:T(8,128)(2,1)S(1)}, u32[]{:S(2)}, u32[]{:S(2)}) collective-permute-start(bf16[128,2560]{1,0:T(8,128)(2,1)S(1)} %get-tuple-element.50), channel_id=1, source_target_pairs={{0,16},{8,24},{16,0},{24,8},{1,17},{9,25},{17,1},{25,9},{2,18},{10... | collective-permute-start | bytes 1966088 | tf_op jit(solution)/shard_map/ppermute | solution.py:82
  274.7 41.7 %collective-permute-start.20 = (bf16[128,2560]{1,0:T(8,128)(2,1)S(1)}, bf16[128,2560]{1,0:T(8,128)(2,1)S(1)}, u32[]{:S(2)}, u32[]{:S(2)}) collective-permute-start(bf16[128,2560]{1,0:T(8,128)(2,1)S(1)} %get-tuple-element.50), channel_id=1, source_target_pairs={{0,24},{8,0},{16,8},{24,16},{1,25},{9,1},{17,9},{25,17},{2,26},{10... | collective-permute-start | bytes 1966088 | tf_op jit(solution)/shard_map/ppermute | solution.py:82
  365.1 43.1 %collective-permute-start.25 = (bf16[128,2560]{1,0:T(8,128)(2,1)}, bf16[128,2560]{1,0:T(8,128)(2,1)}, u32[]{:S(2)}, u32[]{:S(2)}) collective-permute-start(bf16[128,2560]{1,0:T(8,128)(2,1)} %get-tuple-element.65), channel_id=1, source_target_pairs={{0,16},{8,24},{16,0},{24,8},{1,17},{9,25},{17,1},{25,9},{2,18},{10... | collective-permute-start | bytes 1966088 | tf_op jit(solution)/shard_map/ppermute | solution.py:82
  365.1 43.4 %collective-permute-start.24 = (bf16[128,2560]{1,0:T(8,128)(2,1)}, bf16[128,2560]{1,0:T(8,128)(2,1)}, u32[]{:S(2)}, u32[]{:S(2)}) collective-permute-start(bf16[128,2560]{1,0:T(8,128)(2,1)} %get-tuple-element.63), channel_id=1, source_target_pairs={{0,24},{8,0},{16,8},{24,16},{1,25},{9,1},{17,9},{25,17},{2,26},{10... | collective-permute-start | bytes 1966088 | tf_op jit(solution)/shard_map/ppermute | solution.py:82
  378.1 44.4 %collective-permute-start.23 = (bf16[128,2560]{1,0:T(8,128)(2,1)}, bf16[128,2560]{1,0:T(8,128)(2,1)}, u32[]{:S(2)}, u32[]{:S(2)}) collective-permute-start(bf16[128,2560]{1,0:T(8,128)(2,1)} %get-tuple-element.67), channel_id=1, source_target_pairs={{0,8},{8,16},{16,24},{24,0},{1,9},{9,17},{17,25},{25,1},{2,10},{10... | collective-permute-start | bytes 1966088 | tf_op jit(solution)/shard_map/ppermute | solution.py:82
  378.1 84.0 %collective-permute-start.22 = (bf16[128,2560]{1,0:T(8,128)(2,1)}, bf16[128,2560]{1,0:T(8,128)(2,1)}, u32[]{:S(2)}, u32[]{:S(2)}) collective-permute-start(bf16[128,2560]{1,0:T(8,128)(2,1)} %get-tuple-element.68), channel_id=1, source_target_pairs={{0,16},{8,24},{16,0},{24,8},{1,17},{9,25},{17,1},{25,9},{2,18},{10... | collective-permute-start | bytes 1966088 | tf_op jit(solution)/shard_map/ppermute | solution.py:82
  381.5 80.6 %collective-permute-start.21 = (bf16[128,2560]{1,0:T(8,128)(2,1)}, bf16[128,2560]{1,0:T(8,128)(2,1)}, u32[]{:S(2)}, u32[]{:S(2)}) collective-permute-start(bf16[128,2560]{1,0:T(8,128)(2,1)} %get-tuple-element.66), channel_id=1, source_target_pairs={{0,24},{8,0},{16,8},{24,16},{1,25},{9,1},{17,9},{25,17},{2,26},{10... | collective-permute-start | bytes 1966088 | tf_op jit(solution)/shard_map/ppermute | solution.py:82
  499.7 34.6 %collective-permute-start.29 = (bf16[128,2560]{1,0:T(8,128)(2,1)}, bf16[128,2560]{1,0:T(8,128)(2,1)}, u32[]{:S(2)}, u32[]{:S(2)}) collective-permute-start(bf16[128,2560]{1,0:T(8,128)(2,1)} %get-tuple-element.47), channel_id=1, source_target_pairs={{0,6},{1,7},{2,4},{3,5},{4,2},{5,3},{6,0},{7,1},{8,14},{9,15},{10,... | collective-permute-start | bytes 1966088 | tf_op jit(solution)/shard_map/ppermute | solution.py:764
  503.5 34.3 %all-to-all-start.1 = ((bf16[8,128,384]{2,1,0:T(8,128)(2,1)}), bf16[8,128,384]{2,1,0:T(8,128)(2,1)S(1)}, u32[]{:S(2)}, u32[]{:S(2)}) async-start(bf16[8,128,384]{2,1,0:T(8,128)(2,1)} %pad.40), calls=%async_computation.1 | async-start | bytes 1572864 | tf_op jit(solution)/shard_map/all_to_all | solution.py:717
  565.8 64.6 %collective-permute-start.41 = (bf16[4,128,2560]{2,1,0:T(8,128)(2,1)}, bf16[4,128,2560]{2,1,0:T(8,128)(2,1)}, u32[]{:S(2)}, u32[]{:S(2)}) collective-permute-start(bf16[4,128,2560]{2,1,0:T(8,128)(2,1)} %bitcast_dynamic-update-slice_fusion.10.second_ref), channel_id=1, source_target_pairs={{0,1},{1,0},{2,3},{3,2},{4,5},{5,4},{6,7},{7,6},{8,9},{9,8},{10,11... | collective-permute-start | bytes 7864328 | tf_op jit(solution)/shard_map/ppermute | solution.py:713
  642.0 96.3 %all-to-all-start.2 = ((bf16[4,360,1024]{2,1,0:T(8,128)(2,1)}), bf16[4,360,1024]{2,1,0:T(8,128)(2,1)}, u32[]{:S(2)}, u32[]{:S(2)}) async-start(bf16[4,360,1024]{2,1,0:T(8,128)(2,1)} %fusion.13), calls=%async_computation.2 | async-start | bytes 5898240 | tf_op jit(solution)/shard_map/all_to_all | solution.py:717
  667.2 44.5 %collective-permute-start.36 = (bf16[4,80,1152]{2,1,0:T(8,128)(2,1)S(1)}, bf16[4,80,1152]{2,1,0:T(8,128)(2,1)S(1)}, u32[]{:S(2)}, u32[]{:S(2)}) collective-permute-start(bf16[4,80,1152]{2,1,0:T(8,128)(2,1)S(1)} %get-tuple-element.62), channel_id=1, source_target_pairs={{0,4},{1,5},{2,6},{3,7},{4,0},{5,1},{6,2},{7,3},{8,12},{9,13},{10,... | collective-permute-start | bytes 2211848 | tf_op jit(solution)/shard_map/ppermute | solution.py:764
  668.3 43.3 %collective-permute-start.35 = (bf16[4,80,1152]{2,1,0:T(8,128)(2,1)S(1)}, bf16[4,80,1152]{2,1,0:T(8,128)(2,1)S(1)}, u32[]{:S(2)}, u32[]{:S(2)}) collective-permute-start(bf16[4,80,1152]{2,1,0:T(8,128)(2,1)S(1)} %get-tuple-element.60), channel_id=1, source_target_pairs={{0,2},{1,3},{2,0},{3,1},{4,6},{5,7},{6,4},{7,5},{8,10},{9,11},{10,... | collective-permute-start | bytes 2211848 | tf_op jit(solution)/shard_map/ppermute | solution.py:764
  740.7 36.4 %collective-permute-start.42 = (bf16[360,1024]{1,0:T(8,128)(2,1)S(1)}, bf16[360,1024]{1,0:T(8,128)(2,1)S(1)}, u32[]{:S(2)}, u32[]{:S(2)}) collective-permute-start(bf16[360,1024]{1,0:T(8,128)(2,1)S(1)} %reduce_sum.132), channel_id=1, source_target_pairs={{0,0},{1,12},{2,8},{3,20},{4,16},{5,28},{6,24},{7,4},{8,1},{9,13},... | collective-permute-start | bytes 2211848 | tf_op jit(solution)/shard_map/ppermute | solution.py:985
  (82 other events, 1379.5 us)
Sparse Core Ops, SparseCore 0:
  32.5 128.1 all-gather.2
  162.6 129.2 all-gather.4
  498.5 209.8 reduce-scatter.1

commit v5 on v4

--- a/solution.py
+++ b/solution.py
@@ -511,7 +511,7 @@
 
 def attend_back_kernel(
     tokens_ref, query_up_ref, pair_up_ref, query_ref, pairs_ref, log_ref, grad_ref,
-    first_ref, second_ref,
+    earlier_ref,
     grad_query_ref, grad_pairs_ref, grad_tokens_ref,
     keys_ref, cos_ref, left_ref, right_ref, grad_ready_ref, grad_keys_ref, grad_values_ref,
     sum_ref,
@@ -572,12 +572,11 @@
         grad_tokens_ref[...] = sum_ref[...].astype(BF16)
 
 
-def attend_back(tokens, query_up, pair_up, query, pairs, logs, grad, first, second):
+def attend_back(tokens, query_up, pair_up, query, pairs, logs, grad, earlier):
     length, width = tokens.shape
     lanes = query.shape[1]
     heads = lanes // HEAD_LANES
     whole = pl.BlockSpec(memory_space=pltpu.VMEM)
-    anywhere = pl.BlockSpec(memory_space=pl.ANY)
     own = pl.BlockSpec((length, HEAD_LANES), lambda h: (0, h))
     table = pltpu.VMEM((length, HEAD_LANES), F32)
     turned = pltpu.VMEM((HEAD_LANES, length), F32)
@@ -592,8 +591,7 @@
             own,
             own,
             pl.BlockSpec((length, HEAD_LANES), lambda h: (0, h // 2)),
-            anywhere,
-            anywhere,
+            pl.BlockSpec(memory_space=pl.ANY),
         ],
         out_specs=[own, own, pl.BlockSpec((length, width), lambda h: (0, 0))],
         out_shape=[
@@ -617,7 +615,7 @@
             transcendentals=length * length * heads,
         ),
         name="attend_back",
-    )(tokens, query_up, pair_up, query, pairs, logs, grad, first, second)
+    )(tokens, query_up, pair_up, query, pairs, logs, grad, earlier)
 
 
 def ffn_kernel(weights_ref, rows_ref, grads_ref, both_ref, act_ref):
@@ -663,7 +661,7 @@
     )(weights, rows, grads)
 
 
-def ffn_grads_kernel(both_ref, act_ref, rows_ref, grads_ref, earlier_ref, out_ref):
+def ffn_grads_kernel(both_ref, act_ref, rows_ref, grads_ref, out_ref):
     hidden = act_ref.shape[1]
     parts = ((both_ref[0, 0], rows_ref), (both_ref[1, 0], rows_ref), (act_ref[0], grads_ref))
     for place, (left, right) in enumerate(parts):
@@ -672,7 +670,7 @@
         ).astype(BF16)
 
 
-def ffn_grads(grad_both, activated, rows, grads, earlier):
+def ffn_grads(grad_both, activated, rows, grads):
     steps, hidden, count = activated.shape
     width = rows.shape[1]
     whole = pl.BlockSpec(memory_space=pltpu.VMEM)
@@ -685,7 +683,6 @@
             own,
             whole,
             whole,
-            pl.BlockSpec(memory_space=pl.ANY),
         ],
         out_specs=pl.BlockSpec((1, 3 * hidden, width), lambda i: (i, 0, 0)),
         out_shape=jax.ShapeDtypeStruct((steps, 3 * hidden, width), BF16),
@@ -696,12 +693,12 @@
             transcendentals=0,
         ),
         name="ffn_grads",
-    )(grad_both, activated, rows, grads, earlier)
+    )(grad_both, activated, rows, grads)
 
 
 def done(value):
-    first = value[(0,) * value.ndim].astype(F32)
-    return (first != first).astype(jnp.int32)
+    last = value[(-1,) * value.ndim].astype(F32)
+    return (last != last).astype(jnp.int32)
 
 
 def hold(value, token):
@@ -786,10 +783,11 @@
     def scatter_seq(mine, theirs, token=0):
         half = mine.astype(F32) + flip(theirs.astype(BF16)).astype(F32)
         half = half.astype(BF16)
+        core_done = done(half)
         total = choose(half, chip, 0).astype(F32)
         for m in range(1, chips):
             total = total + across(choose(half, (chip ^ m) + token, 0), m).astype(F32)
-        return total
+        return total, core_done
 
     def gather_z(value):
         whole = jnp.zeros((dp_count,) + value.shape, value.dtype)
@@ -803,6 +801,12 @@
         for k in range(1, dp_count):
             block = choose(blocks, (place - k) % dp_count, 0)
             total = total + shift(block, "dp", dp_count, -k).astype(F32)
+        return total
+
+    def send_home(parts):
+        total = parts[0].astype(F32)
+        for k in range(1, dp_count):
+            total = total + shift(parts[k], "dp", dp_count, -k).astype(F32)
         return total
 
     def by_core(value, token=0):
@@ -843,7 +847,7 @@
         1,
     )
     up_moved = lax.ppermute(up_packed, both, to_group)
-    up_group = gather_z(hold(up_moved, done(down_plane)))
+    up_group = exchange(repeat(hold(up_moved, done(down_plane)), dp_count), "dp")
     down_full = gather_seq(down_plane, done(up_group), 1).reshape(width, padded_width)
     gains = down_full[:, down_width : down_width + 4].T.astype(F32)
     attn_gain_full = gains[0]
@@ -888,64 +892,72 @@
     )
     tail_start = query_rank + KV_RANK
     token_all = gather_seq(token_message).reshape(length, token_message.shape[1])
-    proj_full = lax.all_gather(hold(output_proj, done(down_plane)), both, axis=0, tiled=True)
+    proj_moved = lax.ppermute(output_proj, both, to_group)
+    proj_group = exchange(repeat(hold(proj_moved, done(token_message)), dp_count), "dp")
+    proj_group = proj_group.reshape(-1, width)
+    proj_rows = jnp.pad(
+        proj_group, ((0, (heads + 1) // 2 * HEAD_LANES - proj_group.shape[0]), (0, 0))
+    )
     grad_out = cotangent.astype(F32)
     grad_two = (RESIDUAL_SCALE * grad_out).astype(BF16)
-    grad_rows = gather_z(hold(grad_two, done(token_message))).reshape(-1, width)
+    grad_all = exchange(repeat(hold(grad_two, done(token_all)), dp_count), "dp")
+    grad_rows = jnp.concatenate(
+        [choose(grad_all, (place - k) % dp_count, 0) for k in range(dp_count)]
+    )
     ffn_own = hold(jnp.stack([ffn_gate.T, ffn_up.T, ffn_down]), done(down_full))
     ffn_full = lax.all_gather(ffn_own, "seq", axis=1, tiled=True)
 
     query, pairs, attended, logs = attend(token_all, query_up_padded, latent_up_group)
     head_width = heads * VDIM
-    group_place = [group_of.index(g) for g in range(seq_count)]
-    attended_own = exchange(attended.reshape(seq_count, tokens, -1), "seq")[:, :, :head_width]
-    attended_own = jnp.concatenate([attended_own[s] for s in group_place], 1)
-    branch = jnp.dot(attended_own, proj_full, preferred_element_type=F32)
+    attended_mine, attended_theirs = by_core(attended)
+    branch, _ = scatter_seq(
+        dot("mtk,kd->mtd", attended_mine, proj_rows),
+        dot("mtk,kd->mtd", attended_theirs, proj_rows),
+    )
     middle = inputs + RESIDUAL_SCALE * branch
     normal_two, inverse_two = norm_parts(middle)
-    normed_two = hold((normal_two * ffn_gain_full).astype(BF16), done(grad_rows))
-
-    normed_rows = gather_z(normed_two).reshape(-1, width)
+    normed_two = hold((normal_two * ffn_gain_full).astype(BF16), done(grad_all))
+
+    normed_rows = jnp.concatenate(gather_dp(normed_two, dp_count))
+    proj_full = lax.all_gather(hold(proj_group, done(normed_two)), "seq", axis=0, tiled=True)
     own_hidden = ffn_down.shape[0]
     count = dp_count * tokens
     grad_both, activated = ffn_hidden(ffn_full, normed_rows, grad_rows)
     grad_part = dot("gft,gfd->td", grad_both, ffn_full[:2])
-    grad_parts = grad_part.astype(BF16).reshape(dp_count, tokens, width)
-    returned = [
-        shift(choose(grad_parts, (place - k) % dp_count, 0), "dp", dp_count, -k)
-        for k in range(1, dp_count)
-    ]
-    grad_normed_two = choose(grad_parts, place, 0).astype(F32)
-    for piece in returned:
-        grad_normed_two = grad_normed_two + piece.astype(F32)
-    out_part = dot("ft,fd->td", activated, ffn_full[2]).reshape(dp_count, tokens, width)
-    layer_output = (middle + RESIDUAL_SCALE * scatter_z(out_part)).astype(BF16)
-
-    grad_middle_norm, grad_ffn_gain_part = norm_back(
-        grad_normed_two, normal_two, inverse_two, ffn_gain_full
-    )
-    grad_middle = grad_out + grad_middle_norm
-    grad_branch = (RESIDUAL_SCALE * grad_middle).astype(BF16)
-    grad_attended = dot("td,kd->tk", grad_branch, proj_full).astype(BF16)
+    grad_normed_two = send_home(jnp.split(grad_part.astype(BF16), dp_count))
+    out_part = dot("ft,fd->td", activated, ffn_full[2]).astype(BF16)
     ffn_sums = lax.psum_scatter(
         ffn_grads(
             grad_both.reshape(2, seq_count, own_hidden, count),
             activated.reshape(seq_count, own_hidden, count),
             normed_rows,
             grad_rows,
-            grad_attended,
         ),
         "seq",
         scatter_dimension=0,
     ).astype(F32)
-    grad_blocks = jnp.stack(
-        [grad_attended[:, g * head_width : (g + 1) * head_width] for g in group_of]
-    )
+
+    grad_middle_norm, grad_ffn_gain_part = norm_back(
+        grad_normed_two, normal_two, inverse_two, ffn_gain_full
+    )
+    grad_middle = grad_out + grad_middle_norm
+    grad_branch = (RESIDUAL_SCALE * grad_middle).astype(BF16)
+    grad_attended = dot("td,kd->tk", grad_branch, proj_full).astype(BF16)
+    grad_blocks = grad_attended.reshape(tokens, seq_count, head_width).transpose(1, 0, 2)
     grad_blocks = jnp.pad(
         grad_blocks, ((0, 0), (0, 0), (0, attended.shape[1] - head_width))
     )
-    grad_heads = exchange(grad_blocks, "seq").reshape(length, -1)
-    branch_plane = gather_plane(grad_branch)
+    grad_blocks = grad_blocks.reshape(chips, 2, tokens, -1)
+    arrived = flip(choose(grad_blocks, 1 - core, 1))
+    by_chip = jnp.zeros((chips, 2) + grad_blocks.shape[2:], BF16)
+    by_chip = place_in(by_chip, choose(grad_blocks, core, 1), core, 1)
+    by_chip = place_in(by_chip, arrived, 1 - core, 1)
+    grad_heads = jnp.zeros_like(by_chip)
+    for m in range(chips):
+        piece = choose(by_chip, chip ^ m, 0)
+        grad_heads = place_in(grad_heads, across(piece, m) if m else piece, chip ^ m, 0)
+    grad_heads = grad_heads.reshape(length, -1)
+    branch_plane = gather_plane(hold(grad_branch, done(grad_heads)))
     grad_projected, grad_pairs, grad_tokens = attend_back(
         token_all,
         query_up_padded,
@@ -954,10 +966,16 @@
         pairs,
         logs,
         grad_heads,
-        layer_output,
-        branch_plane,
-    )
-    grad_own = scatter_seq(*by_core(grad_tokens))
+        out_part,
+    )
+    grad_own, _ = scatter_seq(*by_core(grad_tokens), done(branch_plane))
+    out_slots = hold(out_part, done(grad_heads)).reshape(dp_count, tokens, width)
+    out_blocks = jnp.stack(
+        [choose(out_slots, (place - j) % dp_count, 0) for j in range(dp_count)]
+    )
+    out_all = exchange(out_blocks, "dp")
+    layer_output = (middle + RESIDUAL_SCALE * jnp.sum(out_all.astype(F32), 0)).astype(BF16)
+    grad_own = hold(grad_own, done(out_all))
 
     query_up_grads = dot("tk,tq->kq", grad_projected, token_all[:, :query_rank]).astype(BF16)
     query_up_grads = query_up_grads.reshape(heads, HEAD_LANES, query_rank)[:, : NOPE + ROPE]
@@ -981,12 +999,6 @@
     group_grads = jnp.concatenate(
         [up_grads, proj_grads.reshape(dp_count, -1, up_grads.shape[2])], 1
     )
-    group_sums = jnp.sum(exchange(group_grads, "dp").astype(F32), 0)
-    group_sums = lax.ppermute(group_sums.astype(BF16), both, to_owner).astype(F32)
-    sum_query_up = group_sums[: query_up.shape[1], :query_rank].T
-    sum_latent_up = group_sums[: latent_up.shape[1], query_rank:].T
-    sum_out = group_sums[up_rows:].reshape(-1, width)
-
     grad_query_latent, grad_query_gain_part = norm_back(
         grad_own[:, :query_rank], normal_query, inverse_query, query_gain_full
     )
@@ -1031,11 +1043,16 @@
     )
     down_sums = down_sums.astype(BF16).reshape(dp_count, chips, 2, own_rows, padded_width)
     down_sums = down_sums.transpose(1, 2, 0, 3, 4)
-    sum_down = scatter_z(
-        scatter_seq(
-            choose(down_sums, core, 1), choose(down_sums, 1 - core + done(group_grads), 1)
-        )
-    )
+    sum_down, core_done = scatter_seq(
+        choose(down_sums, core, 1),
+        choose(down_sums, 1 - core + done(group_grads), 1),
+    )
+    sum_down = scatter_z(sum_down)
+    group_sums = jnp.sum(exchange(hold(group_grads, core_done), "dp").astype(F32), 0)
+    group_sums = lax.ppermute(group_sums.astype(BF16), both, to_owner).astype(F32)
+    sum_query_up = group_sums[: query_up.shape[1], :query_rank].T
+    sum_latent_up = group_sums[: latent_up.shape[1], query_rank:].T
+    sum_out = group_sums[up_rows:].reshape(-1, width)
     sum_gains = sum_down[:, down_width : down_width + 4].T
     return (
         layer_output,

time: 802 us -> 753 us (0.939)
  waiting for transfers between devices: 373 us -> 325 us
  starting transfers between devices: 130 us -> 110 us
  local copies, waits for them, and re-layouts: 85.8 us -> 94.5 us
    ppermute x21 -> x12, waiting for transfers between devices: 202 us -> 95.5 us  [shift(): lax.ppermute(value, axis, [(i, (i + step) % count) for i in range(count)])]
    ppermute x15 -> x21, waiting for transfers between devices: 88.9 us -> 162 us  [across(): lax.ppermute(value, 'seq', [(i, i ^ 2 * steps) for i in range(seq_count)])]
    ppermute x21 -> x12, starting transfers between devices: 69.8 us -> 22.3 us  [shift(): lax.ppermute(value, axis, [(i, (i + step) % count) for i in range(count)])]
    all_to_all x3 -> x5, starting transfers between devices: 28.3 us -> 53.5 us  [exchange(): lax.all_to_all(blocks, axis, split_axis=0, concat_axis=0, axis_index_grou...]
    dot_general x8 -> x10, matrix products: 46.5 us -> 55.6 us  [dot(): return jnp.einsum(spec, left, right, preferred_element_type=F32)]
    ppermute x1, waiting for transfers between devices: 10 us -> 1.98 us  [per_device_heads(): up_moved = lax.ppermute(up_packed, both, to_group)]
    ppermute x15 -> x21, starting transfers between devices: 17.7 us -> 25 us  [across(): lax.ppermute(value, 'seq', [(i, i ^ 2 * steps) for i in range(seq_count)])]
    all_to_all x3 -> x5, waiting for transfers between devices: 34 us -> 26.8 us  [exchange(): lax.all_to_all(blocks, axis, split_axis=0, concat_axis=0, axis_index_grou...]
  transfers between devices with their start and end apart: 49 -> 51, of which waited for: 27 -> 24; matrix products, arithmetic and copies ran while one was open for 15% -> 21% of each run, Pallas kernels for 6% -> 12%
where the time goes in v5:
time: 753 us; the launch traced here: 743 us
  waiting for transfers between devices  325 us (43%)
  starting transfers between devices  110 us (15%)
  local copies, waits for them, and re-layouts  94.5 us (13%)
  Pallas kernels  86 us (11%)
  matrix products  61.5 us (8%)
  other arithmetic  35.6 us (5%)
  between operations  30.1 us (4%)
    ppermute x21, waiting for transfers between devices, across(): lax.ppermute(value, 'seq', [(i, i ^ 2 * steps) for i in range(seq_count)])  162 us
    ppermute x12, waiting for transfers between devices, shift(): lax.ppermute(value, axis, [(i, (i + step) % count) for i in range(count)])  95.5 us
    dot_general x10, matrix products, dot(): return jnp.einsum(spec, left, right, preferred_element_type=F32)  55.6 us
    all_to_all x5, starting transfers between devices, exchange(): lax.all_to_all(blocks, axis, split_axis=0, concat_axis=0, axis_index_grou...  53.5 us
    ppermute x1, waiting for transfers between devices, per_device_heads(): lax.ppermute(group_sums.astype(BF16), both, to_owner).astype(F32)  30.9 us
    all_to_all x5, waiting for transfers between devices, exchange(): lax.all_to_all(blocks, axis, split_axis=0, concat_axis=0, axis_index_grou...  26.8 us
    pallas_call x1, Pallas kernels, attend_back(): pl.pallas_call(attend_back_kernel, grid=(heads,), in_specs=[whole, pl.Blo...  25.1 us
    ppermute x21, starting transfers between devices, across(): lax.ppermute(value, 'seq', [(i, i ^ 2 * steps) for i in range(seq_count)])  25 us
  transfers between devices with their start and end apart: 51, of which 24 were waited for; matrix products, arithmetic and copies ran while one was open for 21% of the time, Pallas kernels for 12%

profile of v5, /device:TPU:2, one launch (start us, length us, event | category | flops | bytes accessed | tf_op | source)
XLA Modules:
  0.0 743.2 jit_solution(13999127482187288667)
XLA Ops:
  34.8 14.0 %all-to-all-start = ((bf16[4,160,1024]{2,1,0:T(8,128)(2,1)}), bf16[4,160,1024]{2,1,0:T(8,128)(2,1)}, u32[]{:S(2)}, u32[]{:S(2)}) async-start(bf16[4,160,1024]{2,1,0:T(8,128)(2,1)} %broadcast_in_dim.189), calls=%async_computation | async-start | bytes 2621440 | tf_op jit(solution)/shard_map/all_to_all | solution.py:714
  54.7 11.5 %collective-permute-done.3 = bf16[4,80,1152]{2,1,0:T(8,128)(2,1)} collective-permute-done((bf16[4,80,1152]{2,1,0:T(8,128)(2,1)}, bf16[4,80,1152]{2,1,0:T(8,128)(2,1)}, u32[]{:S(2)}, u32[]{:S(2)}) %collective-permute-start.3) | collective-permute-done | bytes 737312 | tf_op jit(solution)/shard_map/ppermute | solution.py:761
  67.4 19.1 %collective-permute-done.4 = bf16[4,80,1152]{2,1,0:T(8,128)(2,1)S(1)} collective-permute-done((bf16[4,80,1152]{2,1,0:T(8,128)(2,1)}, bf16[4,80,1152]{2,1,0:T(8,128)(2,1)S(1)}, u32[]{:S(2)}, u32[]{:S(2)}) %collective-permute-start.4) | collective-permute-done | bytes 737312 | tf_op jit(solution)/shard_map/ppermute | solution.py:761
  122.3 12.4 %all-to-all-start.1 = ((bf16[4,80,2560]{2,1,0:T(8,128)(2,1)}), bf16[4,80,2560]{2,1,0:T(8,128)(2,1)}, u32[]{:S(2)}, u32[]{:S(2)}) async-start(bf16[4,80,2560]{2,1,0:T(8,128)(2,1)} %broadcast_in_dim.199), calls=%async_computation.1 | async-start | bytes 3276800 | tf_op jit(solution)/shard_map/all_to_all | solution.py:714
  138.1 19.0 %collective-permute-done.9 = bf16[128,1152]{0,1:T(8,128)(2,1)S(1)} collective-permute-done((bf16[128,1152]{0,1:T(8,128)(2,1)S(1)}, bf16[128,1152]{0,1:T(8,128)(2,1)S(1)}, u32[]{:S(2)}, u32[]{:S(2)}) %collective-permute-start.9) | collective-permute-done | bytes 294944 | tf_op jit(solution)/shard_map/ppermute | solution.py:761
  162.3 23.8 %attend.1 = (bf16[1024,640]{1,0:T(8,128)(2,1)S(1)}, bf16[1024,640]{1,0:T(8,128)(2,1)S(1)}, bf16[1024,384]{1,0:T(8,128)(2,1)S(1)}, f32[1024,640]{1,0:T(8,128)S(1)}) custom-call(bf16[1024,1152]{1,0:T(8,128)(2,1)S(1)} %bitcast.229, bf16[640,768]{1,0:T(8,128)(2,1)S(1)} %bitcast.233, bf16[640,256]{1,0:T(8,128)(2,1)S(1)} %bitcast.237), custom_call_target="tpu_custom_call" | custom-call | flops 2013265920 | bytes 7864320 | tf_op jit(solution)/shard_map/attend/pallas_call | solution.py:485
  211.1 29.0 %collective-permute-done.16 = bf16[128,2560]{1,0:T(8,128)(2,1)S(1)} collective-permute-done((bf16[128,2560]{1,0:T(8,128)(2,1)S(1)}, bf16[128,2560]{1,0:T(8,128)(2,1)S(1)}, u32[]{:S(2)}, u32[]{:S(2)}) %collective-permute-start.16) | collective-permute-done | bytes 655392 | tf_op jit(solution)/shard_map/ppermute | solution.py:761
  240.1 13.9 %collective-permute-done.15 = bf16[128,2560]{1,0:T(8,128)(2,1)S(1)} collective-permute-done((bf16[128,2560]{1,0:T(8,128)(2,1)S(1)}, bf16[128,2560]{1,0:T(8,128)(2,1)S(1)}, u32[]{:S(2)}, u32[]{:S(2)}) %collective-permute-start.15) | collective-permute-done | bytes 655392 | tf_op jit(solution)/shard_map/ppermute | solution.py:761
  254.0 12.7 %collective-permute-done.14 = bf16[128,2560]{1,0:T(8,128)(2,1)S(1)} collective-permute-done((bf16[128,2560]{1,0:T(8,128)(2,1)S(1)}, bf16[128,2560]{1,0:T(8,128)(2,1)S(1)}, u32[]{:S(2)}, u32[]{:S(2)}) %collective-permute-start.14) | collective-permute-done | bytes 655392 | tf_op jit(solution)/shard_map/ppermute | solution.py:761
  283.7 10.2 %collective-permute-done.19 = bf16[128,2560]{1,0:T(8,128)(2,1)S(1)} collective-permute-done((bf16[128,2560]{1,0:T(8,128)(2,1)S(1)}, bf16[128,2560]{1,0:T(8,128)(2,1)S(1)}, u32[]{:S(2)}, u32[]{:S(2)}) %collective-permute-start.19) | collective-permute-done | bytes 655392 | tf_op jit(solution)/shard_map/ppermute | solution.py:82
  293.9 40.4 %collective-permute-done.18 = bf16[128,2560]{1,0:T(8,128)(2,1)S(1)} collective-permute-done((bf16[128,2560]{1,0:T(8,128)(2,1)S(1)}, bf16[128,2560]{1,0:T(8,128)(2,1)S(1)}, u32[]{:S(2)}, u32[]{:S(2)}) %collective-permute-start.18) | collective-permute-done | bytes 655392 | tf_op jit(solution)/shard_map/ppermute | solution.py:82
  334.6 18.7 %ffn_hidden.1 = (bf16[2,1600,512]{2,1,0:T(8,128)(2,1)}, bf16[1600,512]{1,0:T(8,128)(2,1)S(1)}) custom-call(bf16[3,1600,2560]{2,1,0:T(8,128)(2,1)} %all-gather.3.cloned.1.call-done.weights_ref, bf16[512,2560]{1,0:T(8,128)(2,1)S(1)} %pad_maximum_fusion.rows_ref, bf16[512,2560]{1,0:T(8,128)(2,1)} %pad_maximum_fusion.1.grads_ref), custom_call_target="tpu_custom_call" | custom-call | flops 12582912000 | bytes 34734080 | tf_op jit(solution)/shard_map/ffn_hidden/pallas_call | solution.py:645
  353.3 18.4 %ffn_grads.1 = bf16[8,600,2560]{2,1,0:T(8,128)(2,1)} custom-call(bf16[2,8,200,512]{3,2,1,0:T(8,128)(2,1)} %bitcast.272, bf16[8,200,512]{2,1,0:T(8,128)(2,1)S(1)} %bitcast.239, bf16[512,2560]{1,0:T(8,128)(2,1)S(1)} %pad_maximum_fusion.rows_ref, bf16[512,2560]{1,0:T(8,128)(2,1)} %pad_maximum_fusion.1.grads_ref), custom_call_target="tpu_custom_call" | custom-call | flops 12582912000 | bytes 34734080 | tf_op jit(solution)/shard_map/ffn_grads/pallas_call | solution.py:678
  372.9 13.6 %bitcast_convert_fusion = bf16[512,2560]{1,0:T(8,128)(2,1)S(1)} fusion(bf16[2,1600,512]{2,1,0:T(8,128)(2,1)} %get-tuple-element.24, bf16[3,1600,2560]{2,1,0:T(8,128)(2,1)} %all-gather.3.cloned.1.call-done.weights_ref), kind=kOutput, calls=%fused_computation.13 | convolution fusion | flops 8389918720 | bytes 22282240 | tf_op jit(solution)/shard_map/gft,gfd->td/dot_general | solution.py:78
  392.5 13.8 %collective-permute-done.22 = bf16[128,2560]{1,0:T(8,128)(2,1)S(1)} collective-permute-done((bf16[128,2560]{1,0:T(8,128)(2,1)S(1)}, bf16[128,2560]{1,0:T(8,128)(2,1)S(1)}, u32[]{:S(2)}, u32[]{:S(2)}) %collective-permute-start.22) | collective-permute-done | bytes 655392 | tf_op jit(solution)/shard_map/ppermute | solution.py:82
  406.3 25.4 %collective-permute-done.21 = bf16[128,2560]{1,0:T(8,128)(2,1)S(1)} collective-permute-done((bf16[128,2560]{1,0:T(8,128)(2,1)S(1)}, bf16[128,2560]{1,0:T(8,128)(2,1)S(1)}, u32[]{:S(2)}, u32[]{:S(2)}) %collective-permute-start.21) | collective-permute-done | bytes 655392 | tf_op jit(solution)/shard_map/ppermute | solution.py:82
  433.6 10.0 %convolution_convert_fusion.1 = bf16[128,2560]{1,0:T(8,128)(2,1)S(1)} fusion(bf16[2560,2560]{1,0:T(8,128)(2,1)} %all-gather.5.cloned.1.call-done, f32[128,2560]{1,0:T(8,128)S(1)} %convert_add_fusion.2), kind=kOutput, calls=%fused_computation.18 | convolution fusion | flops 1678704640 | bytes 15073280 | tf_op jit(solution)/shard_map/td,kd->tk/dot_general | solution.py:78
  477.1 10.0 %broadcast_select_fusion = (bf16[512,2560]{1,0:T(8,128)(2,1)S(1)}, bf16[512,2560]{1,0:T(8,128)(2,1)}) fusion(pred[]{:T(512)} %bitcast.71, bf16[1600,512]{1,0:T(8,128)(2,1)S(1)} %copy-done.5, bf16[3,1600,2560]{2,1,0:T(8,128)(2,1)} %all-gather.3.cloned.1.call-done.weights_ref), kind=kOutput, calls=%fused_computation.32 | convolution fusion | flops 4196925440 | bytes 15073792 | tf_op jit(solution)/shard_map/ft,fd->td/dot_general | solution.py:78
  489.1 17.8 %all-to-all-start.3 = ((bf16[4,128,2560]{2,1,0:T(8,128)(2,1)}), bf16[4,128,2560]{2,1,0:T(8,128)(2,1)}, u32[]{:S(2)}, u32[]{:S(2)}) async-start(bf16[4,128,2560]{2,1,0:T(8,128)(2,1)} %pad_maximum_fusion.2), calls=%async_computation.3 | async-start | bytes 5242880 | tf_op jit(solution)/shard_map/all_to_all | solution.py:714
  522.4 25.1 %attend_back.1 = (bf16[1024,640]{1,0:T(8,128)(2,1)S(1)}, bf16[1024,640]{1,0:T(8,128)(2,1)S(1)}, bf16[1024,1152]{1,0:T(8,128)(2,1)}) custom-call(bf16[1024,1152]{1,0:T(8,128)(2,1)} %bitcast.230, bf16[640,768]{1,0:T(8,128)(2,1)S(1)} %bitcast.234, bf16[640,256]{1,0:T(8,128)(2,1)S(1)} %bitcast.238, bf16[1024,640]{1,0:T(8,128)(2,1)S(1)} %copy-done.12, ...), custom_call_target="tpu_custom_call" | custom-call | flops 5368709120 | bytes 9175040 | tf_op jit(solution)/shard_map/attend_back/pallas_call | solution.py:583
  621.1 14.8 %collective-permute-done.38 = bf16[4,80,1152]{2,1,0:T(8,128)(2,1)} collective-permute-done((bf16[4,80,1152]{2,1,0:T(8,128)(2,1)}, bf16[4,80,1152]{2,1,0:T(8,128)(2,1)}, u32[]{:S(2)}, u32[]{:S(2)}) %collective-permute-start.38) | collective-permute-done | bytes 737312 | tf_op jit(solution)/shard_map/ppermute | solution.py:761
  636.0 14.6 %collective-permute-done.37 = bf16[4,80,1152]{2,1,0:T(8,128)(2,1)} collective-permute-done((bf16[4,80,1152]{2,1,0:T(8,128)(2,1)}, bf16[4,80,1152]{2,1,0:T(8,128)(2,1)}, u32[]{:S(2)}, u32[]{:S(2)}) %collective-permute-start.37) | collective-permute-done | bytes 737312 | tf_op jit(solution)/shard_map/ppermute | solution.py:761
  661.2 26.8 %all-to-all-done.4 = bf16[4,360,1024]{2,1,0:T(8,128)(2,1)S(1)} async-done(((bf16[4,360,1024]{2,1,0:T(8,128)(2,1)}), bf16[4,360,1024]{2,1,0:T(8,128)(2,1)S(1)}, u32[]{:S(2)}, u32[]{:S(2)}) %all-to-all-start.4) | async-done | bytes 2949152 | tf_op jit(solution)/shard_map/all_to_all | solution.py:714
  696.9 30.9 %collective-permute-done.42 = bf16[360,1024]{1,0:T(8,128)(2,1)S(1)} collective-permute-done((bf16[360,1024]{1,0:T(8,128)(2,1)}, bf16[360,1024]{1,0:T(8,128)(2,1)S(1)}, u32[]{:S(2)}, u32[]{:S(2)}) %collective-permute-start.42) | collective-permute-done | bytes 737312 | tf_op jit(solution)/shard_map/ppermute | solution.py:1052
  (382 shorter events, 267.1 us)
Async XLA Ops:
  34.8 51.8 %all-to-all-start = ((bf16[4,160,1024]{2,1,0:T(8,128)(2,1)}), bf16[4,160,1024]{2,1,0:T(8,128)(2,1)}, u32[]{:S(2)}, u32[]{:S(2)}) async-start(bf16[4,160,1024]{2,1,0:T(8,128)(2,1)} %broadcast_in_dim.189), calls=%async_computation | async-start | bytes 2621440 | tf_op jit(solution)/shard_map/all_to_all | solution.py:714
  48.8 285.8 %all-gather.3.cloned.1.call-start = ((), (), s32[]{:S(2)}) async-start(), calls=%async_computation.6 | async-start | bytes 27648000 | tf_op jit(solution)/shard_map/all_gather | solution.py:908
  48.8 37.7 %collective-permute-start.4 = (bf16[4,80,1152]{2,1,0:T(8,128)(2,1)}, bf16[4,80,1152]{2,1,0:T(8,128)(2,1)S(1)}, u32[]{:S(2)}, u32[]{:S(2)}) collective-permute-start(bf16[4,80,1152]{2,1,0:T(8,128)(2,1)} %bitcast_dynamic-update-slice_fusion.18), channel_id=1, source_target_pairs={{0,4},{1,5},{2,6},{3,7},{4,0},{5,1},{6,2},{7,3},{8,12},{9,13},{10,... | collective-permute-start | bytes 2211848 | tf_op jit(solution)/shard_map/ppermute | solution.py:761
  53.2 35.9 %collective-permute-start.5 = (bf16[4,80,1152]{2,1,0:T(8,128)(2,1)}, bf16[4,80,1152]{2,1,0:T(8,128)(2,1)}, u32[]{:S(2)}, u32[]{:S(2)}) collective-permute-start(bf16[4,80,1152]{2,1,0:T(8,128)(2,1)} %bitcast_dynamic-update-slice_fusion.18), channel_id=1, source_target_pairs={{0,6},{1,7},{2,4},{3,5},{4,2},{5,3},{6,0},{7,1},{8,14},{9,15},{10,... | collective-permute-start | bytes 2211848 | tf_op jit(solution)/shard_map/ppermute | solution.py:761
  122.3 67.9 %all-to-all-start.1 = ((bf16[4,80,2560]{2,1,0:T(8,128)(2,1)}), bf16[4,80,2560]{2,1,0:T(8,128)(2,1)}, u32[]{:S(2)}, u32[]{:S(2)}) async-start(bf16[4,80,2560]{2,1,0:T(8,128)(2,1)} %broadcast_in_dim.199), calls=%async_computation.1 | async-start | bytes 3276800 | tf_op jit(solution)/shard_map/all_to_all | solution.py:714
  198.6 68.7 %all-to-all-start.2 = ((bf16[4,128,2560]{2,1,0:T(8,128)(2,1)}), bf16[4,128,2560]{2,1,0:T(8,128)(2,1)}, u32[]{:S(2)}, u32[]{:S(2)}) async-start(bf16[4,128,2560]{2,1,0:T(8,128)(2,1)} %broadcast_in_dim.201), calls=%async_computation.2 | async-start | bytes 5242880 | tf_op jit(solution)/shard_map/all_to_all | solution.py:714
  203.5 230.1 %all-gather.5.cloned.1.call-start = ((), (), s32[]{:S(2)}) async-start(), calls=%async_computation.7 | async-start | bytes 14745600 | tf_op jit(solution)/shard_map/all_gather | solution.py:922
  209.3 44.7 %collective-permute-start.15 = (bf16[128,2560]{1,0:T(8,128)(2,1)S(1)}, bf16[128,2560]{1,0:T(8,128)(2,1)S(1)}, u32[]{:S(2)}, u32[]{:S(2)}) collective-permute-start(bf16[128,2560]{1,0:T(8,128)(2,1)S(1)} %get-tuple-element.71), channel_id=1, source_target_pairs={{0,4},{1,5},{2,6},{3,7},{4,0},{5,1},{6,2},{7,3},{8,12},{9,13},{10,... | collective-permute-start | bytes 1966088 | tf_op jit(solution)/shard_map/ppermute | solution.py:761
  209.9 56.7 %collective-permute-start.14 = (bf16[128,2560]{1,0:T(8,128)(2,1)S(1)}, bf16[128,2560]{1,0:T(8,128)(2,1)S(1)}, u32[]{:S(2)}, u32[]{:S(2)}) collective-permute-start(bf16[128,2560]{1,0:T(8,128)(2,1)S(1)} %get-tuple-element.69), channel_id=1, source_target_pairs={{0,2},{1,3},{2,0},{3,1},{4,6},{5,7},{6,4},{7,5},{8,10},{9,11},{10,... | collective-permute-start | bytes 1966088 | tf_op jit(solution)/shard_map/ppermute | solution.py:761
  274.8 455.9 %reduce-scatter.2.cloned.1.call-start = ((), (), s32[]{:S(2)}) async-start(), calls=%async_computation.8 | async-start | bytes 27648000 | tf_op jit(solution)/shard_map/reduce_scatter | solution.py:929
  278.6 55.7 %collective-permute-start.18 = (bf16[128,2560]{1,0:T(8,128)(2,1)S(1)}, bf16[128,2560]{1,0:T(8,128)(2,1)S(1)}, u32[]{:S(2)}, u32[]{:S(2)}) collective-permute-start(bf16[128,2560]{1,0:T(8,128)(2,1)S(1)} %fusion.45), channel_id=1, source_target_pairs={{0,16},{8,24},{16,0},{24,8},{1,17},{9,25},{17,1},{25,9},{2,18},{10... | collective-permute-start | bytes 1966088 | tf_op jit(solution)/shard_map/ppermute | solution.py:82
  278.6 55.7 %collective-permute-start.17 = (bf16[128,2560]{1,0:T(8,128)(2,1)S(1)}, bf16[128,2560]{1,0:T(8,128)(2,1)S(1)}, u32[]{:S(2)}, u32[]{:S(2)}) collective-permute-start(bf16[128,2560]{1,0:T(8,128)(2,1)S(1)} %fusion.45), channel_id=1, source_target_pairs={{0,8},{8,16},{16,24},{24,0},{1,9},{9,17},{17,25},{25,1},{2,10},{10... | collective-permute-start | bytes 1966088 | tf_op jit(solution)/shard_map/ppermute | solution.py:82
  387.5 44.2 %collective-permute-start.21 = (bf16[128,2560]{1,0:T(8,128)(2,1)S(1)}, bf16[128,2560]{1,0:T(8,128)(2,1)S(1)}, u32[]{:S(2)}, u32[]{:S(2)}) collective-permute-start(bf16[128,2560]{1,0:T(8,128)(2,1)S(1)} %get-tuple-element.64), channel_id=1, source_target_pairs={{0,16},{8,24},{16,0},{24,8},{1,17},{9,25},{17,1},{25,9},{2,18},{10... | collective-permute-start | bytes 1966088 | tf_op jit(solution)/shard_map/ppermute | solution.py:82
  389.5 42.2 %collective-permute-start.20 = (bf16[128,2560]{1,0:T(8,128)(2,1)S(1)}, bf16[128,2560]{1,0:T(8,128)(2,1)S(1)}, u32[]{:S(2)}, u32[]{:S(2)}) collective-permute-start(bf16[128,2560]{1,0:T(8,128)(2,1)S(1)} %get-tuple-element.62), channel_id=1, source_target_pairs={{0,24},{8,0},{16,8},{24,16},{1,25},{9,1},{17,9},{25,17},{2,26},{10... | collective-permute-start | bytes 1966088 | tf_op jit(solution)/shard_map/ppermute | solution.py:82
  473.7 35.3 %collective-permute-start.29 = (bf16[128,2560]{1,0:T(8,128)(2,1)}, bf16[128,2560]{1,0:T(8,128)(2,1)}, u32[]{:S(2)}, u32[]{:S(2)}) collective-permute-start(bf16[128,2560]{1,0:T(8,128)(2,1)} %get-tuple-element.47), channel_id=1, source_target_pairs={{0,4},{1,5},{2,6},{3,7},{4,0},{5,1},{6,2},{7,3},{8,12},{9,13},{10,... | collective-permute-start | bytes 1966088 | tf_op jit(solution)/shard_map/ppermute | solution.py:761
  474.8 45.6 %collective-permute-start.30 = (bf16[128,2560]{1,0:T(8,128)(2,1)}, bf16[128,2560]{1,0:T(8,128)(2,1)}, u32[]{:S(2)}, u32[]{:S(2)}) collective-permute-start(bf16[128,2560]{1,0:T(8,128)(2,1)} %get-tuple-element.47), channel_id=1, source_target_pairs={{0,6},{1,7},{2,4},{3,5},{4,2},{5,3},{6,0},{7,1},{8,14},{9,15},{10,... | collective-permute-start | bytes 1966088 | tf_op jit(solution)/shard_map/ppermute | solution.py:761
  489.1 89.3 %all-to-all-start.3 = ((bf16[4,128,2560]{2,1,0:T(8,128)(2,1)}), bf16[4,128,2560]{2,1,0:T(8,128)(2,1)}, u32[]{:S(2)}, u32[]{:S(2)}) async-start(bf16[4,128,2560]{2,1,0:T(8,128)(2,1)} %pad_maximum_fusion.2), calls=%async_computation.3 | async-start | bytes 5242880 | tf_op jit(solution)/shard_map/all_to_all | solution.py:714
  522.4 43.4 %collective-permute-start.34 = (bf16[4,128,2560]{2,1,0:T(8,128)(2,1)}, bf16[4,128,2560]{2,1,0:T(8,128)(2,1)}, u32[]{:S(2)}, u32[]{:S(2)}) collective-permute-start(bf16[4,128,2560]{2,1,0:T(8,128)(2,1)} %bitcast_dynamic-update-slice_fusion.10), channel_id=1, source_target_pairs={{0,1},{1,0},{2,3},{3,2},{4,5},{5,4},{6,7},{7,6},{8,9},{9,8},{10,11... | collective-permute-start | bytes 7864328 | tf_op jit(solution)/shard_map/ppermute | solution.py:710
  607.9 80.1 %all-to-all-start.4 = ((bf16[4,360,1024]{2,1,0:T(8,128)(2,1)}), bf16[4,360,1024]{2,1,0:T(8,128)(2,1)S(1)}, u32[]{:S(2)}, u32[]{:S(2)}) async-start(bf16[4,360,1024]{2,1,0:T(8,128)(2,1)} %fusion.13), calls=%async_computation.4 | async-start | bytes 5898240 | tf_op jit(solution)/shard_map/all_to_all | solution.py:714
  616.7 33.9 %collective-permute-start.37 = (bf16[4,80,1152]{2,1,0:T(8,128)(2,1)}, bf16[4,80,1152]{2,1,0:T(8,128)(2,1)}, u32[]{:S(2)}, u32[]{:S(2)}) collective-permute-start(bf16[4,80,1152]{2,1,0:T(8,128)(2,1)} %get-tuple-element.57), channel_id=1, source_target_pairs={{0,4},{1,5},{2,6},{3,7},{4,0},{5,1},{6,2},{7,3},{8,12},{9,13},{10,... | collective-permute-start | bytes 2211848 | tf_op jit(solution)/shard_map/ppermute | solution.py:761
  653.7 38.0 %collective-permute-start.41 = (bf16[80,1152]{1,0:T(8,128)(2,1)S(1)}, bf16[80,1152]{1,0:T(8,128)(2,1)}, u32[]{:S(2)}, u32[]{:S(2)}) collective-permute-start(bf16[80,1152]{1,0:T(8,128)(2,1)S(1)} %get-tuple-element.84), channel_id=1, source_target_pairs={{0,8},{8,16},{16,24},{24,0},{1,9},{9,17},{17,25},{25,1},{2,10},{10... | collective-permute-start | bytes 552968 | tf_op jit(solution)/shard_map/ppermute | solution.py:82
  655.5 36.6 %collective-permute-start.40 = (bf16[80,1152]{1,0:T(8,128)(2,1)S(1)}, bf16[80,1152]{1,0:T(8,128)(2,1)}, u32[]{:S(2)}, u32[]{:S(2)}) collective-permute-start(bf16[80,1152]{1,0:T(8,128)(2,1)S(1)} %get-tuple-element.85), channel_id=1, source_target_pairs={{0,16},{8,24},{16,0},{24,8},{1,17},{9,25},{17,1},{25,9},{2,18},{10... | collective-permute-start | bytes 552968 | tf_op jit(solution)/shard_map/ppermute | solution.py:82
  657.8 34.2 %collective-permute-start.39 = (bf16[80,1152]{1,0:T(8,128)(2,1)S(1)}, bf16[80,1152]{1,0:T(8,128)(2,1)}, u32[]{:S(2)}, u32[]{:S(2)}) collective-permute-start(bf16[80,1152]{1,0:T(8,128)(2,1)S(1)} %get-tuple-element.83), channel_id=1, source_target_pairs={{0,24},{8,0},{16,8},{24,16},{1,25},{9,1},{17,9},{25,17},{2,26},{10... | collective-permute-start | bytes 552968 | tf_op jit(solution)/shard_map/ppermute | solution.py:82
  689.6 38.2 %collective-permute-start.42 = (bf16[360,1024]{1,0:T(8,128)(2,1)}, bf16[360,1024]{1,0:T(8,128)(2,1)S(1)}, u32[]{:S(2)}, u32[]{:S(2)}) collective-permute-start(bf16[360,1024]{1,0:T(8,128)(2,1)} %reduce_sum.142), channel_id=1, source_target_pairs={{0,0},{1,12},{2,8},{3,20},{4,16},{5,28},{6,24},{7,4},{8,1},{9,13},... | collective-permute-start | bytes 2211848 | tf_op jit(solution)/shard_map/ppermute | solution.py:1052
  (86 other events, 1168.9 us)
Sparse Core Ops, SparseCore 0:
  104.8 167.6 all-gather.2
  275.0 75.9 all-gather.4
  373.0 188.6 reduce-scatter.1

commit v6 on v5

--- a/solution.py
+++ b/solution.py
@@ -661,7 +661,7 @@
     )(weights, rows, grads)
 
 
-def ffn_grads_kernel(both_ref, act_ref, rows_ref, grads_ref, out_ref):
+def ffn_grads_kernel(both_ref, act_ref, rows_ref, grads_ref, earlier_ref, out_ref):
     hidden = act_ref.shape[1]
     parts = ((both_ref[0, 0], rows_ref), (both_ref[1, 0], rows_ref), (act_ref[0], grads_ref))
     for place, (left, right) in enumerate(parts):
@@ -670,7 +670,7 @@
         ).astype(BF16)
 
 
-def ffn_grads(grad_both, activated, rows, grads):
+def ffn_grads(grad_both, activated, rows, grads, earlier):
     steps, hidden, count = activated.shape
     width = rows.shape[1]
     whole = pl.BlockSpec(memory_space=pltpu.VMEM)
@@ -683,6 +683,7 @@
             own,
             whole,
             whole,
+            pl.BlockSpec(memory_space=pl.ANY),
         ],
         out_specs=pl.BlockSpec((1, 3 * hidden, width), lambda i: (i, 0, 0)),
         out_shape=jax.ShapeDtypeStruct((steps, 3 * hidden, width), BF16),
@@ -693,7 +694,7 @@
             transcendentals=0,
         ),
         name="ffn_grads",
-    )(grad_both, activated, rows, grads)
+    )(grad_both, activated, rows, grads, earlier)
 
 
 def done(value):
@@ -795,11 +796,11 @@
             whole = lax.dynamic_update_index_in_dim(whole, piece, (place - k) % dp_count, 0)
         return whole
 
-    def scatter_z(blocks):
+    def scatter_z(blocks, token=0):
         blocks = blocks.astype(BF16)
         total = choose(blocks, place, 0).astype(F32)
         for k in range(1, dp_count):
-            block = choose(blocks, (place - k) % dp_count, 0)
+            block = choose(blocks, (place - k) % dp_count + token, 0)
             total = total + shift(block, "dp", dp_count, -k).astype(F32)
         return total
 
@@ -924,24 +925,25 @@
     count = dp_count * tokens
     grad_both, activated = ffn_hidden(ffn_full, normed_rows, grad_rows)
     grad_part = dot("gft,gfd->td", grad_both, ffn_full[:2])
-    grad_normed_two = send_home(jnp.split(grad_part.astype(BF16), dp_count))
+    grad_low = grad_part.astype(BF16)
+    grad_normed_two = send_home(jnp.split(grad_low, dp_count))
     out_part = dot("ft,fd->td", activated, ffn_full[2]).astype(BF16)
-    ffn_sums = lax.psum_scatter(
-        ffn_grads(
-            grad_both.reshape(2, seq_count, own_hidden, count),
-            activated.reshape(seq_count, own_hidden, count),
-            normed_rows,
-            grad_rows,
-        ),
-        "seq",
-        scatter_dimension=0,
-    ).astype(F32)
+    hidden_grads = ffn_grads(
+        grad_both.reshape(2, seq_count, own_hidden, count),
+        activated.reshape(seq_count, own_hidden, count),
+        normed_rows,
+        grad_rows,
+        grad_low,
+    )
+    ffn_sums = lax.psum_scatter(hidden_grads, "seq", scatter_dimension=0).astype(F32)
 
     grad_middle_norm, grad_ffn_gain_part = norm_back(
         grad_normed_two, normal_two, inverse_two, ffn_gain_full
     )
     grad_middle = grad_out + grad_middle_norm
-    grad_branch = (RESIDUAL_SCALE * grad_middle).astype(BF16)
+    grad_branch = hold(
+        (RESIDUAL_SCALE * grad_middle).astype(BF16), done(out_part) + done(hidden_grads)
+    )
     grad_attended = dot("td,kd->tk", grad_branch, proj_full).astype(BF16)
     grad_blocks = grad_attended.reshape(tokens, seq_count, head_width).transpose(1, 0, 2)
     grad_blocks = jnp.pad(
@@ -1047,8 +1049,8 @@
         choose(down_sums, core, 1),
         choose(down_sums, 1 - core + done(group_grads), 1),
     )
-    sum_down = scatter_z(sum_down)
     group_sums = jnp.sum(exchange(hold(group_grads, core_done), "dp").astype(F32), 0)
+    sum_down = scatter_z(sum_down, done(group_sums))
     group_sums = lax.ppermute(group_sums.astype(BF16), both, to_owner).astype(F32)
     sum_query_up = group_sums[: query_up.shape[1], :query_rank].T
     sum_latent_up = group_sums[: latent_up.shape[1], query_rank:].T

time: 753 us -> 776 us (1.031)
  other arithmetic: 35.6 us -> 44.3 us
  waiting for transfers between devices: 325 us -> 333 us
    ppermute x21, waiting for transfers between devices: 162 us -> 180 us  [across(): lax.ppermute(value, 'seq', [(i, i ^ 2 * steps) for i in range(seq_count)])]
    ppermute x12, waiting for transfers between devices: 95.5 us -> 83.8 us  [shift(): lax.ppermute(value, axis, [(i, (i + step) % count) for i in range(count)])]
    unnamed x121 -> x129, local copies, waits for them, and re-layouts: 18.1 us -> 16.2 us
  transfers between devices with their start and end apart: 51 -> 51, of which waited for: 24 -> 24; matrix products, arithmetic and copies ran while one was open for 21% -> 22% of each run, Pallas kernels for 12% -> 11%
where the time goes in v6:
time: 776 us; the launch traced here: 766 us
  waiting for transfers between devices  333 us (43%)
  starting transfers between devices  111 us (14%)
  local copies, waits for them, and re-layouts  94.6 us (12%)
  Pallas kernels  86 us (11%)
  matrix products  63.7 us (8%)
  other arithmetic  44.3 us (6%)
  between operations  34.1 us (4%)
    ppermute x21, waiting for transfers between devices, across(): lax.ppermute(value, 'seq', [(i, i ^ 2 * steps) for i in range(seq_count)])  180 us
    ppermute x12, waiting for transfers between devices, shift(): lax.ppermute(value, axis, [(i, (i + step) % count) for i in range(count)])  83.8 us
    dot_general x10, matrix products, dot(): return jnp.einsum(spec, left, right, preferred_element_type=F32)  57.8 us
    all_to_all x5, starting transfers between devices, exchange(): lax.all_to_all(blocks, axis, split_axis=0, concat_axis=0, axis_index_grou...  53.8 us
    ppermute x1, waiting for transfers between devices, per_device_heads(): lax.ppermute(group_sums.astype(BF16), both, to_owner).astype(F32)  31.4 us
    all_to_all x5, waiting for transfers between devices, exchange(): lax.all_to_all(blocks, axis, split_axis=0, concat_axis=0, axis_index_grou...  27.3 us
    pallas_call x1, Pallas kernels, attend_back(): pl.pallas_call(attend_back_kernel, grid=(heads,), in_specs=[whole, pl.Blo...  25.1 us
    ppermute x21, starting transfers between devices, across(): lax.ppermute(value, 'seq', [(i, i ^ 2 * steps) for i in range(seq_count)])  24.7 us
  transfers between devices with their start and end apart: 51, of which 24 were waited for; matrix products, arithmetic and copies ran while one was open for 22% of the time, Pallas kernels for 11%

profile of v6, /device:TPU:2, one launch (start us, length us, event | category | flops | bytes accessed | tf_op | source)
XLA Modules:
  0.0 765.9 jit_solution(4205289718146917569)
XLA Ops:
  34.8 14.0 %all-to-all-start = ((bf16[4,160,1024]{2,1,0:T(8,128)(2,1)}), bf16[4,160,1024]{2,1,0:T(8,128)(2,1)}, u32[]{:S(2)}, u32[]{:S(2)}) async-start(bf16[4,160,1024]{2,1,0:T(8,128)(2,1)} %broadcast_in_dim.189), calls=%async_computation | async-start | bytes 2621440 | tf_op jit(solution)/shard_map/all_to_all | solution.py:715
  54.7 11.5 %collective-permute-done.3 = bf16[4,80,1152]{2,1,0:T(8,128)(2,1)} collective-permute-done((bf16[4,80,1152]{2,1,0:T(8,128)(2,1)}, bf16[4,80,1152]{2,1,0:T(8,128)(2,1)}, u32[]{:S(2)}, u32[]{:S(2)}) %collective-permute-start.3) | collective-permute-done | bytes 737312 | tf_op jit(solution)/shard_map/ppermute | solution.py:762
  67.4 19.1 %collective-permute-done.4 = bf16[4,80,1152]{2,1,0:T(8,128)(2,1)S(1)} collective-permute-done((bf16[4,80,1152]{2,1,0:T(8,128)(2,1)}, bf16[4,80,1152]{2,1,0:T(8,128)(2,1)S(1)}, u32[]{:S(2)}, u32[]{:S(2)}) %collective-permute-start.4) | collective-permute-done | bytes 737312 | tf_op jit(solution)/shard_map/ppermute | solution.py:762
  122.3 12.4 %all-to-all-start.1 = ((bf16[4,80,2560]{2,1,0:T(8,128)(2,1)}), bf16[4,80,2560]{2,1,0:T(8,128)(2,1)}, u32[]{:S(2)}, u32[]{:S(2)}) async-start(bf16[4,80,2560]{2,1,0:T(8,128)(2,1)} %broadcast_in_dim.199), calls=%async_computation.1 | async-start | bytes 3276800 | tf_op jit(solution)/shard_map/all_to_all | solution.py:715
  138.1 18.9 %collective-permute-done.9 = bf16[128,1152]{0,1:T(8,128)(2,1)S(1)} collective-permute-done((bf16[128,1152]{0,1:T(8,128)(2,1)S(1)}, bf16[128,1152]{0,1:T(8,128)(2,1)S(1)}, u32[]{:S(2)}, u32[]{:S(2)}) %collective-permute-start.9) | collective-permute-done | bytes 294944 | tf_op jit(solution)/shard_map/ppermute | solution.py:762
  162.3 23.8 %attend.1 = (bf16[1024,640]{1,0:T(8,128)(2,1)S(1)}, bf16[1024,640]{1,0:T(8,128)(2,1)S(1)}, bf16[1024,384]{1,0:T(8,128)(2,1)S(1)}, f32[1024,640]{1,0:T(8,128)S(1)}) custom-call(bf16[1024,1152]{1,0:T(8,128)(2,1)S(1)} %bitcast.230, bf16[640,768]{1,0:T(8,128)(2,1)S(1)} %bitcast.234, bf16[640,256]{1,0:T(8,128)(2,1)S(1)} %bitcast.238), custom_call_target="tpu_custom_call" | custom-call | flops 2013265920 | bytes 7864320 | tf_op jit(solution)/shard_map/attend/pallas_call | solution.py:485
  210.8 29.0 %collective-permute-done.16 = bf16[128,2560]{1,0:T(8,128)(2,1)S(1)} collective-permute-done((bf16[128,2560]{1,0:T(8,128)(2,1)S(1)}, bf16[128,2560]{1,0:T(8,128)(2,1)S(1)}, u32[]{:S(2)}, u32[]{:S(2)}) %collective-permute-start.16) | collective-permute-done | bytes 655392 | tf_op jit(solution)/shard_map/ppermute | solution.py:762
  239.8 14.0 %collective-permute-done.15 = bf16[128,2560]{1,0:T(8,128)(2,1)S(1)} collective-permute-done((bf16[128,2560]{1,0:T(8,128)(2,1)S(1)}, bf16[128,2560]{1,0:T(8,128)(2,1)S(1)}, u32[]{:S(2)}, u32[]{:S(2)}) %collective-permute-start.15) | collective-permute-done | bytes 655392 | tf_op jit(solution)/shard_map/ppermute | solution.py:762
  253.8 12.6 %collective-permute-done.14 = bf16[128,2560]{1,0:T(8,128)(2,1)S(1)} collective-permute-done((bf16[128,2560]{1,0:T(8,128)(2,1)S(1)}, bf16[128,2560]{1,0:T(8,128)(2,1)S(1)}, u32[]{:S(2)}, u32[]{:S(2)}) %collective-permute-start.14) | collective-permute-done | bytes 655392 | tf_op jit(solution)/shard_map/ppermute | solution.py:762
  283.6 10.1 %collective-permute-done.19 = bf16[128,2560]{1,0:T(8,128)(2,1)S(1)} collective-permute-done((bf16[128,2560]{1,0:T(8,128)(2,1)S(1)}, bf16[128,2560]{1,0:T(8,128)(2,1)S(1)}, u32[]{:S(2)}, u32[]{:S(2)}) %collective-permute-start.19) | collective-permute-done | bytes 655392 | tf_op jit(solution)/shard_map/ppermute | solution.py:82
  293.6 40.5 %collective-permute-done.18 = bf16[128,2560]{1,0:T(8,128)(2,1)S(1)} collective-permute-done((bf16[128,2560]{1,0:T(8,128)(2,1)S(1)}, bf16[128,2560]{1,0:T(8,128)(2,1)S(1)}, u32[]{:S(2)}, u32[]{:S(2)}) %collective-permute-start.18) | collective-permute-done | bytes 655392 | tf_op jit(solution)/shard_map/ppermute | solution.py:82
  334.3 18.7 %ffn_hidden.1 = (bf16[2,1600,512]{2,1,0:T(8,128)(2,1)}, bf16[1600,512]{1,0:T(8,128)(2,1)S(1)}) custom-call(bf16[3,1600,2560]{2,1,0:T(8,128)(2,1)} %all-gather.3.cloned.1.call-done.weights_ref, bf16[512,2560]{1,0:T(8,128)(2,1)S(1)} %pad_maximum_fusion.rows_ref, bf16[512,2560]{1,0:T(8,128)(2,1)} %pad_maximum_fusion.1.grads_ref), custom_call_target="tpu_custom_call" | custom-call | flops 12582912000 | bytes 34734080 | tf_op jit(solution)/shard_map/ffn_hidden/pallas_call | solution.py:645
  353.1 15.3 %bitcast_convert_fusion.earlier_ref = bf16[512,2560]{1,0:T(8,128)(2,1)} fusion(bf16[2,1600,512]{2,1,0:T(8,128)(2,1)} %get-tuple-element.25, bf16[3,1600,2560]{2,1,0:T(8,128)(2,1)} %all-gather.3.cloned.1.call-done.weights_ref), kind=kOutput, calls=%fused_computation.14 | convolution fusion | flops 8389918720 | bytes 22282240 | tf_op jit(solution)/shard_map/gft,gfd->td/dot_general | solution.py:78
  368.4 18.4 %ffn_grads.1 = bf16[8,600,2560]{2,1,0:T(8,128)(2,1)} custom-call(bf16[2,8,200,512]{3,2,1,0:T(8,128)(2,1)} %bitcast.273, bf16[8,200,512]{2,1,0:T(8,128)(2,1)S(1)} %bitcast.240, bf16[512,2560]{1,0:T(8,128)(2,1)S(1)} %pad_maximum_fusion.rows_ref, bf16[512,2560]{1,0:T(8,128)(2,1)} %pad_maximum_fusion.1.grads_ref, bf16[512,2560]{1,0:T(8,128)(2,1)} %bitcast_convert_fusion.earlier_ref), custom_call_target="tpu_custom_call" | custom-call | flops 12582912000 | bytes 34734080 | tf_op jit(solution)/shard_map/ffn_grads/pallas_call | solution.py:678
  395.7 10.4 %fusion.10.earlier_ref = bf16[512,2560]{1,0:T(8,128)(2,1)S(1)} fusion(bf16[1600,512]{1,0:T(8,128)(2,1)S(1)} %copy-done.5, bf16[3,1600,2560]{2,1,0:T(8,128)(2,1)} %all-gather.3.cloned.1.call-done.weights_ref), kind=kOutput, calls=%fused_computation.17 | convolution fusion | flops 4195614720 | bytes 12451840 | tf_op jit(solution)/shard_map/ft,fd->td/dot_general | solution.py:78
  411.1 24.0 %collective-permute-done.21 = bf16[128,2560]{1,0:T(8,128)(2,1)S(1)} collective-permute-done((bf16[128,2560]{1,0:T(8,128)(2,1)}, bf16[128,2560]{1,0:T(8,128)(2,1)S(1)}, u32[]{:S(2)}, u32[]{:S(2)}) %collective-permute-start.21) | collective-permute-done | bytes 655392 | tf_op jit(solution)/shard_map/ppermute | solution.py:82
  440.8 10.0 %convolution_convert_fusion.1 = bf16[128,2560]{1,0:T(8,128)(2,1)S(1)} fusion(bf16[2560,2560]{1,0:T(8,128)(2,1)} %all-gather.5.cloned.1.call-done, f32[128,2560]{1,0:T(8,128)S(1)} %convert_add_fusion.2, pred[]{:T(512)S(6)} %eq.77), kind=kOutput, calls=%fused_computation.19 | convolution fusion | flops 1679032320 | bytes 15073281 | tf_op jit(solution)/shard_map/td,kd->tk/dot_general | solution.py:78
  483.7 17.9 %all-to-all-start.3 = ((bf16[4,128,2560]{2,1,0:T(8,128)(2,1)}), bf16[4,128,2560]{2,1,0:T(8,128)(2,1)}, u32[]{:S(2)}, u32[]{:S(2)}) async-start(bf16[4,128,2560]{2,1,0:T(8,128)(2,1)} %pad_maximum_fusion.2), calls=%async_computation.3 | async-start | bytes 5242880 | tf_op jit(solution)/shard_map/all_to_all | solution.py:715
  513.9 20.4 %collective-permute-done.30 = bf16[128,2560]{1,0:T(8,128)(2,1)} collective-permute-done((bf16[128,2560]{1,0:T(8,128)(2,1)}, bf16[128,2560]{1,0:T(8,128)(2,1)}, u32[]{:S(2)}, u32[]{:S(2)}) %collective-permute-start.30) | collective-permute-done | bytes 655392 | tf_op jit(solution)/shard_map/ppermute | solution.py:762
  536.3 25.1 %attend_back.1 = (bf16[1024,640]{1,0:T(8,128)(2,1)S(1)}, bf16[1024,640]{1,0:T(8,128)(2,1)S(1)}, bf16[1024,1152]{1,0:T(8,128)(2,1)}) custom-call(bf16[1024,1152]{1,0:T(8,128)(2,1)} %bitcast.231, bf16[640,768]{1,0:T(8,128)(2,1)S(1)} %bitcast.235, bf16[640,256]{1,0:T(8,128)(2,1)S(1)} %bitcast.239, bf16[1024,640]{1,0:T(8,128)(2,1)S(1)} %copy-done.12, ...), custom_call_target="tpu_custom_call" | custom-call | flops 5368709120 | bytes 9175040 | tf_op jit(solution)/shard_map/attend_back/pallas_call | solution.py:583
  633.2 13.8 %collective-permute-done.38 = bf16[4,80,1152]{2,1,0:T(8,128)(2,1)} collective-permute-done((bf16[4,80,1152]{2,1,0:T(8,128)(2,1)}, bf16[4,80,1152]{2,1,0:T(8,128)(2,1)}, u32[]{:S(2)}, u32[]{:S(2)}) %collective-permute-start.38) | collective-permute-done | bytes 737312 | tf_op jit(solution)/shard_map/ppermute | solution.py:762
  647.0 15.0 %collective-permute-done.37 = bf16[4,80,1152]{2,1,0:T(8,128)(2,1)} collective-permute-done((bf16[4,80,1152]{2,1,0:T(8,128)(2,1)}, bf16[4,80,1152]{2,1,0:T(8,128)(2,1)}, u32[]{:S(2)}, u32[]{:S(2)}) %collective-permute-start.37) | collective-permute-done | bytes 737312 | tf_op jit(solution)/shard_map/ppermute | solution.py:762
  664.7 27.3 %all-to-all-done.4 = bf16[4,360,1024]{2,1,0:T(8,128)(2,1)} async-done(((bf16[4,360,1024]{2,1,0:T(8,128)(2,1)}), bf16[4,360,1024]{2,1,0:T(8,128)(2,1)}, u32[]{:S(2)}, u32[]{:S(2)}) %all-to-all-start.4) | async-done | bytes 2949152 | tf_op jit(solution)/shard_map/all_to_all | solution.py:715
  719.1 31.4 %collective-permute-done.42 = bf16[360,1024]{1,0:T(8,128)(2,1)S(1)} collective-permute-done((bf16[360,1024]{1,0:T(8,128)(2,1)S(1)}, bf16[360,1024]{1,0:T(8,128)(2,1)S(1)}, u32[]{:S(2)}, u32[]{:S(2)}) %collective-permute-start.42) | collective-permute-done | bytes 737312 | tf_op jit(solution)/shard_map/ppermute | solution.py:1054
  (395 shorter events, 278.1 us)
Async XLA Ops:
  34.8 51.8 %all-to-all-start = ((bf16[4,160,1024]{2,1,0:T(8,128)(2,1)}), bf16[4,160,1024]{2,1,0:T(8,128)(2,1)}, u32[]{:S(2)}, u32[]{:S(2)}) async-start(bf16[4,160,1024]{2,1,0:T(8,128)(2,1)} %broadcast_in_dim.189), calls=%async_computation | async-start | bytes 2621440 | tf_op jit(solution)/shard_map/all_to_all | solution.py:715
  48.8 285.5 %all-gather.3.cloned.1.call-start = ((), (), s32[]{:S(2)}) async-start(), calls=%async_computation.6 | async-start | bytes 27648000 | tf_op jit(solution)/shard_map/all_gather | solution.py:909
  48.8 37.7 %collective-permute-start.4 = (bf16[4,80,1152]{2,1,0:T(8,128)(2,1)}, bf16[4,80,1152]{2,1,0:T(8,128)(2,1)S(1)}, u32[]{:S(2)}, u32[]{:S(2)}) collective-permute-start(bf16[4,80,1152]{2,1,0:T(8,128)(2,1)} %bitcast_dynamic-update-slice_fusion.18), channel_id=1, source_target_pairs={{0,4},{1,5},{2,6},{3,7},{4,0},{5,1},{6,2},{7,3},{8,12},{9,13},{10,... | collective-permute-start | bytes 2211848 | tf_op jit(solution)/shard_map/ppermute | solution.py:762
  53.2 35.9 %collective-permute-start.5 = (bf16[4,80,1152]{2,1,0:T(8,128)(2,1)}, bf16[4,80,1152]{2,1,0:T(8,128)(2,1)}, u32[]{:S(2)}, u32[]{:S(2)}) collective-permute-start(bf16[4,80,1152]{2,1,0:T(8,128)(2,1)} %bitcast_dynamic-update-slice_fusion.18), channel_id=1, source_target_pairs={{0,6},{1,7},{2,4},{3,5},{4,2},{5,3},{6,0},{7,1},{8,14},{9,15},{10,... | collective-permute-start | bytes 2211848 | tf_op jit(solution)/shard_map/ppermute | solution.py:762
  122.3 67.7 %all-to-all-start.1 = ((bf16[4,80,2560]{2,1,0:T(8,128)(2,1)}), bf16[4,80,2560]{2,1,0:T(8,128)(2,1)}, u32[]{:S(2)}, u32[]{:S(2)}) async-start(bf16[4,80,2560]{2,1,0:T(8,128)(2,1)} %broadcast_in_dim.199), calls=%async_computation.1 | async-start | bytes 3276800 | tf_op jit(solution)/shard_map/all_to_all | solution.py:715
  198.4 68.7 %all-to-all-start.2 = ((bf16[4,128,2560]{2,1,0:T(8,128)(2,1)}), bf16[4,128,2560]{2,1,0:T(8,128)(2,1)}, u32[]{:S(2)}, u32[]{:S(2)}) async-start(bf16[4,128,2560]{2,1,0:T(8,128)(2,1)} %broadcast_in_dim.201), calls=%async_computation.2 | async-start | bytes 5242880 | tf_op jit(solution)/shard_map/all_to_all | solution.py:715
  203.3 237.5 %all-gather.5.cloned.1.call-start = ((), (), s32[]{:S(2)}) async-start(), calls=%async_computation.7 | async-start | bytes 14745600 | tf_op jit(solution)/shard_map/all_gather | solution.py:923
  207.3 32.6 %collective-permute-start.16 = (bf16[128,2560]{1,0:T(8,128)(2,1)S(1)}, bf16[128,2560]{1,0:T(8,128)(2,1)S(1)}, u32[]{:S(2)}, u32[]{:S(2)}) collective-permute-start(bf16[128,2560]{1,0:T(8,128)(2,1)S(1)} %get-tuple-element.70), channel_id=1, source_target_pairs={{0,6},{1,7},{2,4},{3,5},{4,2},{5,3},{6,0},{7,1},{8,14},{9,15},{10,... | collective-permute-start | bytes 1966088 | tf_op jit(solution)/shard_map/ppermute | solution.py:762
  209.0 44.7 %collective-permute-start.15 = (bf16[128,2560]{1,0:T(8,128)(2,1)S(1)}, bf16[128,2560]{1,0:T(8,128)(2,1)S(1)}, u32[]{:S(2)}, u32[]{:S(2)}) collective-permute-start(bf16[128,2560]{1,0:T(8,128)(2,1)S(1)} %get-tuple-element.71), channel_id=1, source_target_pairs={{0,4},{1,5},{2,6},{3,7},{4,0},{5,1},{6,2},{7,3},{8,12},{9,13},{10,... | collective-permute-start | bytes 1966088 | tf_op jit(solution)/shard_map/ppermute | solution.py:762
  209.6 56.8 %collective-permute-start.14 = (bf16[128,2560]{1,0:T(8,128)(2,1)S(1)}, bf16[128,2560]{1,0:T(8,128)(2,1)S(1)}, u32[]{:S(2)}, u32[]{:S(2)}) collective-permute-start(bf16[128,2560]{1,0:T(8,128)(2,1)S(1)} %get-tuple-element.69), channel_id=1, source_target_pairs={{0,2},{1,3},{2,0},{3,1},{4,6},{5,7},{6,4},{7,5},{8,10},{9,11},{10,... | collective-permute-start | bytes 1966088 | tf_op jit(solution)/shard_map/ppermute | solution.py:762
  274.6 478.8 %reduce-scatter.2.cloned.1.call-start = ((), (), s32[]{:S(2)}) async-start(), calls=%async_computation.8 | async-start | bytes 27648000 | tf_op jit(solution)/shard_map/reduce_scatter | solution.py:938
  278.4 55.7 %collective-permute-start.18 = (bf16[128,2560]{1,0:T(8,128)(2,1)S(1)}, bf16[128,2560]{1,0:T(8,128)(2,1)S(1)}, u32[]{:S(2)}, u32[]{:S(2)}) collective-permute-start(bf16[128,2560]{1,0:T(8,128)(2,1)S(1)} %fusion.45), channel_id=1, source_target_pairs={{0,16},{8,24},{16,0},{24,8},{1,17},{9,25},{17,1},{25,9},{2,18},{10... | collective-permute-start | bytes 1966088 | tf_op jit(solution)/shard_map/ppermute | solution.py:82
  278.4 55.7 %collective-permute-start.17 = (bf16[128,2560]{1,0:T(8,128)(2,1)S(1)}, bf16[128,2560]{1,0:T(8,128)(2,1)S(1)}, u32[]{:S(2)}, u32[]{:S(2)}) collective-permute-start(bf16[128,2560]{1,0:T(8,128)(2,1)S(1)} %fusion.45), channel_id=1, source_target_pairs={{0,8},{8,16},{16,24},{24,0},{1,9},{9,17},{17,25},{25,1},{2,10},{10... | collective-permute-start | bytes 1966088 | tf_op jit(solution)/shard_map/ppermute | solution.py:82
  390.7 44.4 %collective-permute-start.21 = (bf16[128,2560]{1,0:T(8,128)(2,1)}, bf16[128,2560]{1,0:T(8,128)(2,1)S(1)}, u32[]{:S(2)}, u32[]{:S(2)}) collective-permute-start(bf16[128,2560]{1,0:T(8,128)(2,1)} %get-tuple-element.64), channel_id=1, source_target_pairs={{0,16},{8,24},{16,0},{24,8},{1,17},{9,25},{17,1},{25,9},{2,18},{10... | collective-permute-start | bytes 1966088 | tf_op jit(solution)/shard_map/ppermute | solution.py:82
  392.6 42.5 %collective-permute-start.20 = (bf16[128,2560]{1,0:T(8,128)(2,1)}, bf16[128,2560]{1,0:T(8,128)(2,1)}, u32[]{:S(2)}, u32[]{:S(2)}) collective-permute-start(bf16[128,2560]{1,0:T(8,128)(2,1)} %get-tuple-element.62), channel_id=1, source_target_pairs={{0,24},{8,0},{16,8},{24,16},{1,25},{9,1},{17,9},{25,17},{2,26},{10... | collective-permute-start | bytes 1966088 | tf_op jit(solution)/shard_map/ppermute | solution.py:82
  478.0 31.9 %collective-permute-start.28 = (bf16[128,2560]{1,0:T(8,128)(2,1)}, bf16[128,2560]{1,0:T(8,128)(2,1)}, u32[]{:S(2)}, u32[]{:S(2)}) collective-permute-start(bf16[128,2560]{1,0:T(8,128)(2,1)} %get-tuple-element.47), channel_id=1, source_target_pairs={{0,2},{1,3},{2,0},{3,1},{4,6},{5,7},{6,4},{7,5},{8,10},{9,11},{10,... | collective-permute-start | bytes 1966088 | tf_op jit(solution)/shard_map/ppermute | solution.py:762
  478.1 33.8 %collective-permute-start.29 = (bf16[128,2560]{1,0:T(8,128)(2,1)}, bf16[128,2560]{1,0:T(8,128)(2,1)}, u32[]{:S(2)}, u32[]{:S(2)}) collective-permute-start(bf16[128,2560]{1,0:T(8,128)(2,1)} %get-tuple-element.47), channel_id=1, source_target_pairs={{0,4},{1,5},{2,6},{3,7},{4,0},{5,1},{6,2},{7,3},{8,12},{9,13},{10,... | collective-permute-start | bytes 1966088 | tf_op jit(solution)/shard_map/ppermute | solution.py:762
  479.5 54.8 %collective-permute-start.30 = (bf16[128,2560]{1,0:T(8,128)(2,1)}, bf16[128,2560]{1,0:T(8,128)(2,1)}, u32[]{:S(2)}, u32[]{:S(2)}) collective-permute-start(bf16[128,2560]{1,0:T(8,128)(2,1)} %get-tuple-element.47), channel_id=1, source_target_pairs={{0,6},{1,7},{2,4},{3,5},{4,2},{5,3},{6,0},{7,1},{8,14},{9,15},{10,... | collective-permute-start | bytes 1966088 | tf_op jit(solution)/shard_map/ppermute | solution.py:762
  483.7 108.5 %all-to-all-start.3 = ((bf16[4,128,2560]{2,1,0:T(8,128)(2,1)}), bf16[4,128,2560]{2,1,0:T(8,128)(2,1)}, u32[]{:S(2)}, u32[]{:S(2)}) async-start(bf16[4,128,2560]{2,1,0:T(8,128)(2,1)} %pad_maximum_fusion.2), calls=%async_computation.3 | async-start | bytes 5242880 | tf_op jit(solution)/shard_map/all_to_all | solution.py:715
  536.3 43.3 %collective-permute-start.34 = (bf16[4,128,2560]{2,1,0:T(8,128)(2,1)}, bf16[4,128,2560]{2,1,0:T(8,128)(2,1)}, u32[]{:S(2)}, u32[]{:S(2)}) collective-permute-start(bf16[4,128,2560]{2,1,0:T(8,128)(2,1)} %bitcast_dynamic-update-slice_fusion.10), channel_id=1, source_target_pairs={{0,1},{1,0},{2,3},{3,2},{4,5},{5,4},{6,7},{7,6},{8,9},{9,8},{10,11... | collective-permute-start | bytes 7864328 | tf_op jit(solution)/shard_map/ppermute | solution.py:711
  620.3 71.7 %all-to-all-start.4 = ((bf16[4,360,1024]{2,1,0:T(8,128)(2,1)}), bf16[4,360,1024]{2,1,0:T(8,128)(2,1)}, u32[]{:S(2)}, u32[]{:S(2)}) async-start(bf16[4,360,1024]{2,1,0:T(8,128)(2,1)} %fusion.13), calls=%async_computation.4 | async-start | bytes 5898240 | tf_op jit(solution)/shard_map/all_to_all | solution.py:715
  627.8 34.2 %collective-permute-start.37 = (bf16[4,80,1152]{2,1,0:T(8,128)(2,1)}, bf16[4,80,1152]{2,1,0:T(8,128)(2,1)}, u32[]{:S(2)}, u32[]{:S(2)}) collective-permute-start(bf16[4,80,1152]{2,1,0:T(8,128)(2,1)} %get-tuple-element.57), channel_id=1, source_target_pairs={{0,4},{1,5},{2,6},{3,7},{4,0},{5,1},{6,2},{7,3},{8,12},{9,13},{10,... | collective-permute-start | bytes 2211848 | tf_op jit(solution)/shard_map/ppermute | solution.py:762
  629.8 32.1 %collective-permute-start.36 = (bf16[4,80,1152]{2,1,0:T(8,128)(2,1)}, bf16[4,80,1152]{2,1,0:T(8,128)(2,1)}, u32[]{:S(2)}, u32[]{:S(2)}) collective-permute-start(bf16[4,80,1152]{2,1,0:T(8,128)(2,1)} %get-tuple-element.55), channel_id=1, source_target_pairs={{0,2},{1,3},{2,0},{3,1},{4,6},{5,7},{6,4},{7,5},{8,10},{9,11},{10,... | collective-permute-start | bytes 2211848 | tf_op jit(solution)/shard_map/ppermute | solution.py:762
  706.8 43.7 %collective-permute-start.42 = (bf16[360,1024]{1,0:T(8,128)(2,1)S(1)}, bf16[360,1024]{1,0:T(8,128)(2,1)S(1)}, u32[]{:S(2)}, u32[]{:S(2)}) collective-permute-start(bf16[360,1024]{1,0:T(8,128)(2,1)S(1)} %convert_element_type.446), channel_id=1, source_target_pairs={{0,0},{1,12},{2,8},{3,20},{4,16},{5,28},{6,24},{7,4},{8,1},{9,13},... | collective-permute-start | bytes 2211848 | tf_op jit(solution)/shard_map/ppermute | solution.py:1054
  (90 other events, 1095.8 us)
Sparse Core Ops, SparseCore 0:
  104.8 167.6 all-gather.2
  275.0 75.7 all-gather.4
  387.0 188.6 reduce-scatter.1

commit v7 on v5

--- a/solution.py
+++ b/solution.py
@@ -662,12 +662,9 @@
 
 
 def ffn_grads_kernel(both_ref, act_ref, rows_ref, grads_ref, out_ref):
-    hidden = act_ref.shape[1]
     parts = ((both_ref[0, 0], rows_ref), (both_ref[1, 0], rows_ref), (act_ref[0], grads_ref))
     for place, (left, right) in enumerate(parts):
-        out_ref[0, place * hidden : (place + 1) * hidden, :] = jnp.dot(
-            left, right[...], preferred_element_type=F32
-        ).astype(BF16)
+        out_ref[0, place] = jnp.dot(left, right[...], preferred_element_type=F32).astype(BF16)
 
 
 def ffn_grads(grad_both, activated, rows, grads):
@@ -684,8 +681,8 @@
             whole,
             whole,
         ],
-        out_specs=pl.BlockSpec((1, 3 * hidden, width), lambda i: (i, 0, 0)),
-        out_shape=jax.ShapeDtypeStruct((steps, 3 * hidden, width), BF16),
+        out_specs=pl.BlockSpec((1, 3, hidden, width), lambda i: (i, 0, 0, 0)),
+        out_shape=jax.ShapeDtypeStruct((steps, 3, hidden, width), BF16),
         compiler_params=pltpu.CompilerParams(vmem_limit_bytes=48 * 1024 * 1024),
         cost_estimate=pl.CostEstimate(
             flops=6 * steps * hidden * width * count,
@@ -694,6 +691,29 @@
         ),
         name="ffn_grads",
     )(grad_both, activated, rows, grads)
+
+
+def ffn_sums_kernel(sums_ref, gate_ref, up_ref, down_ref):
+    gate_ref[...] = sums_ref[0].astype(F32).T
+    up_ref[...] = sums_ref[1].astype(F32).T
+    down_ref[...] = sums_ref[2].astype(F32)
+
+
+def ffn_outputs(sums):
+    _, hidden, width = sums.shape
+    whole = pl.BlockSpec(memory_space=pltpu.VMEM)
+    turned = jax.ShapeDtypeStruct((width, hidden), F32)
+    return pl.pallas_call(
+        ffn_sums_kernel,
+        in_specs=[whole],
+        out_specs=[whole, whole, whole],
+        out_shape=[turned, turned, jax.ShapeDtypeStruct((hidden, width), F32)],
+        compiler_params=pltpu.CompilerParams(vmem_limit_bytes=40 * 1024 * 1024),
+        cost_estimate=pl.CostEstimate(
+            flops=3 * hidden * width, bytes_accessed=18 * hidden * width, transcendentals=0
+        ),
+        name="ffn_outputs",
+    )(sums)
 
 
 def done(value):
@@ -795,11 +815,11 @@
             whole = lax.dynamic_update_index_in_dim(whole, piece, (place - k) % dp_count, 0)
         return whole
 
-    def scatter_z(blocks):
+    def scatter_z(blocks, token=0):
         blocks = blocks.astype(BF16)
         total = choose(blocks, place, 0).astype(F32)
         for k in range(1, dp_count):
-            block = choose(blocks, (place - k) % dp_count, 0)
+            block = choose(blocks, (place - k) % dp_count + token, 0)
             total = total + shift(block, "dp", dp_count, -k).astype(F32)
         return total
 
@@ -904,7 +924,7 @@
     grad_rows = jnp.concatenate(
         [choose(grad_all, (place - k) % dp_count, 0) for k in range(dp_count)]
     )
-    ffn_own = hold(jnp.stack([ffn_gate.T, ffn_up.T, ffn_down]), done(down_full))
+    ffn_own = hold(jnp.stack([ffn_gate.T, ffn_up.T, ffn_down]), done(down_plane))
     ffn_full = lax.all_gather(ffn_own, "seq", axis=1, tiled=True)
 
     query, pairs, attended, logs = attend(token_all, query_up_padded, latent_up_group)
@@ -935,7 +955,8 @@
         ),
         "seq",
         scatter_dimension=0,
-    ).astype(F32)
+    )
+    sum_gate, sum_up, sum_down_rows = ffn_outputs(ffn_sums)
 
     grad_middle_norm, grad_ffn_gain_part = norm_back(
         grad_normed_two, normal_two, inverse_two, ffn_gain_full
@@ -1047,7 +1068,7 @@
         choose(down_sums, core, 1),
         choose(down_sums, 1 - core + done(group_grads), 1),
     )
-    sum_down = scatter_z(sum_down)
+    sum_down = scatter_z(sum_down, done(sum_down_rows))
     group_sums = jnp.sum(exchange(hold(group_grads, core_done), "dp").astype(F32), 0)
     group_sums = lax.ppermute(group_sums.astype(BF16), both, to_owner).astype(F32)
     sum_query_up = group_sums[: query_up.shape[1], :query_rank].T
@@ -1066,9 +1087,9 @@
         sum_latent_up,
         sum_out,
         sum_gains[1],
-        ffn_sums[:own_hidden].T,
-        ffn_sums[own_hidden : 2 * own_hidden].T,
-        ffn_sums[2 * own_hidden :],
+        sum_gate,
+        sum_up,
+        sum_down_rows,
     )
 
 

time: 753 us -> 776 us (1.031)
  the two profiles are of different devices: /device:TPU:2 before, /device:TPU:25 now
where the time goes in v7:
time: 776 us; the launch traced here: 766 us
  waiting for transfers between devices  357 us (46%)
  local copies, waits for them, and re-layouts  97.4 us (13%)
  starting transfers between devices  93.9 us (12%)
  Pallas kernels  88.8 us (11%)
  matrix products  60 us (8%)
  other arithmetic  39.1 us (5%)
  between operations  30.2 us (4%)
    ppermute x21, waiting for transfers between devices, across(): lax.ppermute(value, 'seq', [(i, i ^ 2 * steps) for i in range(seq_count)])  122 us
    ppermute x12, waiting for transfers between devices, shift(): lax.ppermute(value, axis, [(i, (i + step) % count) for i in range(count)])  116 us
    all_to_all x5, waiting for transfers between devices, exchange(): lax.all_to_all(blocks, axis, split_axis=0, concat_axis=0, axis_index_grou...  78.6 us
    dot_general x10, matrix products, dot(): return jnp.einsum(spec, left, right, preferred_element_type=F32)  54.8 us
    ppermute x12, starting transfers between devices, shift(): lax.ppermute(value, axis, [(i, (i + step) % count) for i in range(count)])  35 us
    pallas_call x1, Pallas kernels, attend_back(): pl.pallas_call(attend_back_kernel, grid=(heads,), in_specs=[whole, pl.Blo...  25.5 us
    pallas_call x1, Pallas kernels, attend(): pl.pallas_call(attend_kernel, grid=(heads,), in_specs=[whole, pl.BlockSpe...  23.8 us
    all_to_all x5, starting transfers between devices, exchange(): lax.all_to_all(blocks, axis, split_axis=0, concat_axis=0, axis_index_grou...  23.6 us
  transfers between devices with their start and end apart: 51, of which 26 were waited for; matrix products, arithmetic and copies ran while one was open for 22% of the time, Pallas kernels for 11%

profile of v7, /device:TPU:25, one launch (start us, length us, event | category | flops | bytes accessed | tf_op | source)
XLA Modules:
  0.0 766.4 jit_solution(12511994094373069693)
XLA Ops:
  17.8 11.0 %collective-permute-done.1 = bf16[80,1152]{1,0:T(8,128)(2,1)S(1)} collective-permute-done((bf16[80,1152]{1,0:T(8,128)(2,1)S(1)}, bf16[80,1152]{1,0:T(8,128)(2,1)S(1)}, u32[]{:S(2)}, u32[]{:S(2)}) %collective-permute-start.1) | collective-permute-done | bytes 184352 | tf_op jit(solution)/shard_map/ppermute | solution.py:82
  42.6 15.4 %collective-permute-done.6 = bf16[160,1024]{1,0:T(8,128)(2,1)S(1)} collective-permute-done((bf16[160,1024]{1,0:T(8,128)(2,1)S(1)}, bf16[160,1024]{1,0:T(8,128)(2,1)S(1)}, u32[]{:S(2)}, u32[]{:S(2)}) %collective-permute-start.6) | collective-permute-done | bytes 327712 | tf_op jit(solution)/shard_map/ppermute | solution.py:869
  67.8 30.5 %collective-permute-done.3 = bf16[4,80,1152]{2,1,0:T(8,128)(2,1)} collective-permute-done((bf16[4,80,1152]{2,1,0:T(8,128)(2,1)}, bf16[4,80,1152]{2,1,0:T(8,128)(2,1)}, u32[]{:S(2)}, u32[]{:S(2)}) %collective-permute-start.3) | collective-permute-done | bytes 737312 | tf_op jit(solution)/shard_map/ppermute | solution.py:781
  102.8 15.8 %collective-permute-done.5 = bf16[4,80,1152]{2,1,0:T(8,128)(2,1)} collective-permute-done((bf16[4,80,1152]{2,1,0:T(8,128)(2,1)}, bf16[4,80,1152]{2,1,0:T(8,128)(2,1)}, u32[]{:S(2)}, u32[]{:S(2)}) %collective-permute-start.5) | collective-permute-done | bytes 737312 | tf_op jit(solution)/shard_map/ppermute | solution.py:781
  154.5 16.9 %collective-permute-done.9 = bf16[128,1152]{0,1:T(8,128)(2,1)S(1)} collective-permute-done((bf16[128,1152]{0,1:T(8,128)(2,1)S(1)}, bf16[128,1152]{0,1:T(8,128)(2,1)S(1)}, u32[]{:S(2)}, u32[]{:S(2)}) %collective-permute-start.9) | collective-permute-done | bytes 294944 | tf_op jit(solution)/shard_map/ppermute | solution.py:781
  177.1 23.8 %attend.1 = (bf16[1024,640]{1,0:T(8,128)(2,1)S(1)}, bf16[1024,640]{1,0:T(8,128)(2,1)S(1)}, bf16[1024,384]{1,0:T(8,128)(2,1)S(1)}, f32[1024,640]{1,0:T(8,128)S(1)}) custom-call(bf16[1024,1152]{1,0:T(8,128)(2,1)S(1)} %bitcast.219, bf16[640,768]{1,0:T(8,128)(2,1)S(1)} %bitcast.223, bf16[640,256]{1,0:T(8,128)(2,1)S(1)} %bitcast.227), custom_call_target="tpu_custom_call" | custom-call | flops 2013265920 | bytes 7864320 | tf_op jit(solution)/shard_map/attend/pallas_call | solution.py:485
  224.8 13.7 %collective-permute-done.16 = bf16[128,2560]{1,0:T(8,128)(2,1)S(1)} collective-permute-done((bf16[128,2560]{1,0:T(8,128)(2,1)S(1)}, bf16[128,2560]{1,0:T(8,128)(2,1)S(1)}, u32[]{:S(2)}, u32[]{:S(2)}) %collective-permute-start.16) | collective-permute-done | bytes 655392 | tf_op jit(solution)/shard_map/ppermute | solution.py:781
  238.5 13.5 %collective-permute-done.15 = bf16[128,2560]{1,0:T(8,128)(2,1)S(1)} collective-permute-done((bf16[128,2560]{1,0:T(8,128)(2,1)S(1)}, bf16[128,2560]{1,0:T(8,128)(2,1)S(1)}, u32[]{:S(2)}, u32[]{:S(2)}) %collective-permute-start.15) | collective-permute-done | bytes 655392 | tf_op jit(solution)/shard_map/ppermute | solution.py:781
  253.1 21.8 %all-to-all-done.2 = bf16[4,128,2560]{2,1,0:T(8,128)(2,1)} async-done(((bf16[4,128,2560]{2,1,0:T(8,128)(2,1)}), bf16[4,128,2560]{2,1,0:T(8,128)(2,1)}, u32[]{:S(2)}, u32[]{:S(2)}) %all-to-all-start.2) | async-done | bytes 2621472 | tf_op jit(solution)/shard_map/all_to_all | solution.py:734
  289.6 9.4 %collective-permute-done.19 = bf16[128,2560]{1,0:T(8,128)(2,1)S(1)} collective-permute-done((bf16[128,2560]{1,0:T(8,128)(2,1)S(1)}, bf16[128,2560]{1,0:T(8,128)(2,1)S(1)}, u32[]{:S(2)}, u32[]{:S(2)}) %collective-permute-start.19) | collective-permute-done | bytes 655392 | tf_op jit(solution)/shard_map/ppermute | solution.py:82
  298.9 28.7 %collective-permute-done.18 = bf16[128,2560]{1,0:T(8,128)(2,1)S(1)} collective-permute-done((bf16[128,2560]{1,0:T(8,128)(2,1)S(1)}, bf16[128,2560]{1,0:T(8,128)(2,1)S(1)}, u32[]{:S(2)}, u32[]{:S(2)}) %collective-permute-start.18) | collective-permute-done | bytes 655392 | tf_op jit(solution)/shard_map/ppermute | solution.py:82
  327.8 18.8 %ffn_hidden.1 = (bf16[2,1600,512]{2,1,0:T(8,128)(2,1)}, bf16[1600,512]{1,0:T(8,128)(2,1)S(1)}) custom-call(bf16[3,1600,2560]{2,1,0:T(8,128)(2,1)} %all-gather.3.cloned.1.call-done.weights_ref, bf16[512,2560]{1,0:T(8,128)(2,1)S(1)} %pad_maximum_fusion.rows_ref, bf16[512,2560]{1,0:T(8,128)(2,1)} %pad_maximum_fusion.1.grads_ref), custom_call_target="tpu_custom_call" | custom-call | flops 12582912000 | bytes 34734080 | tf_op jit(solution)/shard_map/ffn_hidden/pallas_call | solution.py:645
  346.7 18.6 %ffn_grads.1 = bf16[8,3,200,2560]{3,2,1,0:T(8,128)(2,1)} custom-call(bf16[2,8,200,512]{3,2,1,0:T(8,128)(2,1)} %bitcast.261, bf16[8,200,512]{2,1,0:T(8,128)(2,1)S(1)} %bitcast.229, bf16[512,2560]{1,0:T(8,128)(2,1)S(1)} %pad_maximum_fusion.rows_ref, bf16[512,2560]{1,0:T(8,128)(2,1)} %pad_maximum_fusion.1.grads_ref), custom_call_target="tpu_custom_call" | custom-call | flops 12582912000 | bytes 34734080 | tf_op jit(solution)/shard_map/ffn_grads/pallas_call | solution.py:675
  366.5 13.7 %bitcast_convert_fusion = bf16[512,2560]{1,0:T(8,128)(2,1)S(1)} fusion(bf16[2,1600,512]{2,1,0:T(8,128)(2,1)} %get-tuple-element.27, bf16[3,1600,2560]{2,1,0:T(8,128)(2,1)} %all-gather.3.cloned.1.call-done.weights_ref), kind=kOutput, calls=%fused_computation.13 | convolution fusion | flops 8389918720 | bytes 22282240 | tf_op jit(solution)/shard_map/gft,gfd->td/dot_general | solution.py:78
  380.4 11.3 %collective-permute-start.22 = (bf16[128,2560]{1,0:T(8,128)(2,1)S(1)}, bf16[128,2560]{1,0:T(8,128)(2,1)S(1)}, u32[]{:S(2)}, u32[]{:S(2)}) collective-permute-start(bf16[128,2560]{1,0:T(8,128)(2,1)S(1)} %get-tuple-element.136), channel_id=1, source_target_pairs={{0,8},{8,16},{16,24},{24,0},{1,9},{9,17},{17,25},{25,1},{2,10},{10... | collective-permute-start | bytes 1966088 | tf_op jit(solution)/shard_map/ppermute | solution.py:82
  395.9 12.6 %collective-permute-done.22 = bf16[128,2560]{1,0:T(8,128)(2,1)S(1)} collective-permute-done((bf16[128,2560]{1,0:T(8,128)(2,1)S(1)}, bf16[128,2560]{1,0:T(8,128)(2,1)S(1)}, u32[]{:S(2)}, u32[]{:S(2)}) %collective-permute-start.22) | collective-permute-done | bytes 655392 | tf_op jit(solution)/shard_map/ppermute | solution.py:82
  408.5 43.0 %collective-permute-done.21 = bf16[128,2560]{1,0:T(8,128)(2,1)S(1)} collective-permute-done((bf16[128,2560]{1,0:T(8,128)(2,1)S(1)}, bf16[128,2560]{1,0:T(8,128)(2,1)S(1)}, u32[]{:S(2)}, u32[]{:S(2)}) %collective-permute-start.21) | collective-permute-done | bytes 655392 | tf_op jit(solution)/shard_map/ppermute | solution.py:82
  453.4 9.5 %convolution_convert_fusion.1 = bf16[128,2560]{1,0:T(8,128)(2,1)S(1)} fusion(bf16[2560,2560]{1,0:T(8,128)(2,1)} %all-gather.5.cloned.1.call-done, f32[128,2560]{1,0:T(8,128)S(1)} %convert_add_fusion.2), kind=kOutput, calls=%fused_computation.18 | convolution fusion | flops 1678704640 | bytes 15073280 | tf_op jit(solution)/shard_map/td,kd->tk/dot_general | solution.py:78
  496.4 9.5 %broadcast_select_fusion = (bf16[512,2560]{1,0:T(8,128)(2,1)S(1)}, bf16[512,2560]{1,0:T(8,128)(2,1)}) fusion(pred[]{:T(512)} %bitcast.69, bf16[1600,512]{1,0:T(8,128)(2,1)S(1)} %copy-done.7, bf16[3,1600,2560]{2,1,0:T(8,128)(2,1)} %all-gather.3.cloned.1.call-done.weights_ref), kind=kOutput, calls=%fused_computation.32 | convolution fusion | flops 4196925440 | bytes 15073792 | tf_op jit(solution)/shard_map/ft,fd->td/dot_general | solution.py:78
  516.8 10.4 %collective-permute-done.30 = bf16[128,2560]{1,0:T(8,128)(2,1)} collective-permute-done((bf16[128,2560]{1,0:T(8,128)(2,1)}, bf16[128,2560]{1,0:T(8,128)(2,1)}, u32[]{:S(2)}, u32[]{:S(2)}) %collective-permute-start.30) | collective-permute-done | bytes 655392 | tf_op jit(solution)/shard_map/ppermute | solution.py:781
  530.1 25.5 %attend_back.1 = (bf16[1024,640]{1,0:T(8,128)(2,1)S(1)}, bf16[1024,640]{1,0:T(8,128)(2,1)S(1)}, bf16[1024,1152]{1,0:T(8,128)(2,1)}) custom-call(bf16[1024,1152]{1,0:T(8,128)(2,1)} %bitcast.220, bf16[640,768]{1,0:T(8,128)(2,1)S(1)} %bitcast.224, bf16[640,256]{1,0:T(8,128)(2,1)S(1)} %bitcast.228, bf16[1024,640]{1,0:T(8,128)(2,1)S(1)} %copy-done.14, ...), custom_call_target="tpu_custom_call" | custom-call | flops 5368709120 | bytes 9175040 | tf_op jit(solution)/shard_map/attend_back/pallas_call | solution.py:583
  626.6 56.8 %all-to-all-done.4 = bf16[4,360,1024]{2,1,0:T(8,128)(2,1)} async-done(((bf16[4,360,1024]{2,1,0:T(8,128)(2,1)}), bf16[4,360,1024]{2,1,0:T(8,128)(2,1)}, u32[]{:S(2)}, u32[]{:S(2)}) %all-to-all-start.4) | async-done | bytes 2949152 | tf_op jit(solution)/shard_map/all_to_all | solution.py:734
  695.0 15.6 %collective-permute-done.42 = bf16[360,1024]{1,0:T(8,128)(2,1)S(1)} collective-permute-done((bf16[360,1024]{1,0:T(8,128)(2,1)}, bf16[360,1024]{1,0:T(8,128)(2,1)S(1)}, u32[]{:S(2)}, u32[]{:S(2)}) %collective-permute-start.42) | collective-permute-done | bytes 737312 | tf_op jit(solution)/shard_map/ppermute | solution.py:1073
  724.8 14.2 %collective-permute-start.40 = (bf16[80,1152]{1,0:T(8,128)(2,1)}, bf16[80,1152]{1,0:T(8,128)(2,1)}, u32[]{:S(2)}, u32[]{:S(2)}) collective-permute-start(bf16[80,1152]{1,0:T(8,128)(2,1)} %get-tuple-element.158), channel_id=1, source_target_pairs={{0,16},{8,24},{16,0},{24,8},{1,17},{9,25},{17,1},{25,9},{2,18},{10... | collective-permute-start | bytes 552968 | tf_op jit(solution)/shard_map/ppermute | solution.py:82
  (387 shorter events, 276.1 us)
Async XLA Ops:
  7.2 320.6 %all-gather.3.cloned.1.call-start = ((), (), s32[]{:S(2)}) async-start(), calls=%async_computation.6 | async-start | bytes 27648000 | tf_op jit(solution)/shard_map/all_gather | solution.py:928
  59.2 41.0 %all-to-all-start = ((bf16[4,160,1024]{2,1,0:T(8,128)(2,1)}), bf16[4,160,1024]{2,1,0:T(8,128)(2,1)}, u32[]{:S(2)}, u32[]{:S(2)}) async-start(bf16[4,160,1024]{2,1,0:T(8,128)(2,1)} %broadcast_in_dim.189), calls=%async_computation | async-start | bytes 2621440 | tf_op jit(solution)/shard_map/all_to_all | solution.py:734
  63.7 34.6 %collective-permute-start.3 = (bf16[4,80,1152]{2,1,0:T(8,128)(2,1)}, bf16[4,80,1152]{2,1,0:T(8,128)(2,1)}, u32[]{:S(2)}, u32[]{:S(2)}) collective-permute-start(bf16[4,80,1152]{2,1,0:T(8,128)(2,1)} %bitcast_dynamic-update-slice_fusion.18), channel_id=1, source_target_pairs={{0,2},{1,3},{2,0},{3,1},{4,6},{5,7},{6,4},{7,5},{8,10},{9,11},{10,... | collective-permute-start | bytes 2211848 | tf_op jit(solution)/shard_map/ppermute | solution.py:781
  63.7 36.4 %collective-permute-start.4 = (bf16[4,80,1152]{2,1,0:T(8,128)(2,1)}, bf16[4,80,1152]{2,1,0:T(8,128)(2,1)S(1)}, u32[]{:S(2)}, u32[]{:S(2)}) collective-permute-start(bf16[4,80,1152]{2,1,0:T(8,128)(2,1)} %bitcast_dynamic-update-slice_fusion.18), channel_id=1, source_target_pairs={{0,4},{1,5},{2,6},{3,7},{4,0},{5,1},{6,2},{7,3},{8,12},{9,13},{10,... | collective-permute-start | bytes 2211848 | tf_op jit(solution)/shard_map/ppermute | solution.py:781
  63.7 54.9 %collective-permute-start.5 = (bf16[4,80,1152]{2,1,0:T(8,128)(2,1)}, bf16[4,80,1152]{2,1,0:T(8,128)(2,1)}, u32[]{:S(2)}, u32[]{:S(2)}) collective-permute-start(bf16[4,80,1152]{2,1,0:T(8,128)(2,1)} %bitcast_dynamic-update-slice_fusion.18), channel_id=1, source_target_pairs={{0,6},{1,7},{2,4},{3,5},{4,2},{5,3},{6,0},{7,1},{8,14},{9,15},{10,... | collective-permute-start | bytes 2211848 | tf_op jit(solution)/shard_map/ppermute | solution.py:781
  145.2 59.8 %all-to-all-start.1 = ((bf16[4,80,2560]{2,1,0:T(8,128)(2,1)}), bf16[4,80,2560]{2,1,0:T(8,128)(2,1)}, u32[]{:S(2)}, u32[]{:S(2)}) async-start(bf16[4,80,2560]{2,1,0:T(8,128)(2,1)} %broadcast_in_dim.199), calls=%async_computation.1 | async-start | bytes 3276800 | tf_op jit(solution)/shard_map/all_to_all | solution.py:734
  213.5 61.3 %all-to-all-start.2 = ((bf16[4,128,2560]{2,1,0:T(8,128)(2,1)}), bf16[4,128,2560]{2,1,0:T(8,128)(2,1)}, u32[]{:S(2)}, u32[]{:S(2)}) async-start(bf16[4,128,2560]{2,1,0:T(8,128)(2,1)} %broadcast_in_dim.201), calls=%async_computation.2 | async-start | bytes 5242880 | tf_op jit(solution)/shard_map/all_to_all | solution.py:734
  218.1 235.4 %all-gather.5.cloned.1.call-start = ((), (), s32[]{:S(2)}) async-start(), calls=%async_computation.7 | async-start | bytes 14745600 | tf_op jit(solution)/shard_map/all_gather | solution.py:942
  222.2 29.9 %collective-permute-start.15 = (bf16[128,2560]{1,0:T(8,128)(2,1)S(1)}, bf16[128,2560]{1,0:T(8,128)(2,1)S(1)}, u32[]{:S(2)}, u32[]{:S(2)}) collective-permute-start(bf16[128,2560]{1,0:T(8,128)(2,1)S(1)} %get-tuple-element.144), channel_id=1, source_target_pairs={{0,4},{1,5},{2,6},{3,7},{4,0},{5,1},{6,2},{7,3},{8,12},{9,13},{10,... | collective-permute-start | bytes 1966088 | tf_op jit(solution)/shard_map/ppermute | solution.py:781
  223.4 29.0 %collective-permute-start.14 = (bf16[128,2560]{1,0:T(8,128)(2,1)S(1)}, bf16[128,2560]{1,0:T(8,128)(2,1)S(1)}, u32[]{:S(2)}, u32[]{:S(2)}) collective-permute-start(bf16[128,2560]{1,0:T(8,128)(2,1)S(1)} %get-tuple-element.142), channel_id=1, source_target_pairs={{0,2},{1,3},{2,0},{3,1},{4,6},{5,7},{6,4},{7,5},{8,10},{9,11},{10,... | collective-permute-start | bytes 1966088 | tf_op jit(solution)/shard_map/ppermute | solution.py:781
  282.3 433.6 %reduce-scatter.2.cloned.1.call-start = ((), (), s32[]{:S(2)}) async-start(), calls=%async_computation.8 | async-start | bytes 27648000 | tf_op jit(solution)/shard_map/reduce_scatter | solution.py:949
  282.4 45.2 %collective-permute-start.18 = (bf16[128,2560]{1,0:T(8,128)(2,1)S(1)}, bf16[128,2560]{1,0:T(8,128)(2,1)S(1)}, u32[]{:S(2)}, u32[]{:S(2)}) collective-permute-start(bf16[128,2560]{1,0:T(8,128)(2,1)S(1)} %fusion.45), channel_id=1, source_target_pairs={{0,16},{8,24},{16,0},{24,8},{1,17},{9,25},{17,1},{25,9},{2,18},{10... | collective-permute-start | bytes 1966088 | tf_op jit(solution)/shard_map/ppermute | solution.py:82
  285.0 42.6 %collective-permute-start.17 = (bf16[128,2560]{1,0:T(8,128)(2,1)S(1)}, bf16[128,2560]{1,0:T(8,128)(2,1)S(1)}, u32[]{:S(2)}, u32[]{:S(2)}) collective-permute-start(bf16[128,2560]{1,0:T(8,128)(2,1)S(1)} %fusion.45), channel_id=1, source_target_pairs={{0,8},{8,16},{16,24},{24,0},{1,9},{9,17},{17,25},{25,1},{2,10},{10... | collective-permute-start | bytes 1966088 | tf_op jit(solution)/shard_map/ppermute | solution.py:82
  380.4 28.1 %collective-permute-start.22 = (bf16[128,2560]{1,0:T(8,128)(2,1)S(1)}, bf16[128,2560]{1,0:T(8,128)(2,1)S(1)}, u32[]{:S(2)}, u32[]{:S(2)}) collective-permute-start(bf16[128,2560]{1,0:T(8,128)(2,1)S(1)} %get-tuple-element.136), channel_id=1, source_target_pairs={{0,8},{8,16},{16,24},{24,0},{1,9},{9,17},{17,25},{25,1},{2,10},{10... | collective-permute-start | bytes 1966088 | tf_op jit(solution)/shard_map/ppermute | solution.py:82
  391.7 59.8 %collective-permute-start.21 = (bf16[128,2560]{1,0:T(8,128)(2,1)S(1)}, bf16[128,2560]{1,0:T(8,128)(2,1)S(1)}, u32[]{:S(2)}, u32[]{:S(2)}) collective-permute-start(bf16[128,2560]{1,0:T(8,128)(2,1)S(1)} %get-tuple-element.137), channel_id=1, source_target_pairs={{0,16},{8,24},{16,0},{24,8},{1,17},{9,25},{17,1},{25,9},{2,18},{10... | collective-permute-start | bytes 1966088 | tf_op jit(solution)/shard_map/ppermute | solution.py:82
  395.7 55.8 %collective-permute-start.20 = (bf16[128,2560]{1,0:T(8,128)(2,1)S(1)}, bf16[128,2560]{1,0:T(8,128)(2,1)S(1)}, u32[]{:S(2)}, u32[]{:S(2)}) collective-permute-start(bf16[128,2560]{1,0:T(8,128)(2,1)S(1)} %get-tuple-element.135), channel_id=1, source_target_pairs={{0,24},{8,0},{16,8},{24,16},{1,25},{9,1},{17,9},{25,17},{2,26},{10... | collective-permute-start | bytes 1966088 | tf_op jit(solution)/shard_map/ppermute | solution.py:82
  494.2 33.0 %collective-permute-start.30 = (bf16[128,2560]{1,0:T(8,128)(2,1)}, bf16[128,2560]{1,0:T(8,128)(2,1)}, u32[]{:S(2)}, u32[]{:S(2)}) collective-permute-start(bf16[128,2560]{1,0:T(8,128)(2,1)} %get-tuple-element.123), channel_id=1, source_target_pairs={{0,6},{1,7},{2,4},{3,5},{4,2},{5,3},{6,0},{7,1},{8,14},{9,15},{10,... | collective-permute-start | bytes 1966088 | tf_op jit(solution)/shard_map/ppermute | solution.py:781
  507.9 77.2 %all-to-all-start.3 = ((bf16[4,128,2560]{2,1,0:T(8,128)(2,1)}), bf16[4,128,2560]{2,1,0:T(8,128)(2,1)}, u32[]{:S(2)}, u32[]{:S(2)}) async-start(bf16[4,128,2560]{2,1,0:T(8,128)(2,1)} %pad_maximum_fusion.2), calls=%async_computation.3 | async-start | bytes 5242880 | tf_op jit(solution)/shard_map/all_to_all | solution.py:734
  529.2 43.4 %collective-permute-start.34 = (bf16[4,128,2560]{2,1,0:T(8,128)(2,1)}, bf16[4,128,2560]{2,1,0:T(8,128)(2,1)}, u32[]{:S(2)}, u32[]{:S(2)}) collective-permute-start(bf16[4,128,2560]{2,1,0:T(8,128)(2,1)} %bitcast_dynamic-update-slice_fusion.10), channel_id=1, source_target_pairs={{0,1},{1,0},{2,3},{3,2},{4,5},{5,4},{6,7},{7,6},{8,9},{9,8},{10,11... | collective-permute-start | bytes 7864328 | tf_op jit(solution)/shard_map/ppermute | solution.py:730
  614.2 69.3 %all-to-all-start.4 = ((bf16[4,360,1024]{2,1,0:T(8,128)(2,1)}), bf16[4,360,1024]{2,1,0:T(8,128)(2,1)}, u32[]{:S(2)}, u32[]{:S(2)}) async-start(bf16[4,360,1024]{2,1,0:T(8,128)(2,1)} %fusion.13), calls=%async_computation.5 | async-start | bytes 5898240 | tf_op jit(solution)/shard_map/all_to_all | solution.py:734
  623.9 68.9 %collective-permute-start.38 = (bf16[4,80,1152]{2,1,0:T(8,128)(2,1)}, bf16[4,80,1152]{2,1,0:T(8,128)(2,1)}, u32[]{:S(2)}, u32[]{:S(2)}) collective-permute-start(bf16[4,80,1152]{2,1,0:T(8,128)(2,1)} %get-tuple-element.129), channel_id=1, source_target_pairs={{0,6},{1,7},{2,4},{3,5},{4,2},{5,3},{6,0},{7,1},{8,14},{9,15},{10,... | collective-permute-start | bytes 2211848 | tf_op jit(solution)/shard_map/ppermute | solution.py:781
  623.9 68.9 %collective-permute-start.37 = (bf16[4,80,1152]{2,1,0:T(8,128)(2,1)}, bf16[4,80,1152]{2,1,0:T(8,128)(2,1)}, u32[]{:S(2)}, u32[]{:S(2)}) collective-permute-start(bf16[4,80,1152]{2,1,0:T(8,128)(2,1)} %get-tuple-element.130), channel_id=1, source_target_pairs={{0,4},{1,5},{2,6},{3,7},{4,0},{5,1},{6,2},{7,3},{8,12},{9,13},{10,... | collective-permute-start | bytes 2211848 | tf_op jit(solution)/shard_map/ppermute | solution.py:781
  624.9 67.9 %collective-permute-start.36 = (bf16[4,80,1152]{2,1,0:T(8,128)(2,1)}, bf16[4,80,1152]{2,1,0:T(8,128)(2,1)}, u32[]{:S(2)}, u32[]{:S(2)}) collective-permute-start(bf16[4,80,1152]{2,1,0:T(8,128)(2,1)} %get-tuple-element.128), channel_id=1, source_target_pairs={{0,2},{1,3},{2,0},{3,1},{4,6},{5,7},{6,4},{7,5},{8,10},{9,11},{10,... | collective-permute-start | bytes 2211848 | tf_op jit(solution)/shard_map/ppermute | solution.py:781
  724.8 29.9 %collective-permute-start.40 = (bf16[80,1152]{1,0:T(8,128)(2,1)}, bf16[80,1152]{1,0:T(8,128)(2,1)}, u32[]{:S(2)}, u32[]{:S(2)}) collective-permute-start(bf16[80,1152]{1,0:T(8,128)(2,1)} %get-tuple-element.158), channel_id=1, source_target_pairs={{0,16},{8,24},{16,0},{24,8},{1,17},{9,25},{17,1},{25,9},{2,18},{10... | collective-permute-start | bytes 552968 | tf_op jit(solution)/shard_map/ppermute | solution.py:82
  (88 other events, 1355.2 us)
Sparse Core Ops, SparseCore 0:
  36.1 179.7 all-gather.2
  282.4 75.6 all-gather.4
  366.6 201.4 reduce-scatter.1
